TPU v7x, 32 devices: a whole 2x2x4 slice. The times are simulated.
32 devices in a mesh: seq: 8 (over y, x, core), hid: 4 (over z).
Axes of the slice: x: 2, y: 2, z: 4, core: 2. Of those that a mesh axis runs over, the one named last changes fastest.
Arguments:
- hidden: bfloat16 [2048, 4096], P('seq', 'hid'), may hold values from -6 to 6
- w_in: bfloat16 [2, 4096, 1024], P(None, 'hid'), may hold values from -0.09863281 to 0.09863281
- embedding: bfloat16 [1, 2048, 1024], replicated, may hold values from -6 to 6
- depth_gain: float32 [2, 1024], replicated, may hold values from 0.25 to 1.75
- w_out: bfloat16 [1024, 2, 2048], P(('seq', 'hid')), may hold values from -0.43554688 to 0.43554688
- codebook_ids: int32 [2, 2048], P(None, ('seq', 'hid')), may hold values from 0 to 2047
Outputs:
- grad_hidden: bfloat16 [2048, 4096], P('seq', 'hid')
- grad_in: float32 [2, 4096, 1024], P(None, 'hid', 'seq')
- grad_out: float32 [1024, 2, 2048], P(('seq', 'hid'))
All inputs are finite; a program needn't handle non-finite values.
Results may differ from a plain program's by a relative error of at most 0.01.
Values may be sent and summed in bfloat16 or wider, within the bound.
No kernel may reach another device: no remote copies, remote signals or barrier semaphores. Data moves between devices by JAX's collectives and lax.ppermute only.
A program may use at most 128 MiB of HBM per device.

v0:
```python
import jax
import jax.numpy as jnp
from jax import lax
from jax.experimental import pallas as pl
from jax.experimental.pallas import tpu as pltpu
from jax.sharding import PartitionSpec as P

F32 = jnp.float32
BF16 = jnp.bfloat16


def pick(values, index):
    return lax.dynamic_index_in_dim(values, index, axis=0, keepdims=False)


def matmul(a, b, contract):
    return lax.dot_general(a, b, (contract, ((), ())), preferred_element_type=F32)


def after(value, *others):
    return lax.optimization_barrier((value, *others))[0]


VMEM = pltpu.CompilerParams(vmem_limit_bytes=48 * 2**20)


def whole(shape):
    return pl.BlockSpec(shape, lambda n, place: (0,) * len(shape))


def call(kernel, place, grid, in_specs, out_specs, out_shape, scratch, flops, args):
    moved = sum(a.size * a.dtype.itemsize for a in args)
    return pl.pallas_call(
        kernel,
        grid_spec=pltpu.PrefetchScalarGridSpec(
            num_scalar_prefetch=1,
            grid=(grid,),
            in_specs=in_specs,
            out_specs=out_specs,
            scratch_shapes=scratch,
        ),
        out_shape=out_shape,
        compiler_params=VMEM,
        cost_estimate=pl.CostEstimate(flops=flops, bytes_accessed=moved, transcendentals=0),
    )(place, *args)


def project(place, group, w_in, hids):
    steps = len(group)
    rows, units = group[0].shape
    depth = w_in.shape[2]
    part = rows // hids
    wide = min(256, depth)

    def kernel(place_ref, *refs):
        hidden, w, outs, sums = refs[:steps], refs[steps], refs[steps + 1 : -1], refs[-1]
        step, j = place_ref[0], place_ref[1]
        for m in range(steps):
            sums[m] = jnp.dot(hidden[m][...], w[0], preferred_element_type=F32)
        for shift in range(hids):
            start = pl.multiple_of(lax.rem(j + shift, hids) * part, part)
            for m in range(steps):
                to = pl.multiple_of(lax.rem(step + m, steps) * part, part)
                outs[shift][pl.ds(to, part), :] = sums[m, pl.ds(start, part), :].astype(
                    outs[shift].dtype
                )

    column = pl.BlockSpec((steps * part, wide), lambda n, place: (0, n))
    return call(
        kernel,
        place,
        depth // wide,
        [whole((rows, units))] * steps
        + [pl.BlockSpec((1, units, wide), lambda n, place: (place[0], 0, n))],
        [column] * hids,
        [
            jax.ShapeDtypeStruct((steps * part, depth), BF16 if shift else F32)
            for shift in range(hids)
        ],
        [pltpu.VMEM((steps, rows, wide), F32)],
        2 * steps * rows * units * depth,
        (*group, w_in),
    )


def spread(place, pieces, ratio, seqs, steps):
    hids = len(pieces)
    owned, depth = pieces[0].shape
    part = owned // steps
    rows = part * hids
    wide = depth // seqs

    def kernel(place_ref, *refs):
        pieces, ratio, scaled, plain = refs[:hids], refs[hids], refs[hids + 1], refs[hids + 2 :]
        step, j = place_ref[0], place_ref[1]
        for shift in range(hids):
            owner = lax.rem(j - shift + hids, hids)
            values = pieces[shift][...].astype(F32) * ratio[owner]
            values = values.astype(BF16)
            for m in range(steps):
                at = pl.multiple_of(m * rows + owner * part, part)
                for q in range(seqs):
                    scaled[q, pl.ds(at, part), :] = values[
                        m * part : (m + 1) * part, q * wide : (q + 1) * wide
                    ]
            to = pl.multiple_of(owner * part, part)
            for m in range(steps):
                start = pl.multiple_of(lax.rem(step + m, steps) * part, part)
                plain[m][pl.ds(to, part), :] = pieces[shift][pl.ds(start, part), :]

    return call(
        kernel,
        place,
        1,
        [whole((owned, depth))] * hids + [whole((hids, owned, 1))],
        [whole((seqs, steps * rows, wide))] + [whole((rows, depth))] * steps,
        [jax.ShapeDtypeStruct((seqs, steps * rows, wide), BF16)]
        + [jax.ShapeDtypeStruct((rows, depth), BF16)] * steps,
        [],
        steps * rows * depth,
        (*pieces, ratio),
    )


def input_gradient(place, blocks, scaled, steps):
    groups = len(blocks)
    units, rows = blocks[0][0].shape
    wide = scaled.shape[2]
    tall = min(256, units)

    def kernel(place_ref, *refs):
        hidden, scaled, out = refs[:-2], refs[-2], refs[-1]
        step, group = place_ref[0], place_ref[2]
        total = None
        for r in range(groups):
            source = lax.rem(group - r + groups, groups)
            for m in range(steps):
                at = pl.multiple_of(lax.rem(step - m + steps, steps) * rows, rows)
                right = jnp.concatenate(
                    [scaled[source * steps + s, pl.ds(at, rows), :] for s in range(steps)], axis=1
                )
                term = jnp.dot(hidden[r * steps + m][...], right, preferred_element_type=F32)
                total = term if total is None else total + term
        for s in range(steps):
            out[s] = total[:, s * wide : (s + 1) * wide]

    flat = [b for line in blocks for b in line]
    return call(
        kernel,
        place,
        units // tall,
        [pl.BlockSpec((tall, rows), lambda n, place: (n, 0))] * len(flat) + [whole(scaled.shape)],
        pl.BlockSpec((steps, tall, wide), lambda n, place: (0, n, 0)),
        jax.ShapeDtypeStruct((steps, units, wide), F32),
        [],
        2 * units * rows * len(flat) * wide * steps,
        (*flat, scaled),
    )


def hidden_gradient(place, d_rows, w_in, hidden, factors):
    steps, units, depth = w_in.shape
    rows = hidden.shape[0]
    wide = min(256, units)

    def kernel(place_ref, *refs):
        d_rows, w, hidden, factors, out = refs[:steps], refs[-4], refs[-3], refs[-2], refs[-1]
        total = None
        for r in range(steps):
            which = lax.rem(place_ref[0] - r + steps, steps)
            term = lax.dot_general(
                d_rows[r][...], w[which], (((1,), (1,)), ((), ())), preferred_element_type=F32
            )
            total = term if total is None else total + term
        out[...] = (factors[0] * total - factors[1] * hidden[...].astype(F32)).astype(BF16)

    return call(
        kernel,
        place,
        units // wide,
        [whole((rows, depth))] * steps
        + [
            pl.BlockSpec((steps, wide, depth), lambda n, place: (0, n, 0)),
            pl.BlockSpec((rows, wide), lambda n, place: (0, n)),
            whole((2, rows, 1)),
        ],
        pl.BlockSpec((rows, wide), lambda n, place: (0, n)),
        jax.ShapeDtypeStruct((rows, units), BF16),
        [],
        2 * steps * rows * units * depth,
        (*d_rows, w_in, hidden, factors),
    )


def shards(hidden, w_in, embedding, depth_gain, w_out, codebook_ids):
    hids = lax.axis_size("hid")
    seqs = lax.axis_size("seq")
    steps, units, depth = w_in.shape
    entries = w_out.shape[2]
    rows = hidden.shape[0]
    part = rows // hids
    width_in = units * hids
    frames = rows * seqs
    halves = 2 if hids % 2 == 0 else 1
    block = entries // halves
    head_rows = w_out.shape[0]
    groups = seqs // steps
    i = lax.axis_index("seq")
    j = lax.axis_index("hid")
    step = i % steps
    half = j % halves

    def along_hid(values, shift):
        return lax.ppermute(values, "hid", [(a, (a + shift) % hids) for a in range(hids)])

    def turn_hid(values, shift):
        return lax.ppermute(
            values,
            "hid",
            [(a, a - a % halves + (a % halves + shift) % halves) for a in range(hids)],
        )

    def flip_seq(values, flip):
        return lax.ppermute(
            values,
            "seq",
            [(a, a - a % steps + (a % steps + flip) % steps) for a in range(seqs)],
        )

    def gather_flips(values, position):
        out = jnp.broadcast_to(values, (steps,) + values.shape)
        for r in range(1, steps):
            out = lax.dynamic_update_index_in_dim(
                out, flip_seq(values, -r), (position + r) % steps, 0
            )
        return out

    def gather_hid(values):
        out = jnp.broadcast_to(values, (hids,) + values.shape)
        for shift in range(1, hids):
            out = lax.dynamic_update_index_in_dim(
                out, along_hid(values, shift), (j - shift) % hids, 0
            )
        return out

    place = jnp.stack([step, j, i // steps]).astype(jnp.int32)

    def along_groups(values, shift):
        return lax.ppermute(values, "seq", [(a, (a + shift * steps) % seqs) for a in range(seqs)])

    group = [hidden] + [flip_seq(hidden, -r) for r in range(1, steps)]
    proj, *send = project(place, group, w_in, hids)
    owned = steps * part

    head_send = w_out.reshape(head_rows, steps, halves, block).transpose(2, 1, 0, 3)
    head_send = jnp.broadcast_to(head_send, (hids // halves,) + head_send.shape)
    head_send = after(head_send.reshape(hids, steps, head_rows, block), *send)
    head_mid = lax.all_to_all(head_send, "hid", 0, 0).transpose(1, 0, 2, 3)

    turned = [after(hidden.T, *send)]
    turned += [along_groups(turned[0], r) for r in range(1, groups)]
    turned = [[t] + [flip_seq(t, m) for m in range(1, steps)] for t in turned]

    squares_part = jnp.sum(jnp.square(hidden.astype(F32)), axis=1)
    small = jnp.concatenate([codebook_ids.reshape(-1).astype(F32), squares_part])
    small = gather_flips(after(small, *send), step)
    for shift in range(1, hids):
        proj += along_hid(send[shift - 1], shift).astype(F32)
    small = gather_hid(small)
    ids_group = small[:, :, : steps * part].astype(jnp.int32).reshape(hids, steps, steps, part)
    squares = jnp.sum(small[:, :, steps * part :], axis=0)
    ratio_group = lax.rsqrt(squares / width_in + 1e-06).reshape(steps, hids, part)
    ratio_own = pick(ratio_group, step).reshape(rows)

    head_send = head_mid.reshape(steps, hids * head_rows, block)
    head_send = jnp.broadcast_to(head_send, (groups,) + head_send.shape)
    head_send = head_send.reshape(seqs, hids * head_rows, block)
    head = lax.all_to_all(head_send, "seq", 0, 0).reshape(depth, block)

    ratio = lax.dynamic_index_in_dim(ratio_group, j, 1, False).reshape(owned)
    before = jnp.maximum(step - 1, 0)
    table = pick(embedding, before)
    ids_before = pick(pick(ids_group, j).transpose(1, 0, 2), before).reshape(-1)
    looked = jnp.take(table, ids_before, axis=0).astype(F32)
    x_rows = ratio[:, None] * proj + jnp.where(step > 0, looked, 0.0)
    scale = lax.rsqrt(jnp.mean(x_rows * x_rows, axis=1, keepdims=True) + 1e-06)
    gain = pick(depth_gain, step)[None, :]
    normed = (x_rows * scale * gain).astype(BF16)

    owners = [j - half + (half + k) % halves for k in range(halves)]
    normed_rows = jnp.concatenate([normed] + [turn_hid(normed, -k) for k in range(1, halves)])
    targets = jnp.concatenate(
        [pick(pick(ids_group, o).transpose(1, 0, 2), step).reshape(-1) for o in owners]
    )
    logits = matmul(normed_rows, head, ((1,), (0,)))
    top = jnp.max(logits, axis=1)
    total = jnp.sum(jnp.exp(logits - top[:, None]), axis=1)
    stats = jnp.stack([top, total]).reshape(2, halves, -1)
    every = [stats] + [jnp.roll(turn_hid(stats, -t), t, axis=1) for t in range(1, halves)]
    tops = jnp.stack([e[0] for e in every]).reshape(halves, -1)
    totals = jnp.stack([e[1] for e in every]).reshape(halves, -1)
    top_all = jnp.max(tops, axis=0)
    lse = top_all + jnp.log(jnp.sum(totals * jnp.exp(tops - top_all), axis=0))
    entry = lax.broadcasted_iota(jnp.int32, logits.shape, 1) + half * block
    onehot = (targets[:, None] == entry).astype(F32)
    loss_weight = 2.0 * entries / frames
    d_logit = ((jnp.exp(logits - lse[:, None]) - onehot) * loss_weight).astype(BF16)

    d_norm_rows = matmul(d_logit, head, ((1,), (1,)))
    d_norm = d_norm_rows[:owned]
    for k in range(1, halves):
        d_norm += turn_hid(d_norm_rows[k * owned : (k + 1) * owned].astype(BF16), k).astype(F32)

    gated = gain * d_norm
    d_x = scale * gated - x_rows * scale**3 * jnp.mean(gated * x_rows, axis=1, keepdims=True)
    d_round = d_x.astype(BF16)
    d_ratio_part = jnp.sum(d_x * proj, axis=1).reshape(steps, part)

    part_out = matmul(normed_rows, d_logit, ((0,), (0,))).astype(BF16)
    pieces = [d_round] + [along_hid(d_round, shift) for shift in range(1, hids)]
    d_ratio = pick(d_ratio_part, step)
    for r in range(1, steps):
        d_ratio += flip_seq(pick(d_ratio_part, (step + r) % steps), r)
    part_out = after(part_out, d_ratio)
    part_out = lax.all_to_all(part_out.reshape(seqs, depth // seqs, block), "seq", 0, 0)
    part_out = part_out.reshape(groups, steps, hids, head_rows, block).astype(F32).sum(0)
    part_out = part_out.astype(BF16)

    ratio_column = ratio_group.transpose(1, 0, 2).reshape(hids, owned, 1)
    scaled, mine, *others = spread(place, pieces, ratio_column, seqs, steps)
    scaled = lax.all_to_all(scaled, "seq", 0, 0)
    grad_in = input_gradient(place, turned, scaled, steps)

    d_ratio = gather_hid(d_ratio).reshape(rows)
    correction = ratio_own**3 * d_ratio / width_in
    factors = jnp.stack([ratio_own, correction])[:, :, None]
    mine = [mine] + [flip_seq(others[r - 1], r) for r in range(1, steps)]
    grad_hidden = hidden_gradient(place, mine, w_in, hidden, factors)

    sums = [None] * halves
    for shift in range(hids):
        piece = lax.dynamic_index_in_dim(part_out, (j + shift) % hids, 1, False)
        piece = along_hid(piece, shift) if shift else piece
        which = shift % halves
        piece = piece.astype(F32)
        sums[which] = piece if sums[which] is None else sums[which] + piece
    grad_out = jnp.zeros((steps, head_rows, halves, block), F32)
    for r in range(halves):
        grad_out = lax.dynamic_update_index_in_dim(grad_out, sums[r], (half - r) % halves, 2)
    grad_out = grad_out.transpose(1, 0, 2, 3).reshape(head_rows, steps, entries)
    return (grad_hidden, grad_in, grad_out)


def solution(mesh):
    placed = (
        P("seq", "hid"),
        P(None, "hid", None),
        P(),
        P(),
        P(("seq", "hid"), None, None),
        P(None, ("seq", "hid")),
    )
    return jax.shard_map(
        shards,
        mesh=mesh,
        in_specs=placed,
        out_specs=(P("seq", "hid"), P(None, "hid", "seq"), P(("seq", "hid"), None, None)),
        check_vma=False,
    )
```

profile of v0, /device:TPU:0, one launch (start us, length us, event | category | flops | bytes accessed | tf_op | source)
XLA Modules:
  0.0 189.2 jit_solution(4763690050528545813)
XLA Ops:
  2.0 1.2 multiply_reduce_fusion
  3.3 1.0 copy-done.2
  4.3 4.3 %shard_map.85 = (f32[128,1024]{1,0:T(8,128)S(1)}, bf16[128,1024]{1,0:T(8,128)(2,1)S(1)}, bf16[128,1024]{1,0:T(8,128)(2,1)S(1)}, bf16[128,1024]{1,0:T(8,128)(2,1)S(1)}) custom-call(s32[3]{0:T(128)S(1)} %pad_add_fusion.1.place_ref, bf16[256,1024]{1,0:T(8,128)(2,1)S(1)} %copy-done.2, bf16[256,1024]{1,0:T(8,128)(2,1)S(1)} %collective-permute-done.refs_1_, ...), custom_call_target="tpu_custom_call" | custom-call | flops 1073741824 | bytes 5242880 | tf_op jit(solution)/shard_map/pallas_call | solution.py:33
  8.8 1.1 collective-permute-done.1
  9.9 2.8 %collective-permute-start.2 = (f32[2,384]{1,0:T(2,128)S(1)}, f32[2,384]{1,0:T(2,128)S(1)}, u32[]{:S(2)}, u32[]{:S(2)}) collective-permute-start(f32[2,384]{1,0:T(2,128)S(1)} %dynamic_update_slice.31), channel_id=1, source_target_pairs={{0,1},{1,2},{2,3},{3,0},{4,5},{5,6},{6,7},{7,4},{8,9},{9,10},{10,1... | collective-permute-start | bytes 9224 | tf_op jit(solution)/shard_map/ppermute | solution.py:214
  13.0 2.2 %collective-permute-start.7 = (bf16[128,1024]{1,0:T(8,128)(2,1)S(1)}, bf16[128,1024]{1,0:T(8,128)(2,1)}, u32[]{:S(2)}, u32[]{:S(2)}) collective-permute-start(bf16[128,1024]{1,0:T(8,128)(2,1)S(1)} %get-tuple-element.16), channel_id=1, source_target_pairs={{0,3},{1,0},{2,1},{3,2},{4,7},{5,4},{6,5},{7,6},{8,11},{9,8},{10,9... | collective-permute-start | bytes 786440 | tf_op jit(solution)/shard_map/ppermute | solution.py:214
  16.1 1.6 collective-permute-start.5
  18.5 3.5 %all-to-all-start = ((bf16[4,2,32,1024]{3,2,1,0:T(8,128)(2,1)}), bf16[4,2,32,1024]{3,2,1,0:T(8,128)(2,1)S(1)}, u32[]{:S(2)}, u32[]{:S(2)}) async-start(bf16[4,2,32,1024]{3,2,1,0:T(8,128)(2,1)} %bitcast.10), calls=%async_computation | async-start | bytes 1048576 | tf_op jit(solution)/shard_map/all_to_all | solution.py:258
  22.0 2.9 %collective-permute-start.3 = (f32[2,384]{1,0:T(2,128)S(1)}, f32[2,384]{1,0:T(2,128)S(1)}, u32[]{:S(2)}, u32[]{:S(2)}) collective-permute-start(f32[2,384]{1,0:T(2,128)S(1)} %dynamic_update_slice.31), channel_id=1, source_target_pairs={{0,2},{1,3},{2,0},{3,1},{4,6},{5,7},{6,4},{7,5},{8,10},{9,11},{10,... | collective-permute-start | bytes 9224 | tf_op jit(solution)/shard_map/ppermute | solution.py:214
  24.9 1.5 collective-permute-start.4
  26.4 24.1 %collective-permute-done.3 = f32[2,384]{1,0:T(2,128)S(1)} collective-permute-done((f32[2,384]{1,0:T(2,128)S(1)}, f32[2,384]{1,0:T(2,128)S(1)}, u32[]{:S(2)}, u32[]{:S(2)}) %collective-permute-start.3) | collective-permute-done | bytes 3104 | tf_op jit(solution)/shard_map/ppermute | solution.py:214
  50.7 1.6 broadcast_in_dim.83
  52.3 3.7 %all-to-all-start.1 = ((bf16[8,128,1024]{2,1,0:T(8,128)(2,1)}), bf16[8,128,1024]{2,1,0:T(8,128)(2,1)S(1)}, u32[]{:S(2)}, u32[]{:S(2)}) async-start(bf16[8,128,1024]{2,1,0:T(8,128)(2,1)} %bitcast.13), calls=%async_computation.1 | async-start | bytes 4194304 | tf_op jit(solution)/shard_map/all_to_all | solution.py:278
  57.6 4.5 %gather_fusion = bf16[128,1024]{1,0:T(8,128)(2,1)} fusion(bf16[2048,1024]{1,0:T(8,128)(2,1)} %bitcast.70, s32[1024]{0:T(1024)S(1)} %pad_clamp_fusion), kind=kCustom, calls=%fused_computation | custom fusion | bytes 524800 | tf_op jit(solution)/shard_map/jit(_take)/gather | solution.py:284
  62.1 1.5 multiply_reduce_fusion.3
  64.6 8.1 %collective-permute-done.8 = bf16[128,1024]{1,0:T(8,128)(2,1)} collective-permute-done((bf16[128,1024]{1,0:T(8,128)(2,1)S(1)}, bf16[128,1024]{1,0:T(8,128)(2,1)}, u32[]{:S(2)}, u32[]{:S(2)}) %collective-permute-start.8) | collective-permute-done | bytes 262176 | tf_op jit(solution)/shard_map/ppermute | solution.py:217
  72.7 10.0 %all-to-all-done.1 = bf16[8,128,1024]{2,1,0:T(8,128)(2,1)S(1)} async-done(((bf16[8,128,1024]{2,1,0:T(8,128)(2,1)}), bf16[8,128,1024]{2,1,0:T(8,128)(2,1)S(1)}, u32[]{:S(2)}, u32[]{:S(2)}) %all-to-all-start.1) | async-done | bytes 2097184 | tf_op jit(solution)/shard_map/all_to_all | solution.py:278
  82.7 1.8 fusion.21
  85.4 3.0 %collective-permute-done.9 = f32[2,2,128]{2,1,0:T(2,128)S(1)} collective-permute-done((f32[2,2,128]{2,1,0:T(2,128)S(1)}, f32[2,2,128]{2,1,0:T(2,128)S(1)}, u32[]{:S(2)}, u32[]{:S(2)}) %collective-permute-start.9) | collective-permute-done | bytes 2080 | tf_op jit(solution)/shard_map/ppermute | solution.py:217
  90.1 5.8 %collective-permute-done.10 = bf16[128,1024]{1,0:T(8,128)(2,1)S(1)} collective-permute-done((bf16[128,1024]{1,0:T(8,128)(2,1)S(1)}, bf16[128,1024]{1,0:T(8,128)(2,1)S(1)}, u32[]{:S(2)}, u32[]{:S(2)}) %collective-permute-start.10) | collective-permute-done | bytes 262176 | tf_op jit(solution)/shard_map/ppermute | solution.py:217
  96.1 1.5 multiply_reduce_fusion.1
  97.7 3.3 %convolution_convert_fusion = bf16[1024,1024]{1,0:T(8,128)(2,1)} fusion(bf16[128,1024]{1,0:T(8,128)(2,1)} %collective-permute-done.8, bf16[128,1024]{1,0:T(8,128)(2,1)S(1)} %copy-done.11, f32[256,1024]{1,0:T(8,128)S(1)} %copy-done.8, s32[1024]{0:T(1024)S(1)} %iota_add_fusion, f32[256]{0:T(256)S(1)} %log_add_fusion, s32[256]{0:T(256)S(1)} %pad_add_fusion), kind=kOutput, calls=%fused_computation.1 | convolution fusion | flops 540540928 | bytes 3676160 | tf_op jit(solution)/shard_map/dot_general | solution.py:17
  101.0 4.5 %all-to-all-start.3 = ((bf16[8,128,1024]{2,1,0:T(8,128)(2,1)}), bf16[8,128,1024]{2,1,0:T(8,128)(2,1)}, u32[]{:S(2)}, u32[]{:S(2)}) async-start(bf16[8,128,1024]{2,1,0:T(8,128)(2,1)} %bitcast.68), calls=%async_computation.3 | async-start | bytes 4194304 | tf_op jit(solution)/shard_map/all_to_all | solution.py:325
  106.2 3.3 %collective-permute-start.12 = (bf16[128,1024]{1,0:T(8,128)(2,1)S(1)}, bf16[128,1024]{1,0:T(8,128)(2,1)S(1)}, u32[]{:S(2)}, u32[]{:S(2)}) collective-permute-start(bf16[128,1024]{1,0:T(8,128)(2,1)S(1)} %get-tuple-element.28.refs_0_), channel_id=1, source_target_pairs={{0,2},{1,3},{2,0},{3,1},{4,6},{5,7},{6,4},{7,5},{8,10},{9,11},{10,... | collective-permute-start | bytes 786440 | tf_op jit(solution)/shard_map/ppermute | solution.py:214
  110.6 1.9 %collective-permute-start.20 = (bf16[1024,256]{1,0:T(8,128)(2,1)S(1)}, bf16[1024,256]{1,0:T(8,128)(2,1)S(1)}, u32[]{:S(2)}, u32[]{:S(2)}) collective-permute-start(bf16[1024,256]{1,0:T(8,128)(2,1)S(1)} %bitcast.60), channel_id=1, source_target_pairs={{0,8},{4,12},{8,16},{12,20},{16,24},{20,28},{24,0},{28,4},{1,9},{5... | collective-permute-start | bytes 1572872 | tf_op jit(solution)/shard_map/ppermute | solution.py:249
  112.5 1.5 collective-permute-start.22
  114.0 2.7 %collective-permute-done.11.refs_1_ = bf16[128,1024]{1,0:T(8,128)(2,1)S(1)} collective-permute-done((bf16[128,1024]{1,0:T(8,128)(2,1)S(1)}, bf16[128,1024]{1,0:T(8,128)(2,1)S(1)}, u32[]{:S(2)}, u32[]{:S(2)}) %collective-permute-start.11) | collective-permute-done | bytes 262176 | tf_op jit(solution)/shard_map/ppermute | solution.py:214
  116.6 2.8 %collective-permute-start.24 = (bf16[1024,256]{1,0:T(8,128)(2,1)S(1)}, bf16[1024,256]{1,0:T(8,128)(2,1)}, u32[]{:S(2)}, u32[]{:S(2)}) collective-permute-start(bf16[1024,256]{1,0:T(8,128)(2,1)S(1)} %bitcast.62), channel_id=1, source_target_pairs={{0,24},{4,28},{8,0},{12,4},{16,8},{20,12},{24,16},{28,20},{1,25},{... | collective-permute-start | bytes 1572872 | tf_op jit(solution)/shard_map/ppermute | solution.py:249
  119.7 7.7 %collective-permute-done.12.refs_2_ = bf16[128,1024]{1,0:T(8,128)(2,1)S(1)} collective-permute-done((bf16[128,1024]{1,0:T(8,128)(2,1)S(1)}, bf16[128,1024]{1,0:T(8,128)(2,1)S(1)}, u32[]{:S(2)}, u32[]{:S(2)}) %collective-permute-start.12) | collective-permute-done | bytes 262176 | tf_op jit(solution)/shard_map/ppermute | solution.py:214
  127.4 1.8 shard_map.86
  130.7 2.0 %all-to-all-done.3 = bf16[8,128,1024]{2,1,0:T(8,128)(2,1)} async-done(((bf16[8,128,1024]{2,1,0:T(8,128)(2,1)}), bf16[8,128,1024]{2,1,0:T(8,128)(2,1)}, u32[]{:S(2)}, u32[]{:S(2)}) %all-to-all-start.3) | async-done | bytes 2097184 | tf_op jit(solution)/shard_map/all_to_all | solution.py:325
  132.8 3.6 %all-to-all-start.2 = ((bf16[8,512,128]{2,1,0:T(8,128)(2,1)}), bf16[8,512,128]{2,1,0:T(8,128)(2,1)S(1)}, u32[]{:S(2)}, u32[]{:S(2)}) async-start(bf16[8,512,128]{2,1,0:T(8,128)(2,1)} %get-tuple-element.23), calls=%async_computation.2 | async-start | bytes 2097152 | tf_op jit(solution)/shard_map/all_to_all | solution.py:331
  136.4 4.2 %collective-permute-start.16 = (f32[64]{0:T(128)S(1)}, f32[64]{0:T(128)S(1)}, u32[]{:S(2)}, u32[]{:S(2)}) collective-permute-start(f32[64]{0:T(128)S(1)} %fusion.13), channel_id=1, source_target_pairs={{0,1},{1,2},{2,3},{3,0},{4,5},{5,6},{6,7},{7,4},{8,9},{9,10},{10,1... | collective-permute-start | bytes 776 | tf_op jit(solution)/shard_map/ppermute | solution.py:214
  142.6 2.4 %collective-permute-done.17 = f32[64]{0:T(128)S(1)} collective-permute-done((f32[64]{0:T(128)S(1)}, f32[64]{0:T(128)S(1)}, u32[]{:S(2)}, u32[]{:S(2)}) %collective-permute-start.17) | collective-permute-done | bytes 288 | tf_op jit(solution)/shard_map/ppermute | solution.py:214
  145.6 8.4 %collective-permute-done.22.refs_4_ = bf16[1024,256]{1,0:T(8,128)(2,1)S(1)} collective-permute-done((bf16[1024,256]{1,0:T(8,128)(2,1)S(1)}, bf16[1024,256]{1,0:T(8,128)(2,1)S(1)}, u32[]{:S(2)}, u32[]{:S(2)}) %collective-permute-start.22) | collective-permute-done | bytes 524320 | tf_op jit(solution)/shard_map/ppermute | solution.py:249
  155.1 2.9 %reduce_sum.82 = bf16[2,4,32,1024]{3,2,1,0:T(8,128)(2,1)} reduce(bf16[4,2,4,32,1024]{4,3,2,1,0:T(8,128)(2,1)} %bitcast.31, bf16[]{:T(256)} %constant.279.clone.1), dimensions={0}, to_apply=%region_8.9 | reduce | flops 786432 | bytes 2621442 | tf_op jit(solution)/shard_map/reduce_sum | solution.py:326
  158.0 1.8 dynamic-slice_bitcast_fusion.1
  159.8 1.9 collective-permute-start.26
  161.6 2.2 %copy-done.1 = bf16[2,1024,1024]{2,1,0:T(8,128)(2,1)S(1)} copy-done((bf16[2,1024,1024]{2,1,0:T(8,128)(2,1)S(1)}, bf16[2,1024,1024]{2,1,0:T(8,128)(2,1)}, u32[]{:S(2)}) %copy-start.1) | copy-done | bytes 4194328
  163.8 1.0 copy-done.5
  164.9 4.6 %shard_map.87 = bf16[256,1024]{1,0:T(8,128)(2,1)} custom-call(s32[3]{0:T(128)S(1)} %pad_add_fusion.1.place_ref, bf16[256,1024]{1,0:T(8,128)(2,1)S(1)} %copy-done.5, bf16[256,1024]{1,0:T(8,128)(2,1)} %collective-permute-done.14.refs_1_, bf16[2,1024,1024]{2,1,0:T(8,128)(2,1)S(1)} %copy-done.1, bf16[256,1024]{1,0:T(8,128)(2,1)S(1)} %copy-done.3, ...), custom_call_target="tpu_custom_call" | custom-call | flops 1073741824 | bytes 5769216 | tf_op jit(solution)/shard_map/pallas_call | solution.py:33
  169.5 5.2 %shard_map.88 = f32[2,1024,128]{2,1,0:T(8,128)} custom-call(s32[3]{0:T(128)S(1)} %pad_add_fusion.1.place_ref, bf16[1024,256]{1,0:T(8,128)(2,1)S(1)} %bitcast.64, bf16[1024,256]{1,0:T(8,128)(2,1)} %collective-permute-done.19.refs_1_, bf16[1024,256]{1,0:T(8,128)(2,1)S(1)} %collective-permute-done.20.refs_2_, ...), custom_call_target="tpu_custom_call" | custom-call | flops 1073741824 | bytes 5242880 | tf_op jit(solution)/shard_map/pallas_call | solution.py:33
  174.7 1.4 collective-permute-start.28
  178.0 2.4 %collective-permute-done.28 = bf16[2,32,1024]{2,1,0:T(8,128)(2,1)S(1)} collective-permute-done((bf16[2,32,1024]{2,1,0:T(8,128)(2,1)S(1)}, bf16[2,32,1024]{2,1,0:T(8,128)(2,1)S(1)}, u32[]{:S(2)}, u32[]{:S(2)}) %collective-permute-start.28) | collective-permute-done | bytes 131104 | tf_op jit(solution)/shard_map/ppermute | solution.py:214
  180.4 3.1 %collective-permute-done.27 = bf16[2,32,1024]{2,1,0:T(8,128)(2,1)S(1)} collective-permute-done((bf16[2,32,1024]{2,1,0:T(8,128)(2,1)S(1)}, bf16[2,32,1024]{2,1,0:T(8,128)(2,1)S(1)}, u32[]{:S(2)}, u32[]{:S(2)}) %collective-permute-start.27) | collective-permute-done | bytes 131104 | tf_op jit(solution)/shard_map/ppermute | solution.py:214
  184.1 1.9 dynamic_update_slice.38
  185.9 1.9 dynamic_update_slice.39
  187.8 1.4 reshape.216
  (130 shorter events, 18.7 us)
Async XLA Ops:
  0.6 2.6 %copy-start = (f32[2,1024]{1,0:T(2,128)S(1)}, f32[2,1024]{1,0:T(2,128)}, u32[]{:S(2)}) copy-start(f32[2,1024]{1,0:T(2,128)} %param.9) | copy-start | bytes 24580
  0.6 2.6 %collective-permute-start = (bf16[256,1024]{1,0:T(8,128)(2,1)}, bf16[256,1024]{1,0:T(8,128)(2,1)S(1)}, u32[]{:S(2)}, u32[]{:S(2)}) collective-permute-start(bf16[256,1024]{1,0:T(8,128)(2,1)} %refs_3_.1), channel_id=1, source_target_pairs={{0,4},{4,0},{8,12},{12,8},{16,20},{20,16},{24,28},{28,24},{1,5},{5... | collective-permute-start | bytes 1572872 | tf_op jit(solution)/shard_map/ppermute | solution.py:224
  3.3 1.0 copy-start.2
  4.3 8.4 %copy-start.9 = (bf16[32,2,2048]{2,1,0:T(2,128)(2,1)S(1)}, bf16[32,2,2048]{2,1,0:T(2,128)(2,1)}, u32[]{:S(2)}) copy-start(bf16[32,2,2048]{2,1,0:T(2,128)(2,1)} %param.10) | copy-start | bytes 786436
  8.6 1.2 collective-permute-start.1
  9.9 15.0 %collective-permute-start.2 = (f32[2,384]{1,0:T(2,128)S(1)}, f32[2,384]{1,0:T(2,128)S(1)}, u32[]{:S(2)}, u32[]{:S(2)}) collective-permute-start(f32[2,384]{1,0:T(2,128)S(1)} %dynamic_update_slice.31), channel_id=1, source_target_pairs={{0,1},{1,2},{2,3},{3,0},{4,5},{5,6},{6,7},{7,4},{8,9},{9,10},{10,1... | collective-permute-start | bytes 9224 | tf_op jit(solution)/shard_map/ppermute | solution.py:214
  13.0 49.1 %collective-permute-start.7 = (bf16[128,1024]{1,0:T(8,128)(2,1)S(1)}, bf16[128,1024]{1,0:T(8,128)(2,1)}, u32[]{:S(2)}, u32[]{:S(2)}) collective-permute-start(bf16[128,1024]{1,0:T(8,128)(2,1)S(1)} %get-tuple-element.16), channel_id=1, source_target_pairs={{0,3},{1,0},{2,1},{3,2},{4,7},{5,4},{6,5},{7,6},{8,11},{9,8},{10,9... | collective-permute-start | bytes 786440 | tf_op jit(solution)/shard_map/ppermute | solution.py:214
  15.1 47.0 %collective-permute-start.6 = (bf16[128,1024]{1,0:T(8,128)(2,1)S(1)}, bf16[128,1024]{1,0:T(8,128)(2,1)}, u32[]{:S(2)}, u32[]{:S(2)}) collective-permute-start(bf16[128,1024]{1,0:T(8,128)(2,1)S(1)} %get-tuple-element.15), channel_id=1, source_target_pairs={{0,2},{1,3},{2,0},{3,1},{4,6},{5,7},{6,4},{7,5},{8,10},{9,11},{10,... | collective-permute-start | bytes 786440 | tf_op jit(solution)/shard_map/ppermute | solution.py:214
  16.1 46.1 %collective-permute-start.5 = (bf16[128,1024]{1,0:T(8,128)(2,1)S(1)}, bf16[128,1024]{1,0:T(8,128)(2,1)}, u32[]{:S(2)}, u32[]{:S(2)}) collective-permute-start(bf16[128,1024]{1,0:T(8,128)(2,1)S(1)} %get-tuple-element.14), channel_id=1, source_target_pairs={{0,1},{1,2},{2,3},{3,0},{4,5},{5,6},{6,7},{7,4},{8,9},{9,10},{10,1... | collective-permute-start | bytes 786440 | tf_op jit(solution)/shard_map/ppermute | solution.py:214
  18.5 32.2 %all-to-all-start = ((bf16[4,2,32,1024]{3,2,1,0:T(8,128)(2,1)}), bf16[4,2,32,1024]{3,2,1,0:T(8,128)(2,1)S(1)}, u32[]{:S(2)}, u32[]{:S(2)}) async-start(bf16[4,2,32,1024]{3,2,1,0:T(8,128)(2,1)} %bitcast.10), calls=%async_computation | async-start | bytes 1048576 | tf_op jit(solution)/shard_map/all_to_all | solution.py:258
  22.0 28.5 %collective-permute-start.3 = (f32[2,384]{1,0:T(2,128)S(1)}, f32[2,384]{1,0:T(2,128)S(1)}, u32[]{:S(2)}, u32[]{:S(2)}) collective-permute-start(f32[2,384]{1,0:T(2,128)S(1)} %dynamic_update_slice.31), channel_id=1, source_target_pairs={{0,2},{1,3},{2,0},{3,1},{4,6},{5,7},{6,4},{7,5},{8,10},{9,11},{10,... | collective-permute-start | bytes 9224 | tf_op jit(solution)/shard_map/ppermute | solution.py:214
  24.9 25.6 %collective-permute-start.4 = (f32[2,384]{1,0:T(2,128)S(1)}, f32[2,384]{1,0:T(2,128)S(1)}, u32[]{:S(2)}, u32[]{:S(2)}) collective-permute-start(f32[2,384]{1,0:T(2,128)S(1)} %dynamic_update_slice.31), channel_id=1, source_target_pairs={{0,3},{1,0},{2,1},{3,2},{4,7},{5,4},{6,5},{7,6},{8,11},{9,8},{10,9... | collective-permute-start | bytes 9224 | tf_op jit(solution)/shard_map/ppermute | solution.py:214
  52.3 30.4 %all-to-all-start.1 = ((bf16[8,128,1024]{2,1,0:T(8,128)(2,1)}), bf16[8,128,1024]{2,1,0:T(8,128)(2,1)S(1)}, u32[]{:S(2)}, u32[]{:S(2)}) async-start(bf16[8,128,1024]{2,1,0:T(8,128)(2,1)} %bitcast.13), calls=%async_computation.1 | async-start | bytes 4194304 | tf_op jit(solution)/shard_map/all_to_all | solution.py:278
  63.8 21.0 %copy-start.10 = (bf16[128,1024]{1,0:T(8,128)(2,1)}, bf16[128,1024]{1,0:T(8,128)(2,1)S(1)}, u32[]{:S(2)}) copy-start(bf16[128,1024]{1,0:T(8,128)(2,1)S(1)} %multiply_convert_fusion.1) | copy-start | bytes 786436
  63.8 8.9 %collective-permute-start.8 = (bf16[128,1024]{1,0:T(8,128)(2,1)S(1)}, bf16[128,1024]{1,0:T(8,128)(2,1)}, u32[]{:S(2)}, u32[]{:S(2)}) collective-permute-start(bf16[128,1024]{1,0:T(8,128)(2,1)S(1)} %multiply_convert_fusion.1), channel_id=1, source_target_pairs={{0,1},{1,0},{2,3},{3,2},{4,5},{5,4},{6,7},{7,6},{8,9},{9,8},{10,11... | collective-permute-start | bytes 786440 | tf_op jit(solution)/shard_map/ppermute | solution.py:217
  84.4 5.0 %copy-start.7 = (f32[256,1024]{1,0:T(8,128)}, f32[256,1024]{1,0:T(8,128)S(1)}, u32[]{:S(2)}) copy-start(f32[256,1024]{1,0:T(8,128)S(1)} %get-tuple-element.45) | copy-start | bytes 3145732
  84.8 3.7 %collective-permute-start.9 = (f32[2,2,128]{2,1,0:T(2,128)S(1)}, f32[2,2,128]{2,1,0:T(2,128)S(1)}, u32[]{:S(2)}, u32[]{:S(2)}) collective-permute-start(f32[2,2,128]{2,1,0:T(2,128)S(1)} %pad_maximum_fusion.4), channel_id=1, source_target_pairs={{0,1},{1,0},{2,3},{3,2},{4,5},{5,4},{6,7},{7,6},{8,9},{9,8},{10,11... | collective-permute-start | bytes 6152 | tf_op jit(solution)/shard_map/ppermute | solution.py:217
  89.4 8.3 %copy-start.8 = (f32[256,1024]{1,0:T(8,128)S(1)}, f32[256,1024]{1,0:T(8,128)}, u32[]{:S(2)}) copy-start(f32[256,1024]{1,0:T(8,128)} %copy-done.7) | copy-start | bytes 3145732
  89.5 8.3 %copy-start.11 = (bf16[128,1024]{1,0:T(8,128)(2,1)S(1)}, bf16[128,1024]{1,0:T(8,128)(2,1)}, u32[]{:S(2)}) copy-start(bf16[128,1024]{1,0:T(8,128)(2,1)} %copy-done.10) | copy-start | bytes 786436
  89.5 6.4 %collective-permute-start.10 = (bf16[128,1024]{1,0:T(8,128)(2,1)S(1)}, bf16[128,1024]{1,0:T(8,128)(2,1)S(1)}, u32[]{:S(2)}, u32[]{:S(2)}) collective-permute-start(bf16[128,1024]{1,0:T(8,128)(2,1)S(1)} %slice.65), channel_id=1, source_target_pairs={{0,1},{1,0},{2,3},{3,2},{4,5},{5,4},{6,7},{7,6},{8,9},{9,8},{10,11... | collective-permute-start | bytes 786440 | tf_op jit(solution)/shard_map/ppermute | solution.py:217
  97.7 3.3 %collective-permute-start.15 = (f32[64]{0:T(128)S(1)}, f32[64]{0:T(128)S(1)}, u32[]{:S(2)}, u32[]{:S(2)}) collective-permute-start(f32[64]{0:T(128)S(1)} %fusion.14), channel_id=1, source_target_pairs={{0,4},{4,0},{8,12},{12,8},{16,20},{20,16},{24,28},{28,24},{1,5},{5... | collective-permute-start | bytes 776 | tf_op jit(solution)/shard_map/ppermute | solution.py:224
  101.0 9.4 %copy-start.3 = (bf16[256,1024]{1,0:T(8,128)(2,1)S(1)}, bf16[256,1024]{1,0:T(8,128)(2,1)}, u32[]{:S(2)}) copy-start(bf16[256,1024]{1,0:T(8,128)(2,1)} %refs_3_.1) | copy-start | bytes 1572868
  101.0 31.7 %all-to-all-start.3 = ((bf16[8,128,1024]{2,1,0:T(8,128)(2,1)}), bf16[8,128,1024]{2,1,0:T(8,128)(2,1)}, u32[]{:S(2)}, u32[]{:S(2)}) async-start(bf16[8,128,1024]{2,1,0:T(8,128)(2,1)} %bitcast.68), calls=%async_computation.3 | async-start | bytes 4194304 | tf_op jit(solution)/shard_map/all_to_all | solution.py:325
  105.5 11.1 %collective-permute-start.11 = (bf16[128,1024]{1,0:T(8,128)(2,1)S(1)}, bf16[128,1024]{1,0:T(8,128)(2,1)S(1)}, u32[]{:S(2)}, u32[]{:S(2)}) collective-permute-start(bf16[128,1024]{1,0:T(8,128)(2,1)S(1)} %get-tuple-element.28.refs_0_), channel_id=1, source_target_pairs={{0,1},{1,2},{2,3},{3,0},{4,5},{5,6},{6,7},{7,4},{8,9},{9,10},{10,1... | collective-permute-start | bytes 786440 | tf_op jit(solution)/shard_map/ppermute | solution.py:214
  106.2 21.2 %collective-permute-start.12 = (bf16[128,1024]{1,0:T(8,128)(2,1)S(1)}, bf16[128,1024]{1,0:T(8,128)(2,1)S(1)}, u32[]{:S(2)}, u32[]{:S(2)}) collective-permute-start(bf16[128,1024]{1,0:T(8,128)(2,1)S(1)} %get-tuple-element.28.refs_0_), channel_id=1, source_target_pairs={{0,2},{1,3},{2,0},{3,1},{4,6},{5,7},{6,4},{7,5},{8,10},{9,11},{10,... | collective-permute-start | bytes 786440 | tf_op jit(solution)/shard_map/ppermute | solution.py:214
  109.5 17.9 %collective-permute-start.13 = (bf16[128,1024]{1,0:T(8,128)(2,1)S(1)}, bf16[128,1024]{1,0:T(8,128)(2,1)S(1)}, u32[]{:S(2)}, u32[]{:S(2)}) collective-permute-start(bf16[128,1024]{1,0:T(8,128)(2,1)S(1)} %get-tuple-element.28.refs_0_), channel_id=1, source_target_pairs={{0,3},{1,0},{2,1},{3,2},{4,7},{5,4},{6,5},{7,6},{8,11},{9,8},{10,9... | collective-permute-start | bytes 786440 | tf_op jit(solution)/shard_map/ppermute | solution.py:214
  110.6 35.0 %collective-permute-start.20 = (bf16[1024,256]{1,0:T(8,128)(2,1)S(1)}, bf16[1024,256]{1,0:T(8,128)(2,1)S(1)}, u32[]{:S(2)}, u32[]{:S(2)}) collective-permute-start(bf16[1024,256]{1,0:T(8,128)(2,1)S(1)} %bitcast.60), channel_id=1, source_target_pairs={{0,8},{4,12},{8,16},{12,20},{16,24},{20,28},{24,0},{28,4},{1,9},{5... | collective-permute-start | bytes 1572872 | tf_op jit(solution)/shard_map/ppermute | solution.py:249
  112.5 41.6 %collective-permute-start.22 = (bf16[1024,256]{1,0:T(8,128)(2,1)S(1)}, bf16[1024,256]{1,0:T(8,128)(2,1)S(1)}, u32[]{:S(2)}, u32[]{:S(2)}) collective-permute-start(bf16[1024,256]{1,0:T(8,128)(2,1)S(1)} %bitcast.61), channel_id=1, source_target_pairs={{0,16},{4,20},{8,24},{12,28},{16,0},{20,4},{24,8},{28,12},{1,17},{... | collective-permute-start | bytes 1572872 | tf_op jit(solution)/shard_map/ppermute | solution.py:249
  116.6 37.6 %collective-permute-start.24 = (bf16[1024,256]{1,0:T(8,128)(2,1)S(1)}, bf16[1024,256]{1,0:T(8,128)(2,1)}, u32[]{:S(2)}, u32[]{:S(2)}) collective-permute-start(bf16[1024,256]{1,0:T(8,128)(2,1)S(1)} %bitcast.62), channel_id=1, source_target_pairs={{0,24},{4,28},{8,0},{12,4},{16,8},{20,12},{24,16},{28,20},{1,25},{... | collective-permute-start | bytes 1572872 | tf_op jit(solution)/shard_map/ppermute | solution.py:249
  129.1 0.8 copy-start.4
  129.9 0.8 copy-start.6
  132.8 36.7 %all-to-all-start.2 = ((bf16[8,512,128]{2,1,0:T(8,128)(2,1)}), bf16[8,512,128]{2,1,0:T(8,128)(2,1)S(1)}, u32[]{:S(2)}, u32[]{:S(2)}) async-start(bf16[8,512,128]{2,1,0:T(8,128)(2,1)} %get-tuple-element.23), calls=%async_computation.2 | async-start | bytes 2097152 | tf_op jit(solution)/shard_map/all_to_all | solution.py:331
  136.4 6.1 %collective-permute-start.16 = (f32[64]{0:T(128)S(1)}, f32[64]{0:T(128)S(1)}, u32[]{:S(2)}, u32[]{:S(2)}) collective-permute-start(f32[64]{0:T(128)S(1)} %fusion.13), channel_id=1, source_target_pairs={{0,1},{1,2},{2,3},{3,0},{4,5},{5,6},{6,7},{7,4},{8,9},{9,10},{10,1... | collective-permute-start | bytes 776 | tf_op jit(solution)/shard_map/ppermute | solution.py:214
  140.6 4.4 %collective-permute-start.17 = (f32[64]{0:T(128)S(1)}, f32[64]{0:T(128)S(1)}, u32[]{:S(2)}, u32[]{:S(2)}) collective-permute-start(f32[64]{0:T(128)S(1)} %fusion.13), channel_id=1, source_target_pairs={{0,2},{1,3},{2,0},{3,1},{4,6},{5,7},{6,4},{7,5},{8,10},{9,11},{10,... | collective-permute-start | bytes 776 | tf_op jit(solution)/shard_map/ppermute | solution.py:214
  142.5 17.3 %collective-permute-start.14 = (bf16[256,1024]{1,0:T(8,128)(2,1)}, bf16[256,1024]{1,0:T(8,128)(2,1)}, u32[]{:S(2)}, u32[]{:S(2)}) collective-permute-start(bf16[256,1024]{1,0:T(8,128)(2,1)} %copy-done.6), channel_id=1, source_target_pairs={{0,4},{4,0},{8,12},{12,8},{16,20},{20,16},{24,28},{28,24},{1,5},{5... | collective-permute-start | bytes 1572872 | tf_op jit(solution)/shard_map/ppermute | solution.py:224
  145.1 9.5 %collective-permute-start.18 = (f32[64]{0:T(128)S(1)}, f32[64]{0:T(128)S(1)}, u32[]{:S(2)}, u32[]{:S(2)}) collective-permute-start(f32[64]{0:T(128)S(1)} %fusion.13), channel_id=1, source_target_pairs={{0,3},{1,0},{2,1},{3,2},{4,7},{5,4},{6,5},{7,6},{8,11},{9,8},{10,9... | collective-permute-start | bytes 776 | tf_op jit(solution)/shard_map/ppermute | solution.py:214
  145.5 23.9 %collective-permute-start.19 = (bf16[1024,256]{1,0:T(8,128)(2,1)S(1)}, bf16[1024,256]{1,0:T(8,128)(2,1)}, u32[]{:S(2)}, u32[]{:S(2)}) collective-permute-start(bf16[1024,256]{1,0:T(8,128)(2,1)S(1)} %bitcast.63), channel_id=1, source_target_pairs={{0,4},{4,0},{8,12},{12,8},{16,20},{20,16},{24,28},{28,24},{1,5},{5... | collective-permute-start | bytes 1572872 | tf_op jit(solution)/shard_map/ppermute | solution.py:224
  154.1 15.4 %collective-permute-start.21 = (bf16[1024,256]{1,0:T(8,128)(2,1)S(1)}, bf16[1024,256]{1,0:T(8,128)(2,1)}, u32[]{:S(2)}, u32[]{:S(2)}) collective-permute-start(bf16[1024,256]{1,0:T(8,128)(2,1)S(1)} %collective-permute-done.20.refs_2_), channel_id=1, source_target_pairs={{0,4},{4,0},{8,12},{12,8},{16,20},{20,16},{24,28},{28,24},{1,5},{5... | collective-permute-start | bytes 1572872 | tf_op jit(solution)/shard_map/ppermute | solution.py:224
  154.2 15.2 %collective-permute-start.23 = (bf16[1024,256]{1,0:T(8,128)(2,1)S(1)}, bf16[1024,256]{1,0:T(8,128)(2,1)}, u32[]{:S(2)}, u32[]{:S(2)}) collective-permute-start(bf16[1024,256]{1,0:T(8,128)(2,1)S(1)} %collective-permute-done.22.refs_4_), channel_id=1, source_target_pairs={{0,4},{4,0},{8,12},{12,8},{16,20},{20,16},{24,28},{28,24},{1,5},{5... | collective-permute-start | bytes 1572872 | tf_op jit(solution)/shard_map/ppermute | solution.py:224
  154.6 14.9 %collective-permute-start.25 = (bf16[1024,256]{1,0:T(8,128)(2,1)}, bf16[1024,256]{1,0:T(8,128)(2,1)}, u32[]{:S(2)}, u32[]{:S(2)}) collective-permute-start(bf16[1024,256]{1,0:T(8,128)(2,1)} %collective-permute-done.24.refs_6_), channel_id=1, source_target_pairs={{0,4},{4,0},{8,12},{12,8},{16,20},{20,16},{24,28},{28,24},{1,5},{5... | collective-permute-start | bytes 1572872 | tf_op jit(solution)/shard_map/ppermute | solution.py:224
  159.8 17.0 %collective-permute-start.26 = (bf16[2,32,1024]{2,1,0:T(8,128)(2,1)}, bf16[2,32,1024]{2,1,0:T(8,128)(2,1)S(1)}, u32[]{:S(2)}, u32[]{:S(2)}) collective-permute-start(bf16[2,32,1024]{2,1,0:T(8,128)(2,1)} %get-tuple-element.37), channel_id=1, source_target_pairs={{0,2},{1,3},{2,0},{3,1},{4,6},{5,7},{6,4},{7,5},{8,10},{9,11},{10,... | collective-permute-start | bytes 393224 | tf_op jit(solution)/shard_map/ppermute | solution.py:214
  161.6 2.2 %copy-start.1 = (bf16[2,1024,1024]{2,1,0:T(8,128)(2,1)S(1)}, bf16[2,1024,1024]{2,1,0:T(8,128)(2,1)}, u32[]{:S(2)}) copy-start(bf16[2,1024,1024]{2,1,0:T(8,128)(2,1)} %refs_2_.3) | copy-start | bytes 12582916
  163.8 1.0 copy-start.5
  169.5 5.2 %copy-start.13 = (bf16[2,32,1024]{2,1,0:T(8,128)(2,1)S(1)}, bf16[2,32,1024]{2,1,0:T(8,128)(2,1)}, u32[]{:S(2)}) copy-start(bf16[2,32,1024]{2,1,0:T(8,128)(2,1)} %get-tuple-element.36) | copy-start | bytes 393220
  169.5 6.7 %copy-start.12 = (bf16[2,32,1024]{2,1,0:T(8,128)(2,1)S(1)}, bf16[2,32,1024]{2,1,0:T(8,128)(2,1)}, u32[]{:S(2)}) copy-start(bf16[2,32,1024]{2,1,0:T(8,128)(2,1)} %get-tuple-element.35) | copy-start | bytes 393220
  174.7 5.7 %collective-permute-start.28 = (bf16[2,32,1024]{2,1,0:T(8,128)(2,1)S(1)}, bf16[2,32,1024]{2,1,0:T(8,128)(2,1)S(1)}, u32[]{:S(2)}, u32[]{:S(2)}) collective-permute-start(bf16[2,32,1024]{2,1,0:T(8,128)(2,1)S(1)} %copy-done.13), channel_id=1, source_target_pairs={{0,3},{1,0},{2,1},{3,2},{4,7},{5,4},{6,5},{7,6},{8,11},{9,8},{10,9... | collective-permute-start | bytes 393224 | tf_op jit(solution)/shard_map/ppermute | solution.py:214
  176.1 7.4 %collective-permute-start.27 = (bf16[2,32,1024]{2,1,0:T(8,128)(2,1)S(1)}, bf16[2,32,1024]{2,1,0:T(8,128)(2,1)S(1)}, u32[]{:S(2)}, u32[]{:S(2)}) collective-permute-start(bf16[2,32,1024]{2,1,0:T(8,128)(2,1)S(1)} %copy-done.12), channel_id=1, source_target_pairs={{0,1},{1,2},{2,3},{3,0},{4,5},{5,6},{6,7},{7,4},{8,9},{9,10},{10,1... | collective-permute-start | bytes 393224 | tf_op jit(solution)/shard_map/ppermute | solution.py:214
where the time goes:
time: 190 us; the launch traced here: 189 us
  waiting for transfers between devices  82.1 us (43%)
  starting transfers between devices  50.9 us (27%)
  local copies, waits for them, and re-layouts  23.7 us (12%)
  Pallas kernels  15.8 us (8%)
  other arithmetic  9.7 us (5%)
  matrix products  5.91 us (3%)
    ppermute x15, waiting for transfers between devices, along_hid(): lax.ppermute(values, 'hid', [(a, (a + shift) % hids) for a in range(hids)])  43.4 us
    ppermute x15, starting transfers between devices, along_hid(): lax.ppermute(values, 'hid', [(a, (a + shift) % hids) for a in range(hids)])  26.2 us
    ppermute x3, waiting for transfers between devices, turn_hid(): lax.ppermute(values, 'hid', [(a, a - a % halves + (a % halves + shift) %...  16.8 us
    pallas_call x4, Pallas kernels, call(): pl.pallas_call(kernel, grid_spec=pltpu.PrefetchScalarGridSpec(num_scalar_...  15.8 us
    all_to_all x1, waiting for transfers between devices, shards(): head = lax.all_to_all(head_send, 'seq', 0, 0).reshape(depth, block)  10 us
    ppermute x3, waiting for transfers between devices, along_groups(): lax.ppermute(values, 'seq', [(a, (a + shift * steps) % seqs) for a in ran...  8.63 us
    ppermute x3, starting transfers between devices, along_groups(): lax.ppermute(values, 'seq', [(a, (a + shift * steps) % seqs) for a in ran...  6.2 us
    unnamed x29, local copies, waits for them, and re-layouts  6.1 us
  transfers between devices with their start and end apart: 33, of which 15 were waited for; matrix products, arithmetic and copies ran while one was open for 12% of the time, Pallas kernels for 6%

commit v1 on v0

v1 whole, which is shorter than its diff:
```python
import jax
import jax.numpy as jnp
from jax import lax
from jax.experimental import pallas as pl
from jax.experimental.pallas import tpu as pltpu
from jax.sharding import PartitionSpec as P

F32 = jnp.float32
BF16 = jnp.bfloat16


def pick(values, index):
    return lax.dynamic_index_in_dim(values, index, axis=0, keepdims=False)


def matmul(a, b, contract):
    return lax.dot_general(a, b, (contract, ((), ())), preferred_element_type=F32)


def after(value, *others):
    return lax.optimization_barrier((value, *others))[0]


VMEM = pltpu.CompilerParams(vmem_limit_bytes=48 * 2**20)


def whole(shape):
    return pl.BlockSpec(shape, lambda n, place: (0,) * len(shape))


def call(kernel, place, grid, in_specs, out_specs, out_shape, scratch, flops, args):
    moved = sum(a.size * a.dtype.itemsize for a in args)
    return pl.pallas_call(
        kernel,
        grid_spec=pltpu.PrefetchScalarGridSpec(
            num_scalar_prefetch=1,
            grid=(grid,),
            in_specs=in_specs,
            out_specs=out_specs,
            scratch_shapes=scratch,
        ),
        out_shape=out_shape,
        compiler_params=VMEM,
        cost_estimate=pl.CostEstimate(flops=flops, bytes_accessed=moved, transcendentals=0),
    )(place, *args)


EXTRA = 128


def parts_of(columns, count):
    rows = columns[0].shape[0]
    lane = lax.broadcasted_iota(jnp.int32, (rows, EXTRA), 1)
    out = jnp.zeros((rows, EXTRA), F32)
    for c in range(count):
        left = columns[c]
        for k in range(3):
            piece = left.astype(BF16).astype(F32)
            left = left - piece
            out = jnp.where(lane == 3 * c + k, piece, out)
    return out.astype(BF16)


def column_of(extra, c):
    return sum(extra[:, 3 * c + k : 3 * c + k + 1].astype(F32) for k in (2, 1, 0))


def project(place, group, w_in, hids):
    steps = len(group)
    rows, units = group[0].shape
    depth = w_in.shape[2]
    part = rows // hids
    owned = steps * part
    wide = min(256, depth)

    def kernel(place_ref, *refs):
        hidden, w, own, squares = refs[:steps], refs[steps], refs[steps + 1], refs[steps + 2]
        sends, sums, totals = refs[steps + 3 : -2], refs[-2], refs[-1]
        n, step, j = pl.program_id(0), place_ref[0], place_ref[1]
        for m in range(steps):
            sums[m] = jnp.dot(hidden[m][...], w[0], preferred_element_type=F32)
        columns = pl.ds(pl.multiple_of(n * wide, wide), wide)
        for shift in range(hids):
            out = own if shift == 0 else sends[shift - 1]
            start = pl.multiple_of(lax.rem(j + shift, hids) * part, part)
            for m in range(steps):
                to = pl.multiple_of(lax.rem(step + m, steps) * part, part)
                out[pl.ds(to, part), columns] = sums[m, pl.ds(start, part), :].astype(out.dtype)

        @pl.when(n == 0)
        def _():
            for m in range(steps):
                values = hidden[m][...].astype(F32)
                totals[m] = jnp.sum(values * values, axis=1, keepdims=True)
            for shift in range(hids):
                start = pl.multiple_of(lax.rem(j + shift, hids) * part, part)
                for m in range(steps):
                    to = pl.multiple_of(lax.rem(step + m, steps) * part, part)
                    total = totals[m, pl.ds(start, part), :]
                    if shift == 0:
                        squares[pl.ds(to, part), :] = total
                    else:
                        sends[shift - 1][pl.ds(to, part), depth:] = parts_of([total], 1)

    return call(
        kernel,
        place,
        depth // wide,
        [whole((rows, units))] * steps
        + [pl.BlockSpec((1, units, wide), lambda n, place: (place[0], 0, n))],
        [whole((owned, depth)), whole((owned, 1))] + [whole((owned, depth + EXTRA))] * (hids - 1),
        [
            jax.ShapeDtypeStruct((owned, depth), F32),
            jax.ShapeDtypeStruct((owned, 1), F32),
        ]
        + [jax.ShapeDtypeStruct((owned, depth + EXTRA), BF16)] * (hids - 1),
        [pltpu.VMEM((steps, rows, wide), F32), pltpu.VMEM((steps, rows, 1), F32)],
        2 * steps * rows * units * depth,
        (*group, w_in),
    )


def row_gradient(place, d_norm, received, x_rows, proj, scale, ratio, gain, width_in):
    owned, depth = x_rows.shape

    def kernel(place_ref, *refs):
        d_norm, received = refs[0], refs[1 : 1 + len_received]
        x_ref, proj_ref, scale_ref, ratio_ref, gain_ref, out = refs[1 + len_received :]
        gated = d_norm[...]
        for r in received:
            gated = gated + r[...].astype(F32)
        gated = gated * gain_ref[...]
        x, scale, ratio = x_ref[...], scale_ref[...], ratio_ref[...]
        mean = jnp.sum(gated * x, axis=1, keepdims=True) * (1.0 / depth)
        d_x = scale * gated - x * (scale * scale * scale * mean)
        out[:, :depth] = d_x.astype(BF16)
        d_ratio = jnp.sum(d_x * proj_ref[...], axis=1, keepdims=True)
        correction = ratio * ratio * ratio * d_ratio * (1.0 / width_in)
        out[:, depth:] = parts_of([ratio, correction], 2)

    len_received = len(received)
    args = (d_norm, *received, x_rows, proj, scale, ratio, gain)
    return call(
        kernel,
        place,
        1,
        [whole((owned, depth))] + [whole(a.shape) for a in args[1:]],
        whole((owned, depth + EXTRA)),
        jax.ShapeDtypeStruct((owned, depth + EXTRA), BF16),
        [],
        10 * owned * depth,
        args,
    )


def spread(place, pieces, seqs, steps):
    hids = len(pieces)
    owned, full = pieces[0].shape
    depth = full - EXTRA
    part = owned // steps
    rows = part * hids
    wide = depth // seqs

    def kernel(place_ref, *refs):
        pieces, scaled, plain = refs[:hids], refs[hids], refs[hids + 1 :]
        step, j = place_ref[0], place_ref[1]
        for shift in range(hids):
            owner = lax.rem(j - shift + hids, hids)
            ratio = column_of(pieces[shift][:, depth:], 0)
            values = (pieces[shift][:, :depth].astype(F32) * ratio).astype(BF16)
            for m in range(steps):
                at = pl.multiple_of(m * rows + owner * part, part)
                for q in range(seqs):
                    scaled[q, pl.ds(at, part), :] = values[
                        m * part : (m + 1) * part, q * wide : (q + 1) * wide
                    ]
            to = pl.multiple_of(owner * part, part)
            for m in range(steps):
                start = pl.multiple_of(lax.rem(step + m, steps) * part, part)
                plain[m][pl.ds(to, part), :] = pieces[shift][pl.ds(start, part), :]

    return call(
        kernel,
        place,
        1,
        [whole((owned, full))] * hids,
        [whole((seqs, steps * rows, wide))] + [whole((rows, full))] * steps,
        [jax.ShapeDtypeStruct((seqs, steps * rows, wide), BF16)]
        + [jax.ShapeDtypeStruct((rows, full), BF16)] * steps,
        [],
        steps * rows * depth,
        tuple(pieces),
    )


def sum_groups(place, received, steps, hids):
    seqs, rows, entries = received.shape
    groups = seqs // steps
    part = rows // hids

    def kernel(place_ref, received, *outs):
        for shift in range(hids):
            start = pl.multiple_of(lax.rem(place_ref[1] + shift, hids) * part, part)
            for s in range(steps):
                total = received[s, pl.ds(start, part), :].astype(F32)
                for g in range(1, groups):
                    total = total + received[g * steps + s, pl.ds(start, part), :].astype(F32)
                outs[shift][s] = total.astype(BF16)

    return call(
        kernel,
        place,
        1,
        [whole(received.shape)],
        [whole((steps, part, entries))] * hids,
        [jax.ShapeDtypeStruct((steps, part, entries), BF16)] * hids,
        [],
        seqs * rows * entries,
        (received,),
    )


def head_gradient(place, pieces, halves):
    hids = len(pieces)
    steps, rows, block = pieces[0].shape

    def kernel(place_ref, *refs):
        pieces, out = refs[:-1], refs[-1]
        for r in range(halves):
            which = lax.rem(place_ref[1] - r + hids, halves)
            columns = pl.ds(pl.multiple_of(which * block, block), block)
            for s in range(steps):
                total = pieces[r][s].astype(F32)
                for k in range(r + halves, hids, halves):
                    total = total + pieces[k][s].astype(F32)
                out[:, s, columns] = total

    return call(
        kernel,
        place,
        1,
        [whole((steps, rows, block))] * hids,
        whole((rows, steps, halves * block)),
        jax.ShapeDtypeStruct((rows, steps, halves * block), F32),
        [],
        hids * steps * rows * block,
        tuple(pieces),
    )


def input_gradient(place, blocks, scaled, steps):
    groups = len(blocks)
    units, rows = blocks[0][0].shape
    wide = scaled.shape[2]
    tall = min(256, units)

    def kernel(place_ref, *refs):
        hidden, scaled, out = refs[:-2], refs[-2], refs[-1]
        step, group = place_ref[0], place_ref[2]
        total = None
        for r in range(groups):
            source = lax.rem(group - r + groups, groups)
            for m in range(steps):
                at = pl.multiple_of(lax.rem(step - m + steps, steps) * rows, rows)
                right = jnp.concatenate(
                    [scaled[source * steps + s, pl.ds(at, rows), :] for s in range(steps)], axis=1
                )
                term = jnp.dot(hidden[r * steps + m][...], right, preferred_element_type=F32)
                total = term if total is None else total + term
        for s in range(steps):
            out[s] = total[:, s * wide : (s + 1) * wide]

    flat = [b for line in blocks for b in line]
    return call(
        kernel,
        place,
        units // tall,
        [pl.BlockSpec((tall, rows), lambda n, place: (n, 0))] * len(flat) + [whole(scaled.shape)],
        pl.BlockSpec((steps, tall, wide), lambda n, place: (0, n, 0)),
        jax.ShapeDtypeStruct((steps, units, wide), F32),
        [],
        2 * units * rows * len(flat) * wide * steps,
        (*flat, scaled),
    )


def hidden_gradient(place, d_rows, w_in, hidden):
    steps, units, depth = w_in.shape
    rows = hidden.shape[0]
    wide = min(256, units)

    def kernel(place_ref, *refs):
        d_rows, w, hidden, out = refs[:steps], refs[-3], refs[-2], refs[-1]
        total, correction = None, None
        for r in range(steps):
            which = lax.rem(place_ref[0] - r + steps, steps)
            term = lax.dot_general(
                d_rows[r][:, :depth], w[which], (((1,), (1,)), ((), ())), preferred_element_type=F32
            )
            share = column_of(d_rows[r][:, depth:], 1)
            total = term if total is None else total + term
            correction = share if correction is None else correction + share
        ratio = column_of(d_rows[0][:, depth:], 0)
        out[...] = (ratio * total - correction * hidden[...].astype(F32)).astype(BF16)

    return call(
        kernel,
        place,
        units // wide,
        [whole((rows, depth + EXTRA))] * steps
        + [
            pl.BlockSpec((steps, wide, depth), lambda n, place: (0, n, 0)),
            pl.BlockSpec((rows, wide), lambda n, place: (0, n)),
        ],
        pl.BlockSpec((rows, wide), lambda n, place: (0, n)),
        jax.ShapeDtypeStruct((rows, units), BF16),
        [],
        2 * steps * rows * units * depth,
        (*d_rows, w_in, hidden),
    )


def shards(hidden, w_in, embedding, depth_gain, w_out, codebook_ids):
    hids = lax.axis_size("hid")
    seqs = lax.axis_size("seq")
    steps, units, depth = w_in.shape
    entries = w_out.shape[2]
    rows = hidden.shape[0]
    part = rows // hids
    width_in = units * hids
    frames = rows * seqs
    halves = 2 if hids % 2 == 0 else 1
    block = entries // halves
    head_rows = w_out.shape[0]
    groups = seqs // steps
    i = lax.axis_index("seq")
    j = lax.axis_index("hid")
    step = i % steps
    half = j % halves
    owned = steps * part

    def along_hid(values, shift):
        return lax.ppermute(values, "hid", [(a, (a + shift) % hids) for a in range(hids)])

    def turn_hid(values, shift):
        return lax.ppermute(
            values,
            "hid",
            [(a, a - a % halves + (a % halves + shift) % halves) for a in range(hids)],
        )

    def flip_seq(values, flip):
        return lax.ppermute(
            values,
            "seq",
            [(a, a - a % steps + (a % steps + flip) % steps) for a in range(seqs)],
        )

    def gather_flips(values, position):
        out = jnp.broadcast_to(values, (steps,) + values.shape)
        for r in range(1, steps):
            out = lax.dynamic_update_index_in_dim(
                out, flip_seq(values, -r), (position + r) % steps, 0
            )
        return out

    place = jnp.stack([step, j, i // steps]).astype(jnp.int32)

    def along_groups(values, shift):
        return lax.ppermute(values, "seq", [(a, (a + shift * steps) % seqs) for a in range(seqs)])

    head_send = w_out.reshape(head_rows, steps, halves, block).transpose(2, 1, 0, 3)
    head_send = jnp.broadcast_to(head_send, (hids // halves,) + head_send.shape)
    head_send = head_send.reshape(hids, steps, head_rows, block)
    head_mid = lax.all_to_all(head_send, "hid", 0, 0).transpose(1, 0, 2, 3)

    ids = gather_flips(codebook_ids, step).transpose(1, 0, 2).reshape(steps, owned)
    ids_rows = [ids] + [turn_hid(ids, -k) for k in range(1, halves)]

    group = [hidden] + [flip_seq(hidden, -r) for r in range(1, steps)]
    proj, squares, *send = project(place, group, w_in, hids)
    for shift in range(1, hids):
        received = along_hid(send[shift - 1], shift)
        proj += received[:, :depth].astype(F32)
        squares += jnp.sum(received[:, depth : depth + 3].astype(F32), axis=1, keepdims=True)
    ratio = lax.rsqrt(squares / width_in + 1e-06)

    head_send = after(head_mid, *send).reshape(steps, hids * head_rows, block)
    head_send = jnp.broadcast_to(head_send, (groups,) + head_send.shape)
    head_send = head_send.reshape(seqs, hids * head_rows, block)
    head = lax.all_to_all(head_send, "seq", 0, 0).reshape(depth, block)

    before = jnp.maximum(step - 1, 0)
    table = pick(embedding, before)
    looked = jnp.take(table, pick(ids, before), axis=0).astype(F32)
    x_rows = ratio * proj + jnp.where(step > 0, looked, 0.0)
    scale = lax.rsqrt(jnp.mean(x_rows * x_rows, axis=1, keepdims=True) + 1e-06)
    gain = pick(depth_gain, step)[None, :]
    normed = (x_rows * scale * gain).astype(BF16)

    turned = [after(hidden.T, normed)]
    turned += [along_groups(turned[0], r) for r in range(1, groups)]
    turned = [[t] + [flip_seq(t, m) for m in range(1, steps)] for t in turned]

    normed_rows = jnp.concatenate([normed] + [turn_hid(normed, -k) for k in range(1, halves)])
    targets = jnp.concatenate([pick(r, step) for r in ids_rows])
    logits = matmul(normed_rows, head, ((1,), (0,)))
    top = jnp.max(logits, axis=1)
    total = jnp.sum(jnp.exp(logits - top[:, None]), axis=1)
    stats = jnp.stack([top, total]).reshape(2, halves, -1)
    every = [stats] + [jnp.roll(turn_hid(stats, -t), t, axis=1) for t in range(1, halves)]
    tops = jnp.stack([e[0] for e in every]).reshape(halves, -1)
    totals = jnp.stack([e[1] for e in every]).reshape(halves, -1)
    top_all = jnp.max(tops, axis=0)
    lse = top_all + jnp.log(jnp.sum(totals * jnp.exp(tops - top_all), axis=0))
    entry = lax.broadcasted_iota(jnp.int32, logits.shape, 1) + half * block
    onehot = (targets[:, None] == entry).astype(F32)
    loss_weight = 2.0 * entries / frames
    d_logit = ((jnp.exp(logits - lse[:, None]) - onehot) * loss_weight).astype(BF16)

    d_norm_rows = matmul(d_logit, head, ((1,), (1,)))
    received = [
        turn_hid(d_norm_rows[k * owned : (k + 1) * owned].astype(BF16), k) for k in range(1, halves)
    ]
    d_round = row_gradient(
        place, d_norm_rows, received, x_rows, proj, scale, ratio, gain, width_in
    )

    part_out = matmul(normed_rows, d_logit, ((0,), (0,))).astype(BF16)
    part_out = lax.all_to_all(part_out.reshape(seqs, depth // seqs, block), "seq", 0, 0)
    sums = sum_groups(place, part_out, steps, hids)
    sums = [along_hid(p, shift) if shift else p for shift, p in enumerate(sums)]
    grad_out = head_gradient(place, sums, halves)

    pieces = [d_round] + [along_hid(d_round, shift) for shift in range(1, hids)]
    scaled, mine, *others = spread(place, pieces, seqs, steps)
    scaled = lax.all_to_all(scaled, "seq", 0, 0)
    grad_in = input_gradient(place, turned, scaled, steps)
    mine = [mine] + [flip_seq(others[r - 1], r) for r in range(1, steps)]
    grad_hidden = hidden_gradient(place, mine, w_in, hidden)
    return (grad_hidden, grad_in, grad_out)


def solution(mesh):
    placed = (
        P("seq", "hid"),
        P(None, "hid", None),
        P(),
        P(),
        P(("seq", "hid"), None, None),
        P(None, ("seq", "hid")),
    )
    return jax.shard_map(
        shards,
        mesh=mesh,
        in_specs=placed,
        out_specs=(P("seq", "hid"), P(None, "hid", "seq"), P(("seq", "hid"), None, None)),
        check_vma=False,
    )
```

time: 190 us -> 164 us (0.86)
  waiting for transfers between devices: 82.1 us -> 43.1 us
  starting transfers between devices: 50.9 us -> 61.9 us
  other arithmetic: 9.7 us -> 3.86 us
  Pallas kernels: 15.8 us -> 19.9 us
  local copies, waits for them, and re-layouts: 23.7 us -> 26.3 us
    ppermute x15 -> x9, waiting for transfers between devices: 43.4 us -> 21 us  [along_hid(): lax.ppermute(values, 'hid', [(a, (a + shift) % hids) for a in range(hids)])]
    unnamed x29 -> x49, local copies, waits for them, and re-layouts: 6.1 us -> 16.8 us
    all_to_all x1, waiting for transfers between devices: 10 us -> 0.01 us  [shards(): head = lax.all_to_all(head_send, 'seq', 0, 0).reshape(depth, block)]
    ppermute x3, waiting for transfers between devices: 8.63 us -> 0.01 us  [along_groups(): lax.ppermute(values, 'seq', [(a, (a + shift * steps) % seqs) for a in ran...]
    all_to_all x1, waiting for transfers between devices: 0.01 us -> 4.95 us  [shards(): head_mid = lax.all_to_all(head_send, 'hid', 0, 0).transpose(1, 0, 2, 3)]
    reduce_sum x5 -> x3, other arithmetic: 5.85 us -> 1.07 us  [shards(): jnp.sum(received[:, depth:depth + 3].astype(F32), axis=1, keepdims=True)]
    ppermute x15 -> x9, starting transfers between devices: 26.2 us -> 30.7 us  [along_hid(): lax.ppermute(values, 'hid', [(a, (a + shift) % hids) for a in range(hids)])]
    pallas_call x4 -> x7, Pallas kernels: 15.8 us -> 19.9 us  [call(): pl.pallas_call(kernel, grid_spec=pltpu.PrefetchScalarGridSpec(num_scalar_...]
  transfers between devices with their start and end apart: 33 -> 27, of which waited for: 15 -> 9; matrix products, arithmetic and copies ran while one was open for 12% -> 8% of each run, Pallas kernels for 6% -> 11%
where the time goes in v1:
time: 164 us; the launch traced here: 163 us
  starting transfers between devices  61.9 us (38%)
  waiting for transfers between devices  43.1 us (26%)
  local copies, waits for them, and re-layouts  26.3 us (16%)
  Pallas kernels  19.9 us (12%)
  matrix products  7.52 us (5%)
  other arithmetic  3.86 us (2%)
    ppermute x9, starting transfers between devices, along_hid(): lax.ppermute(values, 'hid', [(a, (a + shift) % hids) for a in range(hids)])  30.7 us
    ppermute x9, waiting for transfers between devices, along_hid(): lax.ppermute(values, 'hid', [(a, (a + shift) % hids) for a in range(hids)])  21 us
    pallas_call x7, Pallas kernels, call(): pl.pallas_call(kernel, grid_spec=pltpu.PrefetchScalarGridSpec(num_scalar_...  19.9 us
    unnamed x49, local copies, waits for them, and re-layouts  16.8 us
    ppermute x4, waiting for transfers between devices, turn_hid(): lax.ppermute(values, 'hid', [(a, a - a % halves + (a % halves + shift) %...  15.2 us
    dot_general x3, matrix products, matmul(): lax.dot_general(a, b, (contract, ((), ())), preferred_element_type=F32)  7.52 us
    all_to_all x1, starting transfers between devices, shards(): head_mid = lax.all_to_all(head_send, 'hid', 0, 0).transpose(1, 0, 2, 3)  6.32 us
    ppermute x3, starting transfers between devices, along_groups(): lax.ppermute(values, 'seq', [(a, (a + shift * steps) % seqs) for a in ran...  5.83 us
  transfers between devices with their start and end apart: 27, of which 9 were waited for; matrix products, arithmetic and copies ran while one was open for 8% of the time, Pallas kernels for 11%

profile of v1, /device:TPU:0, one launch (start us, length us, event | category | flops | bytes accessed | tf_op | source)
XLA Modules:
  0.0 163.4 jit_solution(18187286488381521531)
XLA Ops:
  0.7 1.2 reshape.115
  2.8 6.3 %all-to-all-start = ((bf16[4,2,32,1024]{3,2,1,0:T(8,128)(2,1)}), bf16[4,2,32,1024]{3,2,1,0:T(8,128)(2,1)S(1)}, u32[]{:S(2)}, u32[]{:S(2)}) async-start(bf16[4,2,32,1024]{3,2,1,0:T(8,128)(2,1)} %bitcast.15), calls=%async_computation | async-start | bytes 1048576 | tf_op jit(solution)/shard_map/all_to_all | solution.py:375
  9.7 1.3 collective-permute-done.4
  11.1 4.6 %shard_map.85 = (f32[128,1024]{1,0:T(8,128)S(1)}, f32[128,1]{1,0:T(8,128)S(1)}, bf16[128,1152]{1,0:T(8,128)(2,1)S(1)}, bf16[128,1152]{1,0:T(8,128)(2,1)S(1)}, bf16[128,1152]{1,0:T(8,128)(2,1)S(1)}) custom-call(s32[3]{0:T(128)S(1)} %pad_add_fusion.1.place_ref, bf16[256,1024]{1,0:T(8,128)(2,1)S(1)} %copy-done.2, ...), custom_call_target="tpu_custom_call" | custom-call | flops 1073741824 | bytes 5242880 | tf_op jit(solution)/shard_map/pallas_call | solution.py:33
  15.8 3.9 %collective-permute-start.3 = (bf16[128,1152]{1,0:T(8,128)(2,1)S(1)}, bf16[128,1152]{1,0:T(8,128)(2,1)S(1)}, u32[]{:S(2)}, u32[]{:S(2)}) collective-permute-start(bf16[128,1152]{1,0:T(8,128)(2,1)S(1)} %get-tuple-element.20), channel_id=1, source_target_pairs={{0,3},{1,0},{2,1},{3,2},{4,7},{5,4},{6,5},{7,6},{8,11},{9,8},{10,9... | collective-permute-start | bytes 884744 | tf_op jit(solution)/shard_map/ppermute | solution.py:343
  19.7 5.0 %all-to-all-done = bf16[4,2,32,1024]{3,2,1,0:T(8,128)(2,1)S(1)} async-done(((bf16[4,2,32,1024]{3,2,1,0:T(8,128)(2,1)}), bf16[4,2,32,1024]{3,2,1,0:T(8,128)(2,1)S(1)}, u32[]{:S(2)}, u32[]{:S(2)}) %all-to-all-start) | async-done | bytes 524320 | tf_op jit(solution)/shard_map/all_to_all | solution.py:375
  24.7 1.6 broadcast_in_dim.51
  26.3 4.3 %all-to-all-start.1 = ((bf16[8,128,1024]{2,1,0:T(8,128)(2,1)}), bf16[8,128,1024]{2,1,0:T(8,128)(2,1)}, u32[]{:S(2)}, u32[]{:S(2)}) async-start(bf16[8,128,1024]{2,1,0:T(8,128)(2,1)} %bitcast.50), calls=%async_computation.1 | async-start | bytes 4194304 | tf_op jit(solution)/shard_map/all_to_all | solution.py:391
  30.7 3.8 %gather_fusion = bf16[128,1024]{1,0:T(8,128)(2,1)S(1)} fusion(bf16[2048,1024]{1,0:T(8,128)(2,1)} %bitcast.53, s32[1024]{0:T(1024)S(1)} %pad_clamp_fusion), kind=kCustom, calls=%fused_computation | custom fusion | bytes 524800 | tf_op jit(solution)/shard_map/jit(_take)/gather | solution.py:395
  34.5 11.9 %collective-permute-start.1 = (bf16[128,1152]{1,0:T(8,128)(2,1)S(1)}, bf16[128,1152]{1,0:T(8,128)(2,1)S(1)}, u32[]{:S(2)}, u32[]{:S(2)}) collective-permute-start(bf16[128,1152]{1,0:T(8,128)(2,1)S(1)} %get-tuple-element.18), channel_id=1, source_target_pairs={{0,1},{1,2},{2,3},{3,0},{4,5},{5,6},{6,7},{7,4},{8,9},{9,10},{10,1... | collective-permute-start | bytes 884744 | tf_op jit(solution)/shard_map/ppermute | solution.py:343
  47.6 9.0 %collective-permute-done.1 = bf16[128,1152]{1,0:T(8,128)(2,1)S(1)} collective-permute-done((bf16[128,1152]{1,0:T(8,128)(2,1)S(1)}, bf16[128,1152]{1,0:T(8,128)(2,1)S(1)}, u32[]{:S(2)}, u32[]{:S(2)}) %collective-permute-start.1) | collective-permute-done | bytes 294944 | tf_op jit(solution)/shard_map/ppermute | solution.py:343
  57.4 2.1 %multiply_reduce_fusion = (f32[128]{0:T(128)S(1)}, f32[128,1024]{1,0:T(8,128)S(1)}, f32[128,1024]{1,0:T(8,128)}) fusion(bf16[128,1024]{1,0:T(8,128)(2,1)S(1)} %gather_fusion, pred[128]{0:T(512)(128)(4,1)S(1)} %compare_and_fusion, pred[]{:T(512)S(6)} %gt.3, f32[128]{0:T(128)S(1)} %get-tuple-element.36, bf16[128,1152]{1,0:T(8,128)(2,1)S(1)} %collective-permute-done.3, ...), kind=kLoop, calls=%fused_computation.8 | loop fusion | flops 1703808 | bytes 2622593 | tf_op jit(solution)/shard_map/reduce_sum | solution.py:397
  59.7 2.0 %collective-permute-start.7 = (s32[2,128]{1,0:T(2,128)S(1)}, s32[2,128]{1,0:T(2,128)S(1)}, u32[]{:S(2)}, u32[]{:S(2)}) collective-permute-start(s32[2,128]{1,0:T(2,128)S(1)} %reshape.114), channel_id=1, source_target_pairs={{0,1},{1,0},{2,3},{3,2},{4,5},{5,4},{6,7},{7,6},{8,9},{9,8},{10,11... | collective-permute-start | bytes 3080 | tf_op jit(solution)/shard_map/ppermute | solution.py:346
  61.7 6.0 %collective-permute-done.7 = s32[2,128]{1,0:T(2,128)S(1)} collective-permute-done((s32[2,128]{1,0:T(2,128)S(1)}, s32[2,128]{1,0:T(2,128)S(1)}, u32[]{:S(2)}, u32[]{:S(2)}) %collective-permute-start.7) | collective-permute-done | bytes 1056 | tf_op jit(solution)/shard_map/ppermute | solution.py:346
  67.7 2.4 %fusion.14 = (f32[256]{0:T(256)S(1)}, f32[256,1024]{1,0:T(8,128)S(1)}) fusion(bf16[1024,1024]{1,0:T(8,128)(2,1)} %bitcast.19, bf16[128,1024]{1,0:T(8,128)(2,1)S(1)} %collective-permute-done.5, bf16[128,1024]{1,0:T(8,128)(2,1)S(1)} %multiply_convert_fusion.1), kind=kOutput, calls=%fused_computation.48 | convolution fusion | flops 538181376 | bytes 3671040 | tf_op jit(solution)/shard_map/dot_general | solution.py:17
  70.5 1.4 collective-permute-start.6
  71.9 2.2 %collective-permute-done.6 = f32[2,2,128]{2,1,0:T(2,128)S(1)} collective-permute-done((f32[2,2,128]{2,1,0:T(2,128)S(1)}, f32[2,2,128]{2,1,0:T(2,128)S(1)}, u32[]{:S(2)}, u32[]{:S(2)}) %collective-permute-start.6) | collective-permute-done | bytes 2080 | tf_op jit(solution)/shard_map/ppermute | solution.py:346
  74.2 2.4 %convolution_convert_fusion = bf16[1024,1024]{1,0:T(8,128)(2,1)} fusion(bf16[128,1024]{1,0:T(8,128)(2,1)S(1)} %collective-permute-done.5, bf16[128,1024]{1,0:T(8,128)(2,1)S(1)} %multiply_convert_fusion.1, f32[256,1024]{1,0:T(8,128)S(1)} %get-tuple-element.43, s32[1024]{0:T(1024)S(1)} %iota_add_fusion, f32[256]{0:T(256)S(1)} %log_add_fusion, ...), kind=kOutput, calls=%fused_computation.1 | convolution fusion | flops 540540928 | bytes 3676160 | tf_op jit(solution)/shard_map/dot_general | solution.py:17
  76.6 3.7 %all-to-all-start.3 = ((bf16[8,128,1024]{2,1,0:T(8,128)(2,1)}), bf16[8,128,1024]{2,1,0:T(8,128)(2,1)S(1)}, u32[]{:S(2)}, u32[]{:S(2)}) async-start(bf16[8,128,1024]{2,1,0:T(8,128)(2,1)} %bitcast.52), calls=%async_computation.3 | async-start | bytes 4194304 | tf_op jit(solution)/shard_map/all_to_all | solution.py:430
  80.3 2.8 %fusion.10.refs_0_ = f32[256,1024]{1,0:T(8,128)S(1)} fusion(bf16[1024,1024]{1,0:T(8,128)(2,1)} %bitcast.19, f32[256,1024]{1,0:T(8,128)} %copy-done.21, s32[1024]{0:T(1024)S(1)} %iota_add_fusion, f32[256]{0:T(256)S(1)} %log_add_fusion, s32[256]{0:T(256)S(1)} %pad_add_fusion), kind=kOutput, calls=%fused_computation.45 | convolution fusion | flops 538443776 | bytes 4200448 | tf_op jit(solution)/shard_map/dot_general | solution.py:17
  83.8 1.0 copy-done.4
  84.8 1.2 collective-permute-start.8
  86.7 6.9 %collective-permute-done.8.refs_1_ = bf16[128,1024]{1,0:T(8,128)(2,1)S(1)} collective-permute-done((bf16[128,1024]{1,0:T(8,128)(2,1)}, bf16[128,1024]{1,0:T(8,128)(2,1)S(1)}, u32[]{:S(2)}, u32[]{:S(2)}) %collective-permute-start.8) | collective-permute-done | bytes 262176 | tf_op jit(solution)/shard_map/ppermute | solution.py:346
  94.4 1.0 copy-done.3
  95.4 1.2 copy-done.5
  98.4 1.0 shard_map.86.refs_0_
  99.5 1.2 collective-permute-start.9
  100.7 3.3 %collective-permute-start.10 = (bf16[128,1152]{1,0:T(8,128)(2,1)S(1)}, bf16[128,1152]{1,0:T(8,128)(2,1)}, u32[]{:S(2)}, u32[]{:S(2)}) collective-permute-start(bf16[128,1152]{1,0:T(8,128)(2,1)S(1)} %shard_map.86.refs_0_), channel_id=1, source_target_pairs={{0,2},{1,3},{2,0},{3,1},{4,6},{5,7},{6,4},{7,5},{8,10},{9,11},{10,... | collective-permute-start | bytes 884744 | tf_op jit(solution)/shard_map/ppermute | solution.py:343
  104.0 1.2 collective-permute-start.11
  105.3 1.7 %collective-permute-start.14 = (bf16[1024,256]{1,0:T(8,128)(2,1)S(1)}, bf16[1024,256]{1,0:T(8,128)(2,1)}, u32[]{:S(2)}, u32[]{:S(2)}) collective-permute-start(bf16[1024,256]{1,0:T(8,128)(2,1)S(1)} %bitcast.44), channel_id=1, source_target_pairs={{0,8},{4,12},{8,16},{12,20},{16,24},{20,28},{24,0},{28,4},{1,9},{5... | collective-permute-start | bytes 1572872 | tf_op jit(solution)/shard_map/ppermute | solution.py:370
  107.1 1.5 collective-permute-start.16
  108.6 3.0 %collective-permute-done.9.refs_1_ = bf16[128,1152]{1,0:T(8,128)(2,1)} collective-permute-done((bf16[128,1152]{1,0:T(8,128)(2,1)S(1)}, bf16[128,1152]{1,0:T(8,128)(2,1)}, u32[]{:S(2)}, u32[]{:S(2)}) %collective-permute-start.9) | collective-permute-done | bytes 294944 | tf_op jit(solution)/shard_map/ppermute | solution.py:343
  111.5 2.6 %collective-permute-start.18 = (bf16[1024,256]{1,0:T(8,128)(2,1)S(1)}, bf16[1024,256]{1,0:T(8,128)(2,1)}, u32[]{:S(2)}, u32[]{:S(2)}) collective-permute-start(bf16[1024,256]{1,0:T(8,128)(2,1)S(1)} %bitcast.46), channel_id=1, source_target_pairs={{0,24},{4,28},{8,0},{12,4},{16,8},{20,12},{24,16},{28,20},{1,25},{... | collective-permute-start | bytes 1572872 | tf_op jit(solution)/shard_map/ppermute | solution.py:370
  114.1 9.0 %collective-permute-done.10.refs_2_ = bf16[128,1152]{1,0:T(8,128)(2,1)} collective-permute-done((bf16[128,1152]{1,0:T(8,128)(2,1)S(1)}, bf16[128,1152]{1,0:T(8,128)(2,1)}, u32[]{:S(2)}, u32[]{:S(2)}) %collective-permute-start.10) | collective-permute-done | bytes 294944 | tf_op jit(solution)/shard_map/ppermute | solution.py:343
  123.1 2.1 %shard_map.87 = (bf16[8,512,128]{2,1,0:T(8,128)(2,1)S(1)}, bf16[256,1152]{1,0:T(8,128)(2,1)S(1)}, bf16[256,1152]{1,0:T(8,128)(2,1)S(1)}) custom-call(s32[3]{0:T(128)S(1)} %pad_add_fusion.1.place_ref, bf16[128,1152]{1,0:T(8,128)(2,1)S(1)} %shard_map.86.refs_0_, bf16[128,1152]{1,0:T(8,128)(2,1)} %collective-permute-done.9.refs_1_, ...), custom_call_target="tpu_custom_call" | custom-call | flops 524288 | bytes 1179648 | tf_op jit(solution)/shard_map/pallas_call | solution.py:33
  125.3 1.0 copy-done.6
  127.9 4.2 %all-to-all-start.2 = ((bf16[8,512,128]{2,1,0:T(8,128)(2,1)}), bf16[8,512,128]{2,1,0:T(8,128)(2,1)}, u32[]{:S(2)}, u32[]{:S(2)}) async-start(bf16[8,512,128]{2,1,0:T(8,128)(2,1)} %copy-done.6), calls=%async_computation.2 | async-start | bytes 2097152 | tf_op jit(solution)/shard_map/all_to_all | solution.py:437
  133.6 1.4 shard_map.90
  135.7 6.8 %collective-permute-start.20 = (bf16[2,32,1024]{2,1,0:T(8,128)(2,1)}, bf16[2,32,1024]{2,1,0:T(8,128)(2,1)S(1)}, u32[]{:S(2)}, u32[]{:S(2)}) collective-permute-start(bf16[2,32,1024]{2,1,0:T(8,128)(2,1)} %get-tuple-element.28), channel_id=1, source_target_pairs={{0,1},{1,2},{2,3},{3,0},{4,5},{5,6},{6,7},{7,4},{8,9},{9,10},{10,1... | collective-permute-start | bytes 393224 | tf_op jit(solution)/shard_map/ppermute | solution.py:343
  143.3 1.6 collective-permute-start.21
  144.9 1.0 collective-permute-start.22
  145.9 2.2 %copy-done.1 = bf16[2,1024,1024]{2,1,0:T(8,128)(2,1)S(1)} copy-done((bf16[2,1024,1024]{2,1,0:T(8,128)(2,1)S(1)}, bf16[2,1024,1024]{2,1,0:T(8,128)(2,1)}, u32[]{:S(2)}) %copy-start.1) | copy-done | bytes 4194328
  148.1 3.6 %shard_map.88 = bf16[256,1024]{1,0:T(8,128)(2,1)} custom-call(s32[3]{0:T(128)S(1)} %pad_add_fusion.1.place_ref, bf16[256,1152]{1,0:T(8,128)(2,1)S(1)} %copy-done.8, bf16[256,1152]{1,0:T(8,128)(2,1)S(1)} %collective-permute-done.12.refs_1_, bf16[2,1024,1024]{2,1,0:T(8,128)(2,1)S(1)} %copy-done.1, bf16[256,1024]{1,0:T(8,128)(2,1)S(1)} %copy-done.2), custom_call_target="tpu_custom_call" | custom-call | flops 1073741824 | bytes 5898240 | tf_op jit(solution)/shard_map/pallas_call | solution.py:33
  153.4 1.0 copy-done.10
  154.4 1.0 copy-done.14
  155.4 1.0 copy-done.16
  156.5 5.5 %shard_map.89 = f32[2,1024,128]{2,1,0:T(8,128)} custom-call(s32[3]{0:T(128)S(1)} %pad_add_fusion.1.place_ref, bf16[1024,256]{1,0:T(8,128)(2,1)S(1)} %bitcast.48, bf16[1024,256]{1,0:T(8,128)(2,1)S(1)} %copy-done.10, bf16[1024,256]{1,0:T(8,128)(2,1)} %collective-permute-done.14.refs_2_, bf16[1024,256]{1,0:T(8,128)(2,1)S(1)} %copy-done.12, ...), custom_call_target="tpu_custom_call" | custom-call | flops 1073741824 | bytes 5242880 | tf_op jit(solution)/shard_map/pallas_call | solution.py:33
  162.0 1.5 shard_map.91
  (102 shorter events, 14.7 us)
Async XLA Ops:
  0.6 9.1 %copy-start = (f32[2,1024]{1,0:T(2,128)S(1)}, f32[2,1024]{1,0:T(2,128)}, u32[]{:S(2)}) copy-start(f32[2,1024]{1,0:T(2,128)} %param.9) | copy-start | bytes 24580
  0.6 8.5 %copy-start.2 = (bf16[256,1024]{1,0:T(8,128)(2,1)S(1)}, bf16[256,1024]{1,0:T(8,128)(2,1)}, u32[]{:S(2)}) copy-start(bf16[256,1024]{1,0:T(8,128)(2,1)} %refs_3_.1) | copy-start | bytes 1572868
  0.7 8.5 %copy-start.23 = (s32[2,64]{1,0:T(2,128)S(1)}, s32[2,64]{1,0:T(2,128)}, u32[]{:S(2)}) copy-start(s32[2,64]{1,0:T(2,128)} %param.11) | copy-start | bytes 1540
  2.8 21.9 %all-to-all-start = ((bf16[4,2,32,1024]{3,2,1,0:T(8,128)(2,1)}), bf16[4,2,32,1024]{3,2,1,0:T(8,128)(2,1)S(1)}, u32[]{:S(2)}, u32[]{:S(2)}) async-start(bf16[4,2,32,1024]{3,2,1,0:T(8,128)(2,1)} %bitcast.15), calls=%async_computation | async-start | bytes 1048576 | tf_op jit(solution)/shard_map/all_to_all | solution.py:375
  9.1 2.0 %collective-permute-start = (bf16[256,1024]{1,0:T(8,128)(2,1)S(1)}, bf16[256,1024]{1,0:T(8,128)(2,1)S(1)}, u32[]{:S(2)}, u32[]{:S(2)}) collective-permute-start(bf16[256,1024]{1,0:T(8,128)(2,1)S(1)} %copy-done.2), channel_id=1, source_target_pairs={{0,4},{4,0},{8,12},{12,8},{16,20},{20,16},{24,28},{28,24},{1,5},{5... | collective-permute-start | bytes 1572872 | tf_op jit(solution)/shard_map/ppermute | solution.py:353
  9.1 1.9 %collective-permute-start.4 = (s32[2,64]{1,0:T(2,128)S(1)}, s32[2,64]{1,0:T(2,128)S(1)}, u32[]{:S(2)}, u32[]{:S(2)}) collective-permute-start(s32[2,64]{1,0:T(2,128)S(1)} %copy-done.23), channel_id=1, source_target_pairs={{0,4},{4,0},{8,12},{12,8},{16,20},{20,16},{24,28},{28,24},{1,5},{5... | collective-permute-start | bytes 1544 | tf_op jit(solution)/shard_map/ppermute | solution.py:353
  15.8 30.5 %collective-permute-start.3 = (bf16[128,1152]{1,0:T(8,128)(2,1)S(1)}, bf16[128,1152]{1,0:T(8,128)(2,1)S(1)}, u32[]{:S(2)}, u32[]{:S(2)}) collective-permute-start(bf16[128,1152]{1,0:T(8,128)(2,1)S(1)} %get-tuple-element.20), channel_id=1, source_target_pairs={{0,3},{1,0},{2,1},{3,2},{4,7},{5,4},{6,5},{7,6},{8,11},{9,8},{10,9... | collective-permute-start | bytes 884744 | tf_op jit(solution)/shard_map/ppermute | solution.py:343
  19.7 26.9 %collective-permute-start.2 = (bf16[128,1152]{1,0:T(8,128)(2,1)S(1)}, bf16[128,1152]{1,0:T(8,128)(2,1)}, u32[]{:S(2)}, u32[]{:S(2)}) collective-permute-start(bf16[128,1152]{1,0:T(8,128)(2,1)S(1)} %get-tuple-element.19), channel_id=1, source_target_pairs={{0,2},{1,3},{2,0},{3,1},{4,6},{5,7},{6,4},{7,5},{8,10},{9,11},{10,... | collective-permute-start | bytes 884744 | tf_op jit(solution)/shard_map/ppermute | solution.py:343
  26.3 41.4 %all-to-all-start.1 = ((bf16[8,128,1024]{2,1,0:T(8,128)(2,1)}), bf16[8,128,1024]{2,1,0:T(8,128)(2,1)}, u32[]{:S(2)}, u32[]{:S(2)}) async-start(bf16[8,128,1024]{2,1,0:T(8,128)(2,1)} %bitcast.50), calls=%async_computation.1 | async-start | bytes 4194304 | tf_op jit(solution)/shard_map/all_to_all | solution.py:391
  34.5 22.1 %collective-permute-start.1 = (bf16[128,1152]{1,0:T(8,128)(2,1)S(1)}, bf16[128,1152]{1,0:T(8,128)(2,1)S(1)}, u32[]{:S(2)}, u32[]{:S(2)}) collective-permute-start(bf16[128,1152]{1,0:T(8,128)(2,1)S(1)} %get-tuple-element.18), channel_id=1, source_target_pairs={{0,1},{1,2},{2,3},{3,0},{4,5},{5,6},{6,7},{7,4},{8,9},{9,10},{10,1... | collective-permute-start | bytes 884744 | tf_op jit(solution)/shard_map/ppermute | solution.py:343
  59.6 8.1 %collective-permute-start.5 = (bf16[128,1024]{1,0:T(8,128)(2,1)S(1)}, bf16[128,1024]{1,0:T(8,128)(2,1)S(1)}, u32[]{:S(2)}, u32[]{:S(2)}) collective-permute-start(bf16[128,1024]{1,0:T(8,128)(2,1)S(1)} %multiply_convert_fusion.1), channel_id=1, source_target_pairs={{0,1},{1,0},{2,3},{3,2},{4,5},{5,4},{6,7},{7,6},{8,9},{9,8},{10,11... | collective-permute-start | bytes 786440 | tf_op jit(solution)/shard_map/ppermute | solution.py:346
  59.7 8.0 %collective-permute-start.7 = (s32[2,128]{1,0:T(2,128)S(1)}, s32[2,128]{1,0:T(2,128)S(1)}, u32[]{:S(2)}, u32[]{:S(2)}) collective-permute-start(s32[2,128]{1,0:T(2,128)S(1)} %reshape.114), channel_id=1, source_target_pairs={{0,1},{1,0},{2,3},{3,2},{4,5},{5,4},{6,7},{7,6},{8,9},{9,8},{10,11... | collective-permute-start | bytes 3080 | tf_op jit(solution)/shard_map/ppermute | solution.py:346
  70.1 6.4 %copy-start.21 = (f32[256,1024]{1,0:T(8,128)}, f32[256,1024]{1,0:T(8,128)S(1)}, u32[]{:S(2)}) copy-start(f32[256,1024]{1,0:T(8,128)S(1)} %get-tuple-element.43) | copy-start | bytes 3145732
  70.5 3.7 %collective-permute-start.6 = (f32[2,2,128]{2,1,0:T(2,128)S(1)}, f32[2,2,128]{2,1,0:T(2,128)S(1)}, u32[]{:S(2)}, u32[]{:S(2)}) collective-permute-start(f32[2,2,128]{2,1,0:T(2,128)S(1)} %pad_maximum_fusion.3), channel_id=1, source_target_pairs={{0,1},{1,0},{2,3},{3,2},{4,5},{5,4},{6,7},{7,6},{8,9},{9,8},{10,11... | collective-permute-start | bytes 6152 | tf_op jit(solution)/shard_map/ppermute | solution.py:346
  76.6 51.3 %all-to-all-start.3 = ((bf16[8,128,1024]{2,1,0:T(8,128)(2,1)}), bf16[8,128,1024]{2,1,0:T(8,128)(2,1)S(1)}, u32[]{:S(2)}, u32[]{:S(2)}) async-start(bf16[8,128,1024]{2,1,0:T(8,128)(2,1)} %bitcast.52), calls=%async_computation.3 | async-start | bytes 4194304 | tf_op jit(solution)/shard_map/all_to_all | solution.py:430
  83.8 1.0 copy-start.4
  84.8 8.9 %collective-permute-start.8 = (bf16[128,1024]{1,0:T(8,128)(2,1)}, bf16[128,1024]{1,0:T(8,128)(2,1)S(1)}, u32[]{:S(2)}, u32[]{:S(2)}) collective-permute-start(bf16[128,1024]{1,0:T(8,128)(2,1)} %slice.77), channel_id=1, source_target_pairs={{0,1},{1,0},{2,3},{3,2},{4,5},{5,4},{6,7},{7,6},{8,9},{9,8},{10,11... | collective-permute-start | bytes 786440 | tf_op jit(solution)/shard_map/ppermute | solution.py:346
  94.4 1.0 copy-start.3
  95.4 1.2 copy-start.5
  96.6 0.9 copy-start.18
  97.6 0.8 copy-start.19
  99.5 12.1 %collective-permute-start.9 = (bf16[128,1152]{1,0:T(8,128)(2,1)S(1)}, bf16[128,1152]{1,0:T(8,128)(2,1)}, u32[]{:S(2)}, u32[]{:S(2)}) collective-permute-start(bf16[128,1152]{1,0:T(8,128)(2,1)S(1)} %shard_map.86.refs_0_), channel_id=1, source_target_pairs={{0,1},{1,2},{2,3},{3,0},{4,5},{5,6},{6,7},{7,4},{8,9},{9,10},{10,1... | collective-permute-start | bytes 884744 | tf_op jit(solution)/shard_map/ppermute | solution.py:343
  100.7 22.4 %collective-permute-start.10 = (bf16[128,1152]{1,0:T(8,128)(2,1)S(1)}, bf16[128,1152]{1,0:T(8,128)(2,1)}, u32[]{:S(2)}, u32[]{:S(2)}) collective-permute-start(bf16[128,1152]{1,0:T(8,128)(2,1)S(1)} %shard_map.86.refs_0_), channel_id=1, source_target_pairs={{0,2},{1,3},{2,0},{3,1},{4,6},{5,7},{6,4},{7,5},{8,10},{9,11},{10,... | collective-permute-start | bytes 884744 | tf_op jit(solution)/shard_map/ppermute | solution.py:343
  104.0 19.1 %collective-permute-start.11 = (bf16[128,1152]{1,0:T(8,128)(2,1)S(1)}, bf16[128,1152]{1,0:T(8,128)(2,1)}, u32[]{:S(2)}, u32[]{:S(2)}) collective-permute-start(bf16[128,1152]{1,0:T(8,128)(2,1)S(1)} %shard_map.86.refs_0_), channel_id=1, source_target_pairs={{0,3},{1,0},{2,1},{3,2},{4,7},{5,4},{6,5},{7,6},{8,11},{9,8},{10,9... | collective-permute-start | bytes 884744 | tf_op jit(solution)/shard_map/ppermute | solution.py:343
  105.3 27.4 %collective-permute-start.14 = (bf16[1024,256]{1,0:T(8,128)(2,1)S(1)}, bf16[1024,256]{1,0:T(8,128)(2,1)}, u32[]{:S(2)}, u32[]{:S(2)}) collective-permute-start(bf16[1024,256]{1,0:T(8,128)(2,1)S(1)} %bitcast.44), channel_id=1, source_target_pairs={{0,8},{4,12},{8,16},{12,20},{16,24},{20,28},{24,0},{28,4},{1,9},{5... | collective-permute-start | bytes 1572872 | tf_op jit(solution)/shard_map/ppermute | solution.py:370
  107.1 26.0 %collective-permute-start.16 = (bf16[1024,256]{1,0:T(8,128)(2,1)S(1)}, bf16[1024,256]{1,0:T(8,128)(2,1)}, u32[]{:S(2)}, u32[]{:S(2)}) collective-permute-start(bf16[1024,256]{1,0:T(8,128)(2,1)S(1)} %bitcast.45), channel_id=1, source_target_pairs={{0,16},{4,20},{8,24},{12,28},{16,0},{20,4},{24,8},{28,12},{1,17},{... | collective-permute-start | bytes 1572872 | tf_op jit(solution)/shard_map/ppermute | solution.py:370
  111.5 21.7 %collective-permute-start.18 = (bf16[1024,256]{1,0:T(8,128)(2,1)S(1)}, bf16[1024,256]{1,0:T(8,128)(2,1)}, u32[]{:S(2)}, u32[]{:S(2)}) collective-permute-start(bf16[1024,256]{1,0:T(8,128)(2,1)S(1)} %bitcast.46), channel_id=1, source_target_pairs={{0,24},{4,28},{8,0},{12,4},{16,8},{20,12},{24,16},{28,20},{1,25},{... | collective-permute-start | bytes 1572872 | tf_op jit(solution)/shard_map/ppermute | solution.py:370
  125.3 1.0 copy-start.6
  126.2 0.8 copy-start.7
  127.1 0.8 copy-start.20
  127.9 25.5 %all-to-all-start.2 = ((bf16[8,512,128]{2,1,0:T(8,128)(2,1)}), bf16[8,512,128]{2,1,0:T(8,128)(2,1)}, u32[]{:S(2)}, u32[]{:S(2)}) async-start(bf16[8,512,128]{2,1,0:T(8,128)(2,1)} %copy-done.6), calls=%async_computation.2 | async-start | bytes 2097152 | tf_op jit(solution)/shard_map/all_to_all | solution.py:437
  132.2 13.7 %copy-start.8 = (bf16[256,1152]{1,0:T(8,128)(2,1)S(1)}, bf16[256,1152]{1,0:T(8,128)(2,1)}, u32[]{:S(2)}) copy-start(bf16[256,1152]{1,0:T(8,128)(2,1)} %copy-done.7) | copy-start | bytes 1769476
  132.2 12.7 %collective-permute-start.12 = (bf16[256,1152]{1,0:T(8,128)(2,1)}, bf16[256,1152]{1,0:T(8,128)(2,1)S(1)}, u32[]{:S(2)}, u32[]{:S(2)}) collective-permute-start(bf16[256,1152]{1,0:T(8,128)(2,1)} %copy-done.20), channel_id=1, source_target_pairs={{0,4},{4,0},{8,12},{12,8},{16,20},{20,16},{24,28},{28,24},{1,5},{5... | collective-permute-start | bytes 1769480 | tf_op jit(solution)/shard_map/ppermute | solution.py:353
  132.5 3.2 %collective-permute-start.13 = (bf16[1024,256]{1,0:T(8,128)(2,1)S(1)}, bf16[1024,256]{1,0:T(8,128)(2,1)S(1)}, u32[]{:S(2)}, u32[]{:S(2)}) collective-permute-start(bf16[1024,256]{1,0:T(8,128)(2,1)S(1)} %bitcast.47), channel_id=1, source_target_pairs={{0,4},{4,0},{8,12},{12,8},{16,20},{20,16},{24,28},{28,24},{1,5},{5... | collective-permute-start | bytes 1572872 | tf_op jit(solution)/shard_map/ppermute | solution.py:353
  132.7 9.8 %collective-permute-start.15 = (bf16[1024,256]{1,0:T(8,128)(2,1)}, bf16[1024,256]{1,0:T(8,128)(2,1)S(1)}, u32[]{:S(2)}, u32[]{:S(2)}) collective-permute-start(bf16[1024,256]{1,0:T(8,128)(2,1)} %collective-permute-done.14.refs_2_), channel_id=1, source_target_pairs={{0,4},{4,0},{8,12},{12,8},{16,20},{20,16},{24,28},{28,24},{1,5},{5... | collective-permute-start | bytes 1572872 | tf_op jit(solution)/shard_map/ppermute | solution.py:353
  133.0 18.7 %collective-permute-start.17 = (bf16[1024,256]{1,0:T(8,128)(2,1)}, bf16[1024,256]{1,0:T(8,128)(2,1)S(1)}, u32[]{:S(2)}, u32[]{:S(2)}) collective-permute-start(bf16[1024,256]{1,0:T(8,128)(2,1)} %collective-permute-done.16.refs_4_), channel_id=1, source_target_pairs={{0,4},{4,0},{8,12},{12,8},{16,20},{20,16},{24,28},{28,24},{1,5},{5... | collective-permute-start | bytes 1572872 | tf_op jit(solution)/shard_map/ppermute | solution.py:353
  133.3 19.3 %collective-permute-start.19 = (bf16[1024,256]{1,0:T(8,128)(2,1)}, bf16[1024,256]{1,0:T(8,128)(2,1)S(1)}, u32[]{:S(2)}, u32[]{:S(2)}) collective-permute-start(bf16[1024,256]{1,0:T(8,128)(2,1)} %collective-permute-done.18.refs_6_), channel_id=1, source_target_pairs={{0,4},{4,0},{8,12},{12,8},{16,20},{20,16},{24,28},{28,24},{1,5},{5... | collective-permute-start | bytes 1572872 | tf_op jit(solution)/shard_map/ppermute | solution.py:353
  135.7 16.0 %copy-start.9 = (bf16[1024,256]{1,0:T(8,128)(2,1)}, bf16[1024,256]{1,0:T(8,128)(2,1)S(1)}, u32[]{:S(2)}) copy-start(bf16[1024,256]{1,0:T(8,128)(2,1)S(1)} %collective-permute-done.13.refs_1_) | copy-start | bytes 1572868
  135.7 26.2 %collective-permute-start.20 = (bf16[2,32,1024]{2,1,0:T(8,128)(2,1)}, bf16[2,32,1024]{2,1,0:T(8,128)(2,1)S(1)}, u32[]{:S(2)}, u32[]{:S(2)}) collective-permute-start(bf16[2,32,1024]{2,1,0:T(8,128)(2,1)} %get-tuple-element.28), channel_id=1, source_target_pairs={{0,1},{1,2},{2,3},{3,0},{4,5},{5,6},{6,7},{7,4},{8,9},{9,10},{10,1... | collective-permute-start | bytes 393224 | tf_op jit(solution)/shard_map/ppermute | solution.py:343
  143.3 18.6 %collective-permute-start.21 = (bf16[2,32,1024]{2,1,0:T(8,128)(2,1)}, bf16[2,32,1024]{2,1,0:T(8,128)(2,1)S(1)}, u32[]{:S(2)}, u32[]{:S(2)}) collective-permute-start(bf16[2,32,1024]{2,1,0:T(8,128)(2,1)} %get-tuple-element.29), channel_id=1, source_target_pairs={{0,2},{1,3},{2,0},{3,1},{4,6},{5,7},{6,4},{7,5},{8,10},{9,11},{10,... | collective-permute-start | bytes 393224 | tf_op jit(solution)/shard_map/ppermute | solution.py:343
  144.9 17.1 %collective-permute-start.22 = (bf16[2,32,1024]{2,1,0:T(8,128)(2,1)S(1)}, bf16[2,32,1024]{2,1,0:T(8,128)(2,1)S(1)}, u32[]{:S(2)}, u32[]{:S(2)}) collective-permute-start(bf16[2,32,1024]{2,1,0:T(8,128)(2,1)S(1)} %get-tuple-element.30), channel_id=1, source_target_pairs={{0,3},{1,0},{2,1},{3,2},{4,7},{5,4},{6,5},{7,6},{8,11},{9,8},{10,9... | collective-permute-start | bytes 393224 | tf_op jit(solution)/shard_map/ppermute | solution.py:343
  145.9 2.2 %copy-start.1 = (bf16[2,1024,1024]{2,1,0:T(8,128)(2,1)S(1)}, bf16[2,1024,1024]{2,1,0:T(8,128)(2,1)}, u32[]{:S(2)}) copy-start(bf16[2,1024,1024]{2,1,0:T(8,128)(2,1)} %refs_2_.3) | copy-start | bytes 12582916
  148.1 5.3 %copy-start.12 = (bf16[1024,256]{1,0:T(8,128)(2,1)S(1)}, bf16[1024,256]{1,0:T(8,128)(2,1)}, u32[]{:S(2)}) copy-start(bf16[1024,256]{1,0:T(8,128)(2,1)} %copy-done.11) | copy-start | bytes 1572868
  151.7 0.8 copy-start.13
  152.6 0.8 copy-start.15
  153.4 1.0 copy-start.10
  154.4 1.0 copy-start.14
  155.4 1.0 copy-start.16
  (3 other events, 2.2 us)

commit v2 on v1

--- a/solution.py
+++ b/solution.py
@@ -21,7 +21,7 @@
     return lax.optimization_barrier((value, *others))[0]
 
 
-VMEM = pltpu.CompilerParams(vmem_limit_bytes=48 * 2**20)
+VMEM = pltpu.CompilerParams(vmem_limit_bytes=60 * 2**20)
 
 
 def whole(shape):
@@ -77,8 +77,8 @@
         hidden, w, own, squares = refs[:steps], refs[steps], refs[steps + 1], refs[steps + 2]
         sends, sums, totals = refs[steps + 3 : -2], refs[-2], refs[-1]
         n, step, j = pl.program_id(0), place_ref[0], place_ref[1]
-        for m in range(steps):
-            sums[m] = jnp.dot(hidden[m][...], w[0], preferred_element_type=F32)
+        left = jnp.concatenate([h[...] for h in hidden], axis=0)
+        sums[...] = jnp.dot(left, w[0], preferred_element_type=F32).reshape(steps, rows, wide)
         columns = pl.ds(pl.multiple_of(n * wide, wide), wide)
         for shift in range(hids):
             out = own if shift == 0 else sends[shift - 1]
@@ -117,6 +117,42 @@
         [pltpu.VMEM((steps, rows, wide), F32), pltpu.VMEM((steps, rows, 1), F32)],
         2 * steps * rows * units * depth,
         (*group, w_in),
+    )
+
+
+def normalise(place, proj, squares, received, looked, gain, width_in):
+    owned, depth = proj.shape
+    count = len(received)
+
+    def kernel(place_ref, *refs):
+        proj, squares, looked, gain = refs[0], refs[1], refs[2 + count], refs[3 + count]
+        proj_out, x_out, normed_out, scale_out, ratio_out = refs[4 + count :]
+        total, square = proj[...], squares[...]
+        for r in refs[2 : 2 + count]:
+            total = total + r[:, :depth].astype(F32)
+            square = square + column_of(r[:, depth:], 0)
+        ratio = lax.rsqrt(square * (1.0 / width_in) + 1e-06)
+        x = ratio * total + jnp.where(place_ref[0] > 0, looked[...].astype(F32), 0.0)
+        scale = lax.rsqrt(jnp.sum(x * x, axis=1, keepdims=True) * (1.0 / depth) + 1e-06)
+        proj_out[...] = total
+        x_out[...] = x
+        normed_out[...] = (x * scale * gain[...]).astype(BF16)
+        scale_out[...] = scale
+        ratio_out[...] = ratio
+
+    args = (proj, squares, *received, looked, gain)
+    full, column = (owned, depth), (owned, 1)
+    shapes = [(full, F32), (full, F32), (full, BF16), (column, F32), (column, F32)]
+    return call(
+        kernel,
+        place,
+        1,
+        [whole(a.shape) for a in args],
+        [whole(shape) for shape, _ in shapes],
+        [jax.ShapeDtypeStruct(shape, dtype) for shape, dtype in shapes],
+        [],
+        10 * owned * depth,
+        args,
     )
 
 
@@ -252,7 +288,7 @@
     groups = len(blocks)
     units, rows = blocks[0][0].shape
     wide = scaled.shape[2]
-    tall = min(256, units)
+    tall = min(512, units)
 
     def kernel(place_ref, *refs):
         hidden, scaled, out = refs[:-2], refs[-2], refs[-1]
@@ -379,11 +415,7 @@
 
     group = [hidden] + [flip_seq(hidden, -r) for r in range(1, steps)]
     proj, squares, *send = project(place, group, w_in, hids)
-    for shift in range(1, hids):
-        received = along_hid(send[shift - 1], shift)
-        proj += received[:, :depth].astype(F32)
-        squares += jnp.sum(received[:, depth : depth + 3].astype(F32), axis=1, keepdims=True)
-    ratio = lax.rsqrt(squares / width_in + 1e-06)
+    received = [along_hid(send[shift - 1], shift) for shift in range(1, hids)]
 
     head_send = after(head_mid, *send).reshape(steps, hids * head_rows, block)
     head_send = jnp.broadcast_to(head_send, (groups,) + head_send.shape)
@@ -392,11 +424,11 @@
 
     before = jnp.maximum(step - 1, 0)
     table = pick(embedding, before)
-    looked = jnp.take(table, pick(ids, before), axis=0).astype(F32)
-    x_rows = ratio * proj + jnp.where(step > 0, looked, 0.0)
-    scale = lax.rsqrt(jnp.mean(x_rows * x_rows, axis=1, keepdims=True) + 1e-06)
+    looked = jnp.take(table, pick(ids, before), axis=0)
     gain = pick(depth_gain, step)[None, :]
-    normed = (x_rows * scale * gain).astype(BF16)
+    proj, x_rows, normed, scale, ratio = normalise(
+        place, proj, squares, received, looked, gain, width_in
+    )
 
     turned = [after(hidden.T, normed)]
     turned += [along_groups(turned[0], r) for r in range(1, groups)]
@@ -419,14 +451,13 @@
     d_logit = ((jnp.exp(logits - lse[:, None]) - onehot) * loss_weight).astype(BF16)
 
     d_norm_rows = matmul(d_logit, head, ((1,), (1,)))
-    received = [
-        turn_hid(d_norm_rows[k * owned : (k + 1) * owned].astype(BF16), k) for k in range(1, halves)
-    ]
+    away = [d_norm_rows[k * owned : (k + 1) * owned].astype(BF16) for k in range(1, halves)]
+    received = [turn_hid(a, k + 1) for k, a in enumerate(away)]
     d_round = row_gradient(
         place, d_norm_rows, received, x_rows, proj, scale, ratio, gain, width_in
     )
 
-    part_out = matmul(normed_rows, d_logit, ((0,), (0,))).astype(BF16)
+    part_out = matmul(normed_rows, after(d_logit, *away), ((0,), (0,))).astype(BF16)
     part_out = lax.all_to_all(part_out.reshape(seqs, depth // seqs, block), "seq", 0, 0)
     sums = sum_groups(place, part_out, steps, hids)
     sums = [along_hid(p, shift) if shift else p for shift, p in enumerate(sums)]

time: 164 us -> 163 us (level)
  Pallas kernels: 19.9 us -> 33.7 us
  local copies, waits for them, and re-layouts: 26.3 us -> 16.7 us
  starting transfers between devices: 61.9 us -> 54.7 us
  waiting for transfers between devices: 43.1 us -> 50.2 us
  matrix products: 7.52 us -> 3.63 us
  other arithmetic: 3.86 us -> 2.15 us
    ppermute x9, starting transfers between devices: 30.7 us -> 14.3 us  [along_hid(): lax.ppermute(values, 'hid', [(a, (a + shift) % hids) for a in range(hids)])]
    pallas_call x7 -> x8, Pallas kernels: 19.9 us -> 33.7 us  [call(): pl.pallas_call(kernel, grid_spec=pltpu.PrefetchScalarGridSpec(num_scalar_...]
    unnamed x49 -> x48, local copies, waits for them, and re-layouts: 16.8 us -> 7.7 us
    ppermute x9, waiting for transfers between devices: 21 us -> 28.6 us  [along_hid(): lax.ppermute(values, 'hid', [(a, (a + shift) % hids) for a in range(hids)])]
    ppermute x4, starting transfers between devices: 4.75 us -> 10.3 us  [turn_hid(): lax.ppermute(values, 'hid', [(a, a - a % halves + (a % halves + shift) %...]
    ppermute x3, starting transfers between devices: 5.83 us -> 10.4 us  [along_groups(): lax.ppermute(values, 'seq', [(a, (a + shift * steps) % seqs) for a in ran...]
    dot_general x3, matrix products: 7.52 us -> 3.63 us  [matmul(): lax.dot_general(a, b, (contract, ((), ())), preferred_element_type=F32)]
    reduce_sum x4 -> x0, other arithmetic: 3.14 us -> none  [the longest x1 2.07 us: shards(): scale = lax.rsqrt(jnp.mean(x_rows * x_rows, axis=1, keepdims=True) + 1e-06)]
  transfers between devices with their start and end apart: 27 -> 27, of which waited for: 9 -> 10; matrix products, arithmetic and copies ran while one was open for 8% -> 5% of each run, Pallas kernels for 11% -> 19%
where the time goes in v2:
time: 163 us; the launch traced here: 162 us
  starting transfers between devices  54.7 us (34%)
  waiting for transfers between devices  50.2 us (31%)
  Pallas kernels  33.7 us (21%)
  local copies, waits for them, and re-layouts  16.7 us (10%)
  matrix products  3.63 us (2%)
  other arithmetic  2.15 us (1%)
    pallas_call x8, Pallas kernels, call(): pl.pallas_call(kernel, grid_spec=pltpu.PrefetchScalarGridSpec(num_scalar_...  33.7 us
    ppermute x9, waiting for transfers between devices, along_hid(): lax.ppermute(values, 'hid', [(a, (a + shift) % hids) for a in range(hids)])  28.6 us
    ppermute x9, starting transfers between devices, along_hid(): lax.ppermute(values, 'hid', [(a, (a + shift) % hids) for a in range(hids)])  14.3 us
    ppermute x4, waiting for transfers between devices, turn_hid(): lax.ppermute(values, 'hid', [(a, a - a % halves + (a % halves + shift) %...  13.8 us
    ppermute x3, starting transfers between devices, along_groups(): lax.ppermute(values, 'seq', [(a, (a + shift * steps) % seqs) for a in ran...  10.4 us
    ppermute x4, starting transfers between devices, turn_hid(): lax.ppermute(values, 'hid', [(a, a - a % halves + (a % halves + shift) %...  10.3 us
    unnamed x48, local copies, waits for them, and re-layouts  7.7 us
    all_to_all x1, starting transfers between devices, shards(): head_mid = lax.all_to_all(head_send, 'hid', 0, 0).transpose(1, 0, 2, 3)  6.32 us
  transfers between devices with their start and end apart: 27, of which 10 were waited for; matrix products, arithmetic and copies ran while one was open for 5% of the time, Pallas kernels for 19%

profile of v2, /device:TPU:0, one launch (start us, length us, event | category | flops | bytes accessed | tf_op | source)
XLA Modules:
  0.0 162.1 jit_solution(7241406895254401678)
XLA Ops:
  0.7 1.2 reshape.94
  1.9 0.9 broadcast_in_dim.32
  2.8 6.3 %all-to-all-start = ((bf16[4,2,32,1024]{3,2,1,0:T(8,128)(2,1)}), bf16[4,2,32,1024]{3,2,1,0:T(8,128)(2,1)S(1)}, u32[]{:S(2)}, u32[]{:S(2)}) async-start(bf16[4,2,32,1024]{3,2,1,0:T(8,128)(2,1)} %bitcast.11), calls=%async_computation | async-start | bytes 1048576 | tf_op jit(solution)/shard_map/all_to_all | solution.py:411
  9.7 1.3 collective-permute-done.refs_1_
  11.0 0.8 copy-done.9
  11.8 6.2 %shard_map.85 = (f32[128,1024]{1,0:T(8,128)}, f32[128,1]{1,0:T(8,128)}, bf16[128,1152]{1,0:T(8,128)(2,1)}, bf16[128,1152]{1,0:T(8,128)(2,1)}, bf16[128,1152]{1,0:T(8,128)(2,1)}) custom-call(s32[3]{0:T(128)} %pad_add_fusion.1.place_ref, bf16[256,1024]{1,0:T(8,128)(2,1)} %refs_3_.1, bf16[256,1024]{1,0:T(8,128)(2,1)} %copy-done.9, bf16[2,1024,1024]{2,1,0:T(8,128)(2,1)} %refs_2_.3), custom_call_target="tpu_custom_call" | custom-call | flops 1073741824 | bytes 5242880 | tf_op jit(solution)/shard_map/pallas_call | solution.py:33
  18.0 5.6 %all-to-all-done = bf16[4,2,32,1024]{3,2,1,0:T(8,128)(2,1)S(1)} async-done(((bf16[4,2,32,1024]{3,2,1,0:T(8,128)(2,1)}), bf16[4,2,32,1024]{3,2,1,0:T(8,128)(2,1)S(1)}, u32[]{:S(2)}, u32[]{:S(2)}) %all-to-all-start) | async-done | bytes 524320 | tf_op jit(solution)/shard_map/all_to_all | solution.py:411
  23.6 1.6 broadcast_in_dim.33
  25.2 3.9 %all-to-all-start.1 = ((bf16[8,128,1024]{2,1,0:T(8,128)(2,1)}), bf16[8,128,1024]{2,1,0:T(8,128)(2,1)S(1)}, u32[]{:S(2)}, u32[]{:S(2)}) async-start(bf16[8,128,1024]{2,1,0:T(8,128)(2,1)} %bitcast.44), calls=%async_computation.1 | async-start | bytes 4194304 | tf_op jit(solution)/shard_map/all_to_all | solution.py:423
  30.8 3.8 %gather_fusion = bf16[128,1024]{1,0:T(8,128)(2,1)S(1)} fusion(bf16[2048,1024]{1,0:T(8,128)(2,1)} %bitcast.47, s32[1024]{0:T(1024)S(1)} %pad_clamp_fusion), kind=kCustom, calls=%fused_computation | custom fusion | bytes 524800 | tf_op jit(solution)/shard_map/jit(_take)/gather | solution.py:427
  34.5 2.1 %collective-permute-start.1 = (bf16[128,1152]{1,0:T(8,128)(2,1)}, bf16[128,1152]{1,0:T(8,128)(2,1)S(1)}, u32[]{:S(2)}, u32[]{:S(2)}) collective-permute-start(bf16[128,1152]{1,0:T(8,128)(2,1)} %get-tuple-element.25), channel_id=1, source_target_pairs={{0,1},{1,2},{2,3},{3,0},{4,5},{5,6},{6,7},{7,4},{8,9},{9,10},{10,1... | collective-permute-start | bytes 884744 | tf_op jit(solution)/shard_map/ppermute | solution.py:379
  36.7 2.8 %collective-permute-start.3 = (bf16[128,1152]{1,0:T(8,128)(2,1)S(1)}, bf16[128,1152]{1,0:T(8,128)(2,1)S(1)}, u32[]{:S(2)}, u32[]{:S(2)}) collective-permute-start(bf16[128,1152]{1,0:T(8,128)(2,1)S(1)} %copy-done.21), channel_id=1, source_target_pairs={{0,3},{1,0},{2,1},{3,2},{4,7},{5,4},{6,5},{7,6},{8,11},{9,8},{10,9... | collective-permute-start | bytes 884744 | tf_op jit(solution)/shard_map/ppermute | solution.py:379
  39.5 0.8 broadcast_select_fusion.refs_5_
  40.3 6.2 %collective-permute-done.1.refs_2_ = bf16[128,1152]{1,0:T(8,128)(2,1)S(1)} collective-permute-done((bf16[128,1152]{1,0:T(8,128)(2,1)}, bf16[128,1152]{1,0:T(8,128)(2,1)S(1)}, u32[]{:S(2)}, u32[]{:S(2)}) %collective-permute-start.1) | collective-permute-done | bytes 294944 | tf_op jit(solution)/shard_map/ppermute | solution.py:379
  46.6 11.9 %collective-permute-done.2.refs_3_ = bf16[128,1152]{1,0:T(8,128)(2,1)S(1)} collective-permute-done((bf16[128,1152]{1,0:T(8,128)(2,1)S(1)}, bf16[128,1152]{1,0:T(8,128)(2,1)S(1)}, u32[]{:S(2)}, u32[]{:S(2)}) %collective-permute-start.2) | collective-permute-done | bytes 294944 | tf_op jit(solution)/shard_map/ppermute | solution.py:379
  58.5 0.7 copy-done.11
  59.3 3.6 %shard_map.86 = (f32[128,1024]{1,0:T(8,128)}, f32[128,1024]{1,0:T(8,128)}, bf16[128,1024]{1,0:T(8,128)(2,1)}, f32[128,1]{1,0:T(8,128)}, f32[128,1]{1,0:T(8,128)}) custom-call(s32[3]{0:T(128)} %pad_add_fusion.1.place_ref, f32[128,1024]{1,0:T(8,128)} %get-tuple-element.23.refs_0_, f32[128,1]{1,0:T(8,128)} %get-tuple-element.24.refs_1_, ...), custom_call_target="tpu_custom_call" | custom-call | flops 1310720 | bytes 1675776 | tf_op jit(solution)/shard_map/pallas_call | solution.py:33
  62.9 6.7 %collective-permute-start.5 = (bf16[128,1024]{1,0:T(8,128)(2,1)}, bf16[128,1024]{1,0:T(8,128)(2,1)S(1)}, u32[]{:S(2)}, u32[]{:S(2)}) collective-permute-start(bf16[128,1024]{1,0:T(8,128)(2,1)} %get-tuple-element.28), channel_id=1, source_target_pairs={{0,1},{1,0},{2,3},{3,2},{4,5},{5,4},{6,7},{7,6},{8,9},{9,8},{10,11... | collective-permute-start | bytes 786440 | tf_op jit(solution)/shard_map/ppermute | solution.py:382
  70.2 1.0 constant_dynamic-update-slice_fusion.1
  71.2 5.0 %collective-permute-done.5 = bf16[128,1024]{1,0:T(8,128)(2,1)S(1)} collective-permute-done((bf16[128,1024]{1,0:T(8,128)(2,1)}, bf16[128,1024]{1,0:T(8,128)(2,1)S(1)}, u32[]{:S(2)}, u32[]{:S(2)}) %collective-permute-start.5) | collective-permute-done | bytes 262176 | tf_op jit(solution)/shard_map/ppermute | solution.py:382
  76.3 0.8 fusion.8
  77.4 1.8 %collective-permute-start.6 = (f32[2,2,128]{2,1,0:T(2,128)S(1)}, f32[2,2,128]{2,1,0:T(2,128)S(1)}, u32[]{:S(2)}, u32[]{:S(2)}) collective-permute-start(f32[2,2,128]{2,1,0:T(2,128)S(1)} %pad_maximum_fusion), channel_id=1, source_target_pairs={{0,1},{1,0},{2,3},{3,2},{4,5},{5,4},{6,7},{7,6},{8,9},{9,8},{10,11... | collective-permute-start | bytes 6152 | tf_op jit(solution)/shard_map/ppermute | solution.py:382
  79.3 1.8 %collective-permute-done.6 = f32[2,2,128]{2,1,0:T(2,128)S(1)} collective-permute-done((f32[2,2,128]{2,1,0:T(2,128)S(1)}, f32[2,2,128]{2,1,0:T(2,128)S(1)}, u32[]{:S(2)}, u32[]{:S(2)}) %collective-permute-start.6) | collective-permute-done | bytes 2080 | tf_op jit(solution)/shard_map/ppermute | solution.py:382
  81.5 0.7 fusion.9.refs_0_
  82.6 2.1 %convolution_convert_fusion = bf16[1024,1024]{1,0:T(8,128)(2,1)} fusion(bf16[256,1024]{1,0:T(8,128)(2,1)S(1)} %copy-done.7, bf16[256,1024]{1,0:T(8,128)(2,1)S(1)} %multiply_convert_fusion), kind=kOutput, calls=%fused_computation.1 | convolution fusion | flops 537919488 | bytes 3145728 | tf_op jit(solution)/shard_map/dot_general | solution.py:17
  84.6 4.0 %all-to-all-start.3 = ((bf16[8,128,1024]{2,1,0:T(8,128)(2,1)}), bf16[8,128,1024]{2,1,0:T(8,128)(2,1)S(1)}, u32[]{:S(2)}, u32[]{:S(2)}) async-start(bf16[8,128,1024]{2,1,0:T(8,128)(2,1)} %bitcast.45), calls=%async_computation.3 | async-start | bytes 4194304 | tf_op jit(solution)/shard_map/all_to_all | solution.py:461
  88.6 1.8 %collective-permute-start.8 = (bf16[128,1024]{1,0:T(8,128)(2,1)S(1)}, bf16[128,1024]{1,0:T(8,128)(2,1)S(1)}, u32[]{:S(2)}, u32[]{:S(2)}) collective-permute-start(bf16[128,1024]{1,0:T(8,128)(2,1)S(1)} %slice.41), channel_id=1, source_target_pairs={{0,1},{1,0},{2,3},{3,2},{4,5},{5,4},{6,7},{7,6},{8,9},{9,8},{10,11... | collective-permute-start | bytes 786440 | tf_op jit(solution)/shard_map/ppermute | solution.py:382
  90.5 6.9 %collective-permute-done.8.refs_1_ = bf16[128,1024]{1,0:T(8,128)(2,1)S(1)} collective-permute-done((bf16[128,1024]{1,0:T(8,128)(2,1)S(1)}, bf16[128,1024]{1,0:T(8,128)(2,1)S(1)}, u32[]{:S(2)}, u32[]{:S(2)}) %collective-permute-start.8) | collective-permute-done | bytes 262176 | tf_op jit(solution)/shard_map/ppermute | solution.py:382
  97.4 0.7 copy-done.16
  98.1 3.3 %shard_map.87.refs_0_ = bf16[128,1152]{1,0:T(8,128)(2,1)} custom-call(s32[3]{0:T(128)} %pad_add_fusion.1.place_ref, f32[256,1024]{1,0:T(8,128)} %copy-done.2, bf16[128,1024]{1,0:T(8,128)(2,1)} %copy-done.16, f32[128,1024]{1,0:T(8,128)} %get-tuple-element.30.refs_2_, f32[128,1024]{1,0:T(8,128)} %get-tuple-element.31.refs_3_, ...), custom_call_target="tpu_custom_call" | custom-call | flops 1310720 | bytes 2364416 | tf_op jit(solution)/shard_map/pallas_call | solution.py:33
  101.4 0.7 collective-permute-start.10
  102.1 3.4 %collective-permute-start.11 = (bf16[128,1152]{1,0:T(8,128)(2,1)}, bf16[128,1152]{1,0:T(8,128)(2,1)S(1)}, u32[]{:S(2)}, u32[]{:S(2)}) collective-permute-start(bf16[128,1152]{1,0:T(8,128)(2,1)} %shard_map.87.refs_0_), channel_id=1, source_target_pairs={{0,3},{1,0},{2,1},{3,2},{4,7},{5,4},{6,5},{7,6},{8,11},{9,8},{10,9... | collective-permute-start | bytes 884744 | tf_op jit(solution)/shard_map/ppermute | solution.py:379
  105.5 1.0 copy.22
  106.5 1.7 %collective-permute-start.14 = (bf16[1024,256]{1,0:T(8,128)(2,1)}, bf16[1024,256]{1,0:T(8,128)(2,1)}, u32[]{:S(2)}, u32[]{:S(2)}) collective-permute-start(bf16[1024,256]{1,0:T(8,128)(2,1)} %bitcast.25.refs_0_), channel_id=1, source_target_pairs={{0,8},{4,12},{8,16},{12,20},{16,24},{20,28},{24,0},{28,4},{1,9},{5... | collective-permute-start | bytes 1572872 | tf_op jit(solution)/shard_map/ppermute | solution.py:406
  108.2 1.5 collective-permute-start.16
  109.6 10.4 %collective-permute-done.10.refs_2_ = bf16[128,1152]{1,0:T(8,128)(2,1)S(1)} collective-permute-done((bf16[128,1152]{1,0:T(8,128)(2,1)}, bf16[128,1152]{1,0:T(8,128)(2,1)S(1)}, u32[]{:S(2)}, u32[]{:S(2)}) %collective-permute-start.10) | collective-permute-done | bytes 294944 | tf_op jit(solution)/shard_map/ppermute | solution.py:379
  120.0 7.3 %collective-permute-start.18 = (bf16[1024,256]{1,0:T(8,128)(2,1)}, bf16[1024,256]{1,0:T(8,128)(2,1)}, u32[]{:S(2)}, u32[]{:S(2)}) collective-permute-start(bf16[1024,256]{1,0:T(8,128)(2,1)} %bitcast.25.refs_0_), channel_id=1, source_target_pairs={{0,24},{4,28},{8,0},{12,4},{16,8},{20,12},{24,16},{28,20},{1,25},{... | collective-permute-start | bytes 1572872 | tf_op jit(solution)/shard_map/ppermute | solution.py:406
  127.3 0.7 copy-done.14
  128.0 0.7 copy-done.15
  128.7 3.7 %shard_map.88 = (bf16[8,512,128]{2,1,0:T(8,128)(2,1)}, bf16[256,1152]{1,0:T(8,128)(2,1)}, bf16[256,1152]{1,0:T(8,128)(2,1)}) custom-call(s32[3]{0:T(128)} %pad_add_fusion.1.place_ref, bf16[128,1152]{1,0:T(8,128)(2,1)} %shard_map.87.refs_0_, bf16[128,1152]{1,0:T(8,128)(2,1)} %copy-done.15, bf16[128,1152]{1,0:T(8,128)(2,1)} %copy-done.13, ...), custom_call_target="tpu_custom_call" | custom-call | flops 524288 | bytes 1179648 | tf_op jit(solution)/shard_map/pallas_call | solution.py:33
  132.4 3.6 %all-to-all-start.2 = ((bf16[8,512,128]{2,1,0:T(8,128)(2,1)}), bf16[8,512,128]{2,1,0:T(8,128)(2,1)S(1)}, u32[]{:S(2)}, u32[]{:S(2)}) async-start(bf16[8,512,128]{2,1,0:T(8,128)(2,1)} %get-tuple-element.37), calls=%async_computation.2 | async-start | bytes 2097152 | tf_op jit(solution)/shard_map/all_to_all | solution.py:468
  138.0 3.2 %shard_map.91 = (bf16[2,32,1024]{2,1,0:T(8,128)(2,1)}, bf16[2,32,1024]{2,1,0:T(8,128)(2,1)}, bf16[2,32,1024]{2,1,0:T(8,128)(2,1)}, bf16[2,32,1024]{2,1,0:T(8,128)(2,1)}) custom-call(s32[3]{0:T(128)} %pad_add_fusion.1.place_ref, bf16[8,128,1024]{2,1,0:T(8,128)(2,1)} %copy-done.1), custom_call_target="tpu_custom_call" | custom-call | flops 1048576 | bytes 2097152 | tf_op jit(solution)/shard_map/pallas_call | solution.py:33
  141.3 2.8 %collective-permute-start.20 = (bf16[2,32,1024]{2,1,0:T(8,128)(2,1)}, bf16[2,32,1024]{2,1,0:T(8,128)(2,1)S(1)}, u32[]{:S(2)}, u32[]{:S(2)}) collective-permute-start(bf16[2,32,1024]{2,1,0:T(8,128)(2,1)} %get-tuple-element.40), channel_id=1, source_target_pairs={{0,1},{1,2},{2,3},{3,0},{4,5},{5,6},{6,7},{7,4},{8,9},{9,10},{10,1... | collective-permute-start | bytes 393224 | tf_op jit(solution)/shard_map/ppermute | solution.py:379
  144.3 2.3 %collective-permute-start.22 = (bf16[2,32,1024]{2,1,0:T(8,128)(2,1)}, bf16[2,32,1024]{2,1,0:T(8,128)(2,1)S(1)}, u32[]{:S(2)}, u32[]{:S(2)}) collective-permute-start(bf16[2,32,1024]{2,1,0:T(8,128)(2,1)} %get-tuple-element.42), channel_id=1, source_target_pairs={{0,3},{1,0},{2,1},{3,2},{4,7},{5,4},{6,5},{7,6},{8,11},{9,8},{10,9... | collective-permute-start | bytes 393224 | tf_op jit(solution)/shard_map/ppermute | solution.py:379
  146.5 5.9 %shard_map.89 = bf16[256,1024]{1,0:T(8,128)(2,1)} custom-call(s32[3]{0:T(128)} %pad_add_fusion.1.place_ref, bf16[256,1152]{1,0:T(8,128)(2,1)} %get-tuple-element.34.refs_0_, bf16[256,1152]{1,0:T(8,128)(2,1)} %collective-permute-done.12.refs_1_, bf16[2,1024,1024]{2,1,0:T(8,128)(2,1)} %refs_2_.3, bf16[256,1024]{1,0:T(8,128)(2,1)} %refs_3_.1), custom_call_target="tpu_custom_call" | custom-call | flops 1073741824 | bytes 5898240 | tf_op jit(solution)/shard_map/pallas_call | solution.py:33
  152.5 1.0 copy-done.5
  153.5 5.2 %shard_map.90 = f32[2,1024,128]{2,1,0:T(8,128)} custom-call(s32[3]{0:T(128)} %pad_add_fusion.1.place_ref, bf16[1024,256]{1,0:T(8,128)(2,1)} %bitcast.25.refs_0_, bf16[1024,256]{1,0:T(8,128)(2,1)} %copy-done.8, bf16[1024,256]{1,0:T(8,128)(2,1)} %collective-permute-done.14.refs_2_, bf16[1024,256]{1,0:T(8,128)(2,1)} %collective-permute-done.15.refs_3_, ...), custom_call_target="tpu_custom_call" | custom-call | flops 1073741824 | bytes 5242880 | tf_op jit(solution)/shard_map/pallas_call | solution.py:33
  159.4 2.7 %shard_map.92 = f32[32,2,2048]{2,1,0:T(2,128)} custom-call(s32[3]{0:T(128)} %pad_add_fusion.1.place_ref, bf16[2,32,1024]{2,1,0:T(8,128)(2,1)} %get-tuple-element.39.refs_0_, bf16[2,32,1024]{2,1,0:T(8,128)(2,1)} %copy-done.17, bf16[2,32,1024]{2,1,0:T(8,128)(2,1)} %copy-done.18, bf16[2,32,1024]{2,1,0:T(8,128)(2,1)} %copy-done.19), custom_call_target="tpu_custom_call" | custom-call | flops 262144 | bytes 524288 | tf_op jit(solution)/shard_map/pallas_call | solution.py:33
  (94 shorter events, 7.3 us)
Async XLA Ops:
  0.6 29.1 %copy-start = (f32[2,1024]{1,0:T(2,128)S(1)}, f32[2,1024]{1,0:T(2,128)}, u32[]{:S(2)}) copy-start(f32[2,1024]{1,0:T(2,128)} %param.9) | copy-start | bytes 24580
  0.6 8.5 %copy-start.3 = (bf16[256,1024]{1,0:T(8,128)(2,1)S(1)}, bf16[256,1024]{1,0:T(8,128)(2,1)}, u32[]{:S(2)}) copy-start(bf16[256,1024]{1,0:T(8,128)(2,1)} %refs_3_.1) | copy-start | bytes 1572868
  2.8 20.8 %all-to-all-start = ((bf16[4,2,32,1024]{3,2,1,0:T(8,128)(2,1)}), bf16[4,2,32,1024]{3,2,1,0:T(8,128)(2,1)S(1)}, u32[]{:S(2)}, u32[]{:S(2)}) async-start(bf16[4,2,32,1024]{3,2,1,0:T(8,128)(2,1)} %bitcast.11), calls=%async_computation | async-start | bytes 1048576 | tf_op jit(solution)/shard_map/all_to_all | solution.py:411
  9.1 1.9 %collective-permute-start = (bf16[256,1024]{1,0:T(8,128)(2,1)S(1)}, bf16[256,1024]{1,0:T(8,128)(2,1)S(1)}, u32[]{:S(2)}, u32[]{:S(2)}) collective-permute-start(bf16[256,1024]{1,0:T(8,128)(2,1)S(1)} %copy-done.3), channel_id=1, source_target_pairs={{0,4},{4,0},{8,12},{12,8},{16,20},{20,16},{24,28},{28,24},{1,5},{5... | collective-permute-start | bytes 1572872 | tf_op jit(solution)/shard_map/ppermute | solution.py:389
  11.0 0.8 copy-start.9
  25.2 3.9 %copy-start.20 = (s32[2,64]{1,0:T(2,128)S(1)}, s32[2,64]{1,0:T(2,128)}, u32[]{:S(2)}) copy-start(s32[2,64]{1,0:T(2,128)} %param.11) | copy-start | bytes 1540
  25.2 51.0 %all-to-all-start.1 = ((bf16[8,128,1024]{2,1,0:T(8,128)(2,1)}), bf16[8,128,1024]{2,1,0:T(8,128)(2,1)S(1)}, u32[]{:S(2)}, u32[]{:S(2)}) async-start(bf16[8,128,1024]{2,1,0:T(8,128)(2,1)} %bitcast.44), calls=%async_computation.1 | async-start | bytes 4194304 | tf_op jit(solution)/shard_map/all_to_all | solution.py:423
  29.1 7.5 %copy-start.22 = (bf16[128,1152]{1,0:T(8,128)(2,1)S(1)}, bf16[128,1152]{1,0:T(8,128)(2,1)}, u32[]{:S(2)}) copy-start(bf16[128,1152]{1,0:T(8,128)(2,1)} %get-tuple-element.26) | copy-start | bytes 884740
  29.1 7.6 %copy-start.21 = (bf16[128,1152]{1,0:T(8,128)(2,1)S(1)}, bf16[128,1152]{1,0:T(8,128)(2,1)}, u32[]{:S(2)}) copy-start(bf16[128,1152]{1,0:T(8,128)(2,1)} %get-tuple-element.27) | copy-start | bytes 884740
  29.1 1.5 collective-permute-start.4
  30.7 38.8 %collective-permute-start.7 = (s32[2,128]{1,0:T(2,128)S(1)}, s32[2,128]{1,0:T(2,128)}, u32[]{:S(2)}, u32[]{:S(2)}) collective-permute-start(s32[2,128]{1,0:T(2,128)S(1)} %reshape.93), channel_id=1, source_target_pairs={{0,1},{1,0},{2,3},{3,2},{4,5},{5,4},{6,7},{7,6},{8,9},{9,8},{10,11... | collective-permute-start | bytes 3080 | tf_op jit(solution)/shard_map/ppermute | solution.py:382
  34.5 12.0 %collective-permute-start.1 = (bf16[128,1152]{1,0:T(8,128)(2,1)}, bf16[128,1152]{1,0:T(8,128)(2,1)S(1)}, u32[]{:S(2)}, u32[]{:S(2)}) collective-permute-start(bf16[128,1152]{1,0:T(8,128)(2,1)} %get-tuple-element.25), channel_id=1, source_target_pairs={{0,1},{1,2},{2,3},{3,0},{4,5},{5,6},{6,7},{7,4},{8,9},{9,10},{10,1... | collective-permute-start | bytes 884744 | tf_op jit(solution)/shard_map/ppermute | solution.py:379
  36.6 21.9 %collective-permute-start.2 = (bf16[128,1152]{1,0:T(8,128)(2,1)S(1)}, bf16[128,1152]{1,0:T(8,128)(2,1)S(1)}, u32[]{:S(2)}, u32[]{:S(2)}) collective-permute-start(bf16[128,1152]{1,0:T(8,128)(2,1)S(1)} %copy-done.22), channel_id=1, source_target_pairs={{0,2},{1,3},{2,0},{3,1},{4,6},{5,7},{6,4},{7,5},{8,10},{9,11},{10,... | collective-permute-start | bytes 884744 | tf_op jit(solution)/shard_map/ppermute | solution.py:379
  36.7 21.8 %collective-permute-start.3 = (bf16[128,1152]{1,0:T(8,128)(2,1)S(1)}, bf16[128,1152]{1,0:T(8,128)(2,1)S(1)}, u32[]{:S(2)}, u32[]{:S(2)}) collective-permute-start(bf16[128,1152]{1,0:T(8,128)(2,1)S(1)} %copy-done.21), channel_id=1, source_target_pairs={{0,3},{1,0},{2,1},{3,2},{4,7},{5,4},{6,5},{7,6},{8,11},{9,8},{10,9... | collective-permute-start | bytes 884744 | tf_op jit(solution)/shard_map/ppermute | solution.py:379
  46.6 11.9 %copy-start.10 = (bf16[128,1152]{1,0:T(8,128)(2,1)}, bf16[128,1152]{1,0:T(8,128)(2,1)S(1)}, u32[]{:S(2)}) copy-start(bf16[128,1152]{1,0:T(8,128)(2,1)S(1)} %collective-permute-done.1.refs_2_) | copy-start | bytes 884740
  58.5 0.7 copy-start.11
  58.5 0.8 copy-start.12
  62.9 13.4 %collective-permute-start.5 = (bf16[128,1024]{1,0:T(8,128)(2,1)}, bf16[128,1024]{1,0:T(8,128)(2,1)S(1)}, u32[]{:S(2)}, u32[]{:S(2)}) collective-permute-start(bf16[128,1024]{1,0:T(8,128)(2,1)} %get-tuple-element.28), channel_id=1, source_target_pairs={{0,1},{1,0},{2,3},{3,2},{4,5},{5,4},{6,7},{7,6},{8,9},{9,8},{10,11... | collective-permute-start | bytes 786440 | tf_op jit(solution)/shard_map/ppermute | solution.py:382
  76.3 1.1 copy-start.6
  77.4 3.7 %collective-permute-start.6 = (f32[2,2,128]{2,1,0:T(2,128)S(1)}, f32[2,2,128]{2,1,0:T(2,128)S(1)}, u32[]{:S(2)}, u32[]{:S(2)}) collective-permute-start(f32[2,2,128]{2,1,0:T(2,128)S(1)} %pad_maximum_fusion), channel_id=1, source_target_pairs={{0,1},{1,0},{2,3},{3,2},{4,5},{5,4},{6,7},{7,6},{8,9},{9,8},{10,11... | collective-permute-start | bytes 6152 | tf_op jit(solution)/shard_map/ppermute | solution.py:382
  81.5 1.0 copy-start.7
  82.3 2.4 %copy-start.2 = (f32[256,1024]{1,0:T(8,128)}, f32[256,1024]{1,0:T(8,128)S(1)}, u32[]{:S(2)}) copy-start(f32[256,1024]{1,0:T(8,128)S(1)} %fusion.9.refs_0_) | copy-start | bytes 3145732
  84.6 47.7 %all-to-all-start.3 = ((bf16[8,128,1024]{2,1,0:T(8,128)(2,1)}), bf16[8,128,1024]{2,1,0:T(8,128)(2,1)S(1)}, u32[]{:S(2)}, u32[]{:S(2)}) async-start(bf16[8,128,1024]{2,1,0:T(8,128)(2,1)} %bitcast.45), calls=%async_computation.3 | async-start | bytes 4194304 | tf_op jit(solution)/shard_map/all_to_all | solution.py:461
  88.6 16.8 %copy-start.4 = (bf16[256,1024]{1,0:T(8,128)(2,1)S(1)}, bf16[256,1024]{1,0:T(8,128)(2,1)}, u32[]{:S(2)}) copy-start(bf16[256,1024]{1,0:T(8,128)(2,1)} %refs_3_.1) | copy-start | bytes 1572868
  88.6 8.7 %collective-permute-start.8 = (bf16[128,1024]{1,0:T(8,128)(2,1)S(1)}, bf16[128,1024]{1,0:T(8,128)(2,1)S(1)}, u32[]{:S(2)}, u32[]{:S(2)}) collective-permute-start(bf16[128,1024]{1,0:T(8,128)(2,1)S(1)} %slice.41), channel_id=1, source_target_pairs={{0,1},{1,0},{2,3},{3,2},{4,5},{5,4},{6,7},{7,6},{8,9},{9,8},{10,11... | collective-permute-start | bytes 786440 | tf_op jit(solution)/shard_map/ppermute | solution.py:382
  97.4 0.7 copy-start.16
  101.4 18.6 %collective-permute-start.10 = (bf16[128,1152]{1,0:T(8,128)(2,1)}, bf16[128,1152]{1,0:T(8,128)(2,1)S(1)}, u32[]{:S(2)}, u32[]{:S(2)}) collective-permute-start(bf16[128,1152]{1,0:T(8,128)(2,1)} %shard_map.87.refs_0_), channel_id=1, source_target_pairs={{0,2},{1,3},{2,0},{3,1},{4,6},{5,7},{6,4},{7,5},{8,10},{9,11},{10,... | collective-permute-start | bytes 884744 | tf_op jit(solution)/shard_map/ppermute | solution.py:379
  102.1 25.2 %collective-permute-start.11 = (bf16[128,1152]{1,0:T(8,128)(2,1)}, bf16[128,1152]{1,0:T(8,128)(2,1)S(1)}, u32[]{:S(2)}, u32[]{:S(2)}) collective-permute-start(bf16[128,1152]{1,0:T(8,128)(2,1)} %shard_map.87.refs_0_), channel_id=1, source_target_pairs={{0,3},{1,0},{2,1},{3,2},{4,7},{5,4},{6,5},{7,6},{8,11},{9,8},{10,9... | collective-permute-start | bytes 884744 | tf_op jit(solution)/shard_map/ppermute | solution.py:379
  105.5 21.8 %collective-permute-start.9 = (bf16[128,1152]{1,0:T(8,128)(2,1)}, bf16[128,1152]{1,0:T(8,128)(2,1)S(1)}, u32[]{:S(2)}, u32[]{:S(2)}) collective-permute-start(bf16[128,1152]{1,0:T(8,128)(2,1)} %shard_map.87.refs_0_), channel_id=1, source_target_pairs={{0,1},{1,2},{2,3},{3,0},{4,5},{5,6},{6,7},{7,4},{8,9},{9,10},{10,1... | collective-permute-start | bytes 884744 | tf_op jit(solution)/shard_map/ppermute | solution.py:379
  106.5 30.0 %collective-permute-start.14 = (bf16[1024,256]{1,0:T(8,128)(2,1)}, bf16[1024,256]{1,0:T(8,128)(2,1)}, u32[]{:S(2)}, u32[]{:S(2)}) collective-permute-start(bf16[1024,256]{1,0:T(8,128)(2,1)} %bitcast.25.refs_0_), channel_id=1, source_target_pairs={{0,8},{4,12},{8,16},{12,20},{16,24},{20,28},{24,0},{28,4},{1,9},{5... | collective-permute-start | bytes 1572872 | tf_op jit(solution)/shard_map/ppermute | solution.py:406
  108.2 29.4 %collective-permute-start.16 = (bf16[1024,256]{1,0:T(8,128)(2,1)}, bf16[1024,256]{1,0:T(8,128)(2,1)}, u32[]{:S(2)}, u32[]{:S(2)}) collective-permute-start(bf16[1024,256]{1,0:T(8,128)(2,1)} %bitcast.25.refs_0_), channel_id=1, source_target_pairs={{0,16},{4,20},{8,24},{12,28},{16,0},{20,4},{24,8},{28,12},{1,17},{... | collective-permute-start | bytes 1572872 | tf_op jit(solution)/shard_map/ppermute | solution.py:406
  120.0 7.3 %copy-start.13 = (bf16[128,1152]{1,0:T(8,128)(2,1)}, bf16[128,1152]{1,0:T(8,128)(2,1)S(1)}, u32[]{:S(2)}) copy-start(bf16[128,1152]{1,0:T(8,128)(2,1)S(1)} %collective-permute-done.10.refs_2_) | copy-start | bytes 884740
  120.0 17.5 %collective-permute-start.18 = (bf16[1024,256]{1,0:T(8,128)(2,1)}, bf16[1024,256]{1,0:T(8,128)(2,1)}, u32[]{:S(2)}, u32[]{:S(2)}) collective-permute-start(bf16[1024,256]{1,0:T(8,128)(2,1)} %bitcast.25.refs_0_), channel_id=1, source_target_pairs={{0,24},{4,28},{8,0},{12,4},{16,8},{20,12},{24,16},{28,20},{1,25},{... | collective-permute-start | bytes 1572872 | tf_op jit(solution)/shard_map/ppermute | solution.py:406
  127.3 0.7 copy-start.14
  128.0 0.7 copy-start.15
  132.4 5.7 %copy-start.1 = (bf16[8,128,1024]{2,1,0:T(8,128)(2,1)}, bf16[8,128,1024]{2,1,0:T(8,128)(2,1)S(1)}, u32[]{:S(2)}) copy-start(bf16[8,128,1024]{2,1,0:T(8,128)(2,1)S(1)} %all-to-all-done.3.received) | copy-start | bytes 6291460
  132.4 20.1 %all-to-all-start.2 = ((bf16[8,512,128]{2,1,0:T(8,128)(2,1)}), bf16[8,512,128]{2,1,0:T(8,128)(2,1)S(1)}, u32[]{:S(2)}, u32[]{:S(2)}) async-start(bf16[8,512,128]{2,1,0:T(8,128)(2,1)} %get-tuple-element.37), calls=%async_computation.2 | async-start | bytes 2097152 | tf_op jit(solution)/shard_map/all_to_all | solution.py:468
  136.0 8.3 %collective-permute-start.12 = (bf16[256,1152]{1,0:T(8,128)(2,1)}, bf16[256,1152]{1,0:T(8,128)(2,1)}, u32[]{:S(2)}, u32[]{:S(2)}) collective-permute-start(bf16[256,1152]{1,0:T(8,128)(2,1)} %get-tuple-element.35), channel_id=1, source_target_pairs={{0,4},{4,0},{8,12},{12,8},{16,20},{20,16},{24,28},{28,24},{1,5},{5... | collective-permute-start | bytes 1769480 | tf_op jit(solution)/shard_map/ppermute | solution.py:389
  136.4 4.9 %collective-permute-start.13 = (bf16[1024,256]{1,0:T(8,128)(2,1)}, bf16[1024,256]{1,0:T(8,128)(2,1)S(1)}, u32[]{:S(2)}, u32[]{:S(2)}) collective-permute-start(bf16[1024,256]{1,0:T(8,128)(2,1)} %bitcast.25.refs_0_), channel_id=1, source_target_pairs={{0,4},{4,0},{8,12},{12,8},{16,20},{20,16},{24,28},{28,24},{1,5},{5... | collective-permute-start | bytes 1572872 | tf_op jit(solution)/shard_map/ppermute | solution.py:389
  136.5 7.5 %collective-permute-start.15 = (bf16[1024,256]{1,0:T(8,128)(2,1)}, bf16[1024,256]{1,0:T(8,128)(2,1)}, u32[]{:S(2)}, u32[]{:S(2)}) collective-permute-start(bf16[1024,256]{1,0:T(8,128)(2,1)} %collective-permute-done.14.refs_2_), channel_id=1, source_target_pairs={{0,4},{4,0},{8,12},{12,8},{16,20},{20,16},{24,28},{28,24},{1,5},{5... | collective-permute-start | bytes 1572872 | tf_op jit(solution)/shard_map/ppermute | solution.py:389
  137.5 14.9 %collective-permute-start.17 = (bf16[1024,256]{1,0:T(8,128)(2,1)}, bf16[1024,256]{1,0:T(8,128)(2,1)}, u32[]{:S(2)}, u32[]{:S(2)}) collective-permute-start(bf16[1024,256]{1,0:T(8,128)(2,1)} %collective-permute-done.16.refs_4_), channel_id=1, source_target_pairs={{0,4},{4,0},{8,12},{12,8},{16,20},{20,16},{24,28},{28,24},{1,5},{5... | collective-permute-start | bytes 1572872 | tf_op jit(solution)/shard_map/ppermute | solution.py:389
  137.5 14.9 %collective-permute-start.19 = (bf16[1024,256]{1,0:T(8,128)(2,1)}, bf16[1024,256]{1,0:T(8,128)(2,1)}, u32[]{:S(2)}, u32[]{:S(2)}) collective-permute-start(bf16[1024,256]{1,0:T(8,128)(2,1)} %collective-permute-done.18.refs_6_), channel_id=1, source_target_pairs={{0,4},{4,0},{8,12},{12,8},{16,20},{20,16},{24,28},{28,24},{1,5},{5... | collective-permute-start | bytes 1572872 | tf_op jit(solution)/shard_map/ppermute | solution.py:389
  141.3 11.2 %copy-start.8 = (bf16[1024,256]{1,0:T(8,128)(2,1)}, bf16[1024,256]{1,0:T(8,128)(2,1)S(1)}, u32[]{:S(2)}) copy-start(bf16[1024,256]{1,0:T(8,128)(2,1)S(1)} %collective-permute-done.13.refs_1_) | copy-start | bytes 1572868
  141.3 17.4 %collective-permute-start.20 = (bf16[2,32,1024]{2,1,0:T(8,128)(2,1)}, bf16[2,32,1024]{2,1,0:T(8,128)(2,1)S(1)}, u32[]{:S(2)}, u32[]{:S(2)}) collective-permute-start(bf16[2,32,1024]{2,1,0:T(8,128)(2,1)} %get-tuple-element.40), channel_id=1, source_target_pairs={{0,1},{1,2},{2,3},{3,0},{4,5},{5,6},{6,7},{7,4},{8,9},{9,10},{10,1... | collective-permute-start | bytes 393224 | tf_op jit(solution)/shard_map/ppermute | solution.py:379
  144.1 14.6 %collective-permute-start.21 = (bf16[2,32,1024]{2,1,0:T(8,128)(2,1)}, bf16[2,32,1024]{2,1,0:T(8,128)(2,1)S(1)}, u32[]{:S(2)}, u32[]{:S(2)}) collective-permute-start(bf16[2,32,1024]{2,1,0:T(8,128)(2,1)} %get-tuple-element.41), channel_id=1, source_target_pairs={{0,2},{1,3},{2,0},{3,1},{4,6},{5,7},{6,4},{7,5},{8,10},{9,11},{10,... | collective-permute-start | bytes 393224 | tf_op jit(solution)/shard_map/ppermute | solution.py:379
  144.3 14.4 %collective-permute-start.22 = (bf16[2,32,1024]{2,1,0:T(8,128)(2,1)}, bf16[2,32,1024]{2,1,0:T(8,128)(2,1)S(1)}, u32[]{:S(2)}, u32[]{:S(2)}) collective-permute-start(bf16[2,32,1024]{2,1,0:T(8,128)(2,1)} %get-tuple-element.42), channel_id=1, source_target_pairs={{0,3},{1,0},{2,1},{3,2},{4,7},{5,4},{6,5},{7,6},{8,11},{9,8},{10,9... | collective-permute-start | bytes 393224 | tf_op jit(solution)/shard_map/ppermute | solution.py:379
  152.5 1.0 copy-start.5
  158.7 0.7 copy-start.19
  (2 other events, 1.3 us)

commit v3 on v2

--- a/solution.py
+++ b/solution.py
@@ -26,6 +26,10 @@
 
 def whole(shape):
     return pl.BlockSpec(shape, lambda n, place: (0,) * len(shape))
+
+
+def rows_of(shape, some):
+    return pl.BlockSpec((some, shape[1]), lambda n, place: (n, 0))
 
 
 def call(kernel, place, grid, in_specs, out_specs, out_shape, scratch, flops, args):
@@ -77,8 +81,8 @@
         hidden, w, own, squares = refs[:steps], refs[steps], refs[steps + 1], refs[steps + 2]
         sends, sums, totals = refs[steps + 3 : -2], refs[-2], refs[-1]
         n, step, j = pl.program_id(0), place_ref[0], place_ref[1]
-        left = jnp.concatenate([h[...] for h in hidden], axis=0)
-        sums[...] = jnp.dot(left, w[0], preferred_element_type=F32).reshape(steps, rows, wide)
+        for m in range(steps):
+            sums[m] = jnp.dot(hidden[m][...], w[0], preferred_element_type=F32)
         columns = pl.ds(pl.multiple_of(n * wide, wide), wide)
         for shift in range(hids):
             out = own if shift == 0 else sends[shift - 1]
@@ -123,6 +127,7 @@
 def normalise(place, proj, squares, received, looked, gain, width_in):
     owned, depth = proj.shape
     count = len(received)
+    some = min(32, owned)
 
     def kernel(place_ref, *refs):
         proj, squares, looked, gain = refs[0], refs[1], refs[2 + count], refs[3 + count]
@@ -146,9 +151,9 @@
     return call(
         kernel,
         place,
-        1,
-        [whole(a.shape) for a in args],
-        [whole(shape) for shape, _ in shapes],
+        owned // some,
+        [rows_of(a.shape, some) for a in args[:-1]] + [whole(gain.shape)],
+        [rows_of(shape, some) for shape, _ in shapes],
         [jax.ShapeDtypeStruct(shape, dtype) for shape, dtype in shapes],
         [],
         10 * owned * depth,
@@ -175,13 +180,14 @@
         out[:, depth:] = parts_of([ratio, correction], 2)
 
     len_received = len(received)
+    some = min(32, owned)
     args = (d_norm, *received, x_rows, proj, scale, ratio, gain)
     return call(
         kernel,
         place,
-        1,
-        [whole((owned, depth))] + [whole(a.shape) for a in args[1:]],
-        whole((owned, depth + EXTRA)),
+        owned // some,
+        [rows_of(a.shape, some) for a in args[:-1]] + [whole(gain.shape)],
+        rows_of((owned, depth + EXTRA), some),
         jax.ShapeDtypeStruct((owned, depth + EXTRA), BF16),
         [],
         10 * owned * depth,
@@ -189,43 +195,58 @@
     )
 
 
-def spread(place, pieces, seqs, steps):
-    hids = len(pieces)
+def input_gradient(place, pieces, turned, seqs):
+    hids, steps = len(pieces), len(turned)
     owned, full = pieces[0].shape
     depth = full - EXTRA
+    units, rows = turned[0].shape
     part = owned // steps
-    rows = part * hids
-    wide = depth // seqs
-
-    def kernel(place_ref, *refs):
-        pieces, scaled, plain = refs[:hids], refs[hids], refs[hids + 1 :]
-        step, j = place_ref[0], place_ref[1]
-        for shift in range(hids):
-            owner = lax.rem(j - shift + hids, hids)
-            ratio = column_of(pieces[shift][:, depth:], 0)
-            values = (pieces[shift][:, :depth].astype(F32) * ratio).astype(BF16)
-            for m in range(steps):
-                at = pl.multiple_of(m * rows + owner * part, part)
-                for q in range(seqs):
-                    scaled[q, pl.ds(at, part), :] = values[
-                        m * part : (m + 1) * part, q * wide : (q + 1) * wide
-                    ]
-            to = pl.multiple_of(owner * part, part)
+    slice_wide = depth // seqs
+    wide = max(min(256, depth), slice_wide)
+    count = wide // slice_wide
+
+    def kernel(place_ref, *refs):
+        chunks, extras, turned = refs[:hids], refs[hids : 2 * hids], refs[2 * hids : 2 * hids + steps]
+        out, plain, scaled = refs[2 * hids + steps], refs[2 * hids + steps + 1 : -1], refs[-1]
+        n, step, j = pl.program_id(0), place_ref[0], place_ref[1]
+        columns = pl.ds(pl.multiple_of(n * wide, wide), wide)
+        for r in range(hids):
+            to = pl.multiple_of(lax.rem(j - r + hids, hids) * part, part)
             for m in range(steps):
                 start = pl.multiple_of(lax.rem(step + m, steps) * part, part)
-                plain[m][pl.ds(to, part), :] = pieces[shift][pl.ds(start, part), :]
-
-    return call(
-        kernel,
-        place,
-        1,
-        [whole((owned, full))] * hids,
-        [whole((seqs, steps * rows, wide))] + [whole((rows, full))] * steps,
-        [jax.ShapeDtypeStruct((seqs, steps * rows, wide), BF16)]
+                values = chunks[r][pl.ds(start, part), :]
+                plain[m][pl.ds(to, part), columns] = values
+                ratio = column_of(extras[r][pl.ds(start, part), :], 0)
+                scaled[m, pl.ds(to, part), :] = (values.astype(F32) * ratio).astype(BF16)
+
+        @pl.when(n == 0)
+        def _():
+            for r in range(hids):
+                to = pl.multiple_of(lax.rem(j - r + hids, hids) * part, part)
+                for m in range(steps):
+                    start = pl.multiple_of(lax.rem(step + m, steps) * part, part)
+                    plain[m][pl.ds(to, part), depth:] = extras[r][pl.ds(start, part), :]
+
+        total = jnp.dot(turned[0][...], scaled[0], preferred_element_type=F32)
+        for m in range(1, steps):
+            total = total + jnp.dot(turned[m][...], scaled[m], preferred_element_type=F32)
+        for k in range(count):
+            out[k] = total[:, k * slice_wide : (k + 1) * slice_wide].astype(BF16)
+
+    return call(
+        kernel,
+        place,
+        depth // wide,
+        [pl.BlockSpec((owned, wide), lambda n, place: (0, n))] * hids
+        + [pl.BlockSpec((owned, EXTRA), lambda n, place: (0, depth // EXTRA))] * hids
+        + [whole((units, rows))] * steps,
+        [pl.BlockSpec((count, units, slice_wide), lambda n, place: (n, 0, 0))]
+        + [whole((rows, full))] * steps,
+        [jax.ShapeDtypeStruct((seqs, units, slice_wide), BF16)]
         + [jax.ShapeDtypeStruct((rows, full), BF16)] * steps,
-        [],
-        steps * rows * depth,
-        tuple(pieces),
+        [pltpu.VMEM((steps, rows, wide), BF16)],
+        2 * steps * rows * units * depth,
+        (*pieces, *pieces, *turned),
     )
 
 
@@ -233,6 +254,7 @@
     seqs, rows, entries = received.shape
     groups = seqs // steps
     part = rows // hids
+    wide = min(256, entries)
 
     def kernel(place_ref, received, *outs):
         for shift in range(hids):
@@ -246,9 +268,9 @@
     return call(
         kernel,
         place,
-        1,
-        [whole(received.shape)],
-        [whole((steps, part, entries))] * hids,
+        entries // wide,
+        [pl.BlockSpec((seqs, rows, wide), lambda n, place: (0, 0, n))],
+        [pl.BlockSpec((steps, part, wide), lambda n, place: (0, 0, n))] * hids,
         [jax.ShapeDtypeStruct((steps, part, entries), BF16)] * hids,
         [],
         seqs * rows * entries,
@@ -281,42 +303,6 @@
         [],
         hids * steps * rows * block,
         tuple(pieces),
-    )
-
-
-def input_gradient(place, blocks, scaled, steps):
-    groups = len(blocks)
-    units, rows = blocks[0][0].shape
-    wide = scaled.shape[2]
-    tall = min(512, units)
-
-    def kernel(place_ref, *refs):
-        hidden, scaled, out = refs[:-2], refs[-2], refs[-1]
-        step, group = place_ref[0], place_ref[2]
-        total = None
-        for r in range(groups):
-            source = lax.rem(group - r + groups, groups)
-            for m in range(steps):
-                at = pl.multiple_of(lax.rem(step - m + steps, steps) * rows, rows)
-                right = jnp.concatenate(
-                    [scaled[source * steps + s, pl.ds(at, rows), :] for s in range(steps)], axis=1
-                )
-                term = jnp.dot(hidden[r * steps + m][...], right, preferred_element_type=F32)
-                total = term if total is None else total + term
-        for s in range(steps):
-            out[s] = total[:, s * wide : (s + 1) * wide]
-
-    flat = [b for line in blocks for b in line]
-    return call(
-        kernel,
-        place,
-        units // tall,
-        [pl.BlockSpec((tall, rows), lambda n, place: (n, 0))] * len(flat) + [whole(scaled.shape)],
-        pl.BlockSpec((steps, tall, wide), lambda n, place: (0, n, 0)),
-        jax.ShapeDtypeStruct((steps, units, wide), F32),
-        [],
-        2 * units * rows * len(flat) * wide * steps,
-        (*flat, scaled),
     )
 
 
@@ -402,9 +388,6 @@
 
     place = jnp.stack([step, j, i // steps]).astype(jnp.int32)
 
-    def along_groups(values, shift):
-        return lax.ppermute(values, "seq", [(a, (a + shift * steps) % seqs) for a in range(seqs)])
-
     head_send = w_out.reshape(head_rows, steps, halves, block).transpose(2, 1, 0, 3)
     head_send = jnp.broadcast_to(head_send, (hids // halves,) + head_send.shape)
     head_send = head_send.reshape(hids, steps, head_rows, block)
@@ -413,8 +396,11 @@
     ids = gather_flips(codebook_ids, step).transpose(1, 0, 2).reshape(steps, owned)
     ids_rows = [ids] + [turn_hid(ids, -k) for k in range(1, halves)]
 
+    before = jnp.maximum(step - 1, 0)
+    looked = jnp.take(pick(embedding, before), pick(ids, before), axis=0)
+
     group = [hidden] + [flip_seq(hidden, -r) for r in range(1, steps)]
-    proj, squares, *send = project(place, group, w_in, hids)
+    proj, squares, *send = project(after(place, looked), group, w_in, hids)
     received = [along_hid(send[shift - 1], shift) for shift in range(1, hids)]
 
     head_send = after(head_mid, *send).reshape(steps, hids * head_rows, block)
@@ -422,17 +408,10 @@
     head_send = head_send.reshape(seqs, hids * head_rows, block)
     head = lax.all_to_all(head_send, "seq", 0, 0).reshape(depth, block)
 
-    before = jnp.maximum(step - 1, 0)
-    table = pick(embedding, before)
-    looked = jnp.take(table, pick(ids, before), axis=0)
     gain = pick(depth_gain, step)[None, :]
     proj, x_rows, normed, scale, ratio = normalise(
         place, proj, squares, received, looked, gain, width_in
     )
-
-    turned = [after(hidden.T, normed)]
-    turned += [along_groups(turned[0], r) for r in range(1, groups)]
-    turned = [[t] + [flip_seq(t, m) for m in range(1, steps)] for t in turned]
 
     normed_rows = jnp.concatenate([normed] + [turn_hid(normed, -k) for k in range(1, halves)])
     targets = jnp.concatenate([pick(r, step) for r in ids_rows])
@@ -457,16 +436,17 @@
         place, d_norm_rows, received, x_rows, proj, scale, ratio, gain, width_in
     )
 
-    part_out = matmul(normed_rows, after(d_logit, *away), ((0,), (0,))).astype(BF16)
+    part_out = matmul(normed_rows, after(d_logit, *received), ((0,), (0,))).astype(BF16)
     part_out = lax.all_to_all(part_out.reshape(seqs, depth // seqs, block), "seq", 0, 0)
     sums = sum_groups(place, part_out, steps, hids)
     sums = [along_hid(p, shift) if shift else p for shift, p in enumerate(sums)]
     grad_out = head_gradient(place, sums, halves)
 
+    turned = [after(h, normed).T for h in group]
     pieces = [d_round] + [along_hid(d_round, shift) for shift in range(1, hids)]
-    scaled, mine, *others = spread(place, pieces, seqs, steps)
-    scaled = lax.all_to_all(scaled, "seq", 0, 0)
-    grad_in = input_gradient(place, turned, scaled, steps)
+    grad_in, mine, *others = input_gradient(place, pieces, turned, seqs)
+    grad_in = lax.all_to_all(grad_in, "seq", 0, 0)
+    grad_in = grad_in.reshape(groups, steps, units, depth // seqs).astype(F32).sum(0)
     mine = [mine] + [flip_seq(others[r - 1], r) for r in range(1, steps)]
     grad_hidden = hidden_gradient(place, mine, w_in, hidden)
     return (grad_hidden, grad_in, grad_out)

time: 163 us -> 169 us (1.037)
  the two profiles are of different devices: /device:TPU:0 before, /device:TPU:8 now
where the time goes in v3:
time: 169 us; the launch traced here: 168 us
  waiting for transfers between devices  74.5 us (44%)
  Pallas kernels  35.2 us (21%)
  starting transfers between devices  30.5 us (18%)
  local copies, waits for them, and re-layouts  17.8 us (11%)
  other arithmetic  5.15 us (3%)
  matrix products  3.64 us (2%)
    ppermute x9, waiting for transfers between devices, along_hid(): lax.ppermute(values, 'hid', [(a, (a + shift) % hids) for a in range(hids)])  52.5 us
    pallas_call x7, Pallas kernels, call(): pl.pallas_call(kernel, grid_spec=pltpu.PrefetchScalarGridSpec(num_scalar_...  35.2 us
    ppermute x4, waiting for transfers between devices, turn_hid(): lax.ppermute(values, 'hid', [(a, a - a % halves + (a % halves + shift) %...  16.4 us
    ppermute x9, starting transfers between devices, along_hid(): lax.ppermute(values, 'hid', [(a, (a + shift) % hids) for a in range(hids)])  10.1 us
    unnamed x40, local copies, waits for them, and re-layouts  7.52 us
    all_to_all x1, waiting for transfers between devices, shards(): grad_in = lax.all_to_all(grad_in, 'seq', 0, 0)  5.64 us
    all_to_all x1, starting transfers between devices, shards(): head_mid = lax.all_to_all(head_send, 'hid', 0, 0).transpose(1, 0, 2, 3)  5.32 us
    all_to_all x1, starting transfers between devices, shards(): grad_in = lax.all_to_all(grad_in, 'seq', 0, 0)  4.35 us
  transfers between devices with their start and end apart: 20, of which 12 were waited for; matrix products, arithmetic and copies ran while one was open for 7% of the time, Pallas kernels for 21%

profile of v3, /device:TPU:8, one launch (start us, length us, event | category | flops | bytes accessed | tf_op | source)
XLA Modules:
  0.0 167.7 jit_solution(3760929031512792667)
XLA Ops:
  0.7 1.2 copy.26
  2.5 1.1 reshape.97
  3.8 0.9 broadcast_in_dim.32
  4.6 5.3 %all-to-all-start = ((bf16[4,2,32,1024]{3,2,1,0:T(8,128)(2,1)}), bf16[4,2,32,1024]{3,2,1,0:T(8,128)(2,1)S(1)}, u32[]{:S(2)}, u32[]{:S(2)}) async-start(bf16[4,2,32,1024]{3,2,1,0:T(8,128)(2,1)} %bitcast.11), calls=%async_computation | async-start | bytes 1048576 | tf_op jit(solution)/shard_map/all_to_all | solution.py:394
  10.7 3.8 %gather_fusion = bf16[128,1024]{1,0:T(8,128)(2,1)S(1)} fusion(bf16[2048,1024]{1,0:T(8,128)(2,1)} %bitcast.50, s32[1024]{0:T(1024)S(1)} %pad_clamp_fusion), kind=kCustom, calls=%fused_computation | custom fusion | bytes 524800 | tf_op jit(solution)/shard_map/jit(_take)/gather | solution.py:400
  14.5 0.8 broadcast_select_fusion.refs_5_
  15.3 1.0 copy.27.refs_1_
  16.3 6.2 %shard_map.85 = (f32[128,1024]{1,0:T(8,128)}, f32[128,1]{1,0:T(8,128)}, bf16[128,1152]{1,0:T(8,128)(2,1)}, bf16[128,1152]{1,0:T(8,128)(2,1)}, bf16[128,1152]{1,0:T(8,128)(2,1)}) custom-call(s32[3]{0:T(128)} %pad_add_fusion.1.place_ref, bf16[256,1024]{1,0:T(8,128)(2,1)} %refs_3_.1, bf16[256,1024]{1,0:T(8,128)(2,1)} %copy.27.refs_1_, ...), custom_call_target="tpu_custom_call" | custom-call | flops 1073741824 | bytes 5242880 | tf_op jit(solution)/shard_map/pallas_call | solution.py:37
  22.6 1.6 broadcast_in_dim.33
  24.2 3.9 %all-to-all-start.1 = ((bf16[8,128,1024]{2,1,0:T(8,128)(2,1)}), bf16[8,128,1024]{2,1,0:T(8,128)(2,1)S(1)}, u32[]{:S(2)}, u32[]{:S(2)}) async-start(bf16[8,128,1024]{2,1,0:T(8,128)(2,1)} %bitcast.47), calls=%async_computation.1 | async-start | bytes 4194304 | tf_op jit(solution)/shard_map/all_to_all | solution.py:409
  28.1 1.5 collective-permute-start.2
  29.5 3.0 %collective-permute-start.3 = (bf16[128,1152]{1,0:T(8,128)(2,1)}, bf16[128,1152]{1,0:T(8,128)(2,1)S(1)}, u32[]{:S(2)}, u32[]{:S(2)}) collective-permute-start(bf16[128,1152]{1,0:T(8,128)(2,1)} %get-tuple-element.29), channel_id=1, source_target_pairs={{0,2},{1,3},{2,0},{3,1},{4,6},{5,7},{6,4},{7,5},{8,10},{9,11},{10,... | collective-permute-start | bytes 884744 | tf_op jit(solution)/shard_map/ppermute | solution.py:365
  33.1 1.4 collective-permute-start.7
  34.6 3.6 %collective-permute-done.2.refs_2_ = bf16[128,1152]{1,0:T(8,128)(2,1)S(1)} collective-permute-done((bf16[128,1152]{1,0:T(8,128)(2,1)}, bf16[128,1152]{1,0:T(8,128)(2,1)S(1)}, u32[]{:S(2)}, u32[]{:S(2)}) %collective-permute-start.2) | collective-permute-done | bytes 294944 | tf_op jit(solution)/shard_map/ppermute | solution.py:365
  38.2 17.5 %collective-permute-done.3.refs_3_ = bf16[128,1152]{1,0:T(8,128)(2,1)S(1)} collective-permute-done((bf16[128,1152]{1,0:T(8,128)(2,1)}, bf16[128,1152]{1,0:T(8,128)(2,1)S(1)}, u32[]{:S(2)}, u32[]{:S(2)}) %collective-permute-start.3) | collective-permute-done | bytes 294944 | tf_op jit(solution)/shard_map/ppermute | solution.py:365
  55.7 2.5 %collective-permute-done.4.refs_4_ = bf16[128,1152]{1,0:T(8,128)(2,1)S(1)} collective-permute-done((bf16[128,1152]{1,0:T(8,128)(2,1)S(1)}, bf16[128,1152]{1,0:T(8,128)(2,1)S(1)}, u32[]{:S(2)}, u32[]{:S(2)}) %collective-permute-start.4) | collective-permute-done | bytes 294944 | tf_op jit(solution)/shard_map/ppermute | solution.py:365
  58.2 0.7 copy-done.8
  58.9 4.7 %shard_map.86 = (f32[128,1024]{1,0:T(8,128)}, f32[128,1024]{1,0:T(8,128)}, bf16[128,1024]{1,0:T(8,128)(2,1)}, f32[128,1]{1,0:T(8,128)}, f32[128,1]{1,0:T(8,128)}) custom-call(s32[3]{0:T(128)} %pad_add_fusion.1.place_ref, f32[128,1024]{1,0:T(8,128)} %get-tuple-element.26.refs_0_, f32[128,1]{1,0:T(8,128)} %get-tuple-element.27.refs_1_, ...), custom_call_target="tpu_custom_call" | custom-call | flops 1310720 | bytes 1675776 | tf_op jit(solution)/shard_map/pallas_call | solution.py:37
  63.8 1.0 constant_dynamic-update-slice_fusion.1
  64.7 7.0 %collective-permute-done.5 = bf16[128,1024]{1,0:T(8,128)(2,1)S(1)} collective-permute-done((bf16[128,1024]{1,0:T(8,128)(2,1)}, bf16[128,1024]{1,0:T(8,128)(2,1)S(1)}, u32[]{:S(2)}, u32[]{:S(2)}) %collective-permute-start.5) | collective-permute-done | bytes 262176 | tf_op jit(solution)/shard_map/ppermute | solution.py:368
  71.8 0.8 fusion.8
  73.3 3.3 %collective-permute-done.6 = f32[2,2,128]{2,1,0:T(2,128)S(1)} collective-permute-done((f32[2,2,128]{2,1,0:T(2,128)S(1)}, f32[2,2,128]{2,1,0:T(2,128)S(1)}, u32[]{:S(2)}, u32[]{:S(2)}) %collective-permute-start.6) | collective-permute-done | bytes 2080 | tf_op jit(solution)/shard_map/ppermute | solution.py:368
  77.0 0.7 fusion.9.refs_0_
  77.8 1.0 copy-done.3
  79.1 6.1 %collective-permute-done.8.refs_1_ = bf16[128,1024]{1,0:T(8,128)(2,1)S(1)} collective-permute-done((bf16[128,1024]{1,0:T(8,128)(2,1)S(1)}, bf16[128,1024]{1,0:T(8,128)(2,1)S(1)}, u32[]{:S(2)}, u32[]{:S(2)}) %collective-permute-start.8) | collective-permute-done | bytes 262176 | tf_op jit(solution)/shard_map/ppermute | solution.py:368
  85.2 2.1 %convolution_convert_fusion = bf16[1024,1024]{1,0:T(8,128)(2,1)} fusion(bf16[256,1024]{1,0:T(8,128)(2,1)S(1)} %constant_dynamic-update-slice_fusion, bf16[256,1024]{1,0:T(8,128)(2,1)S(1)} %multiply_convert_fusion), kind=kOutput, calls=%fused_computation.2 | convolution fusion | flops 537919488 | bytes 3145728 | tf_op jit(solution)/shard_map/dot_general | solution.py:17
  87.3 3.6 %all-to-all-start.3 = ((bf16[8,128,1024]{2,1,0:T(8,128)(2,1)}), bf16[8,128,1024]{2,1,0:T(8,128)(2,1)S(1)}, u32[]{:S(2)}, u32[]{:S(2)}) async-start(bf16[8,128,1024]{2,1,0:T(8,128)(2,1)} %bitcast.48), calls=%async_computation.3 | async-start | bytes 4194304 | tf_op jit(solution)/shard_map/all_to_all | solution.py:440
  90.9 4.9 %shard_map.87.refs_0_.refs_4_ = bf16[128,1152]{1,0:T(8,128)(2,1)} custom-call(s32[3]{0:T(128)} %pad_add_fusion.1.place_ref, f32[256,1024]{1,0:T(8,128)} %copy-done.3, bf16[128,1024]{1,0:T(8,128)(2,1)} %copy-done.9, f32[128,1024]{1,0:T(8,128)} %get-tuple-element.33.refs_2_, f32[128,1024]{1,0:T(8,128)} %get-tuple-element.34.refs_3_, ...), custom_call_target="tpu_custom_call" | custom-call | flops 1310720 | bytes 2364416 | tf_op jit(solution)/shard_map/pallas_call | solution.py:37
  95.8 2.6 %collective-permute-start.10 = (bf16[128,1152]{1,0:T(8,128)(2,1)}, bf16[128,1152]{1,0:T(8,128)(2,1)S(1)}, u32[]{:S(2)}, u32[]{:S(2)}) collective-permute-start(bf16[128,1152]{1,0:T(8,128)(2,1)} %shard_map.87.refs_0_.refs_4_), channel_id=1, source_target_pairs={{0,2},{1,3},{2,0},{3,1},{4,6},{5,7},{6,4},{7,5},{8,10},{9,11},{10,... | collective-permute-start | bytes 884744 | tf_op jit(solution)/shard_map/ppermute | solution.py:365
  98.9 1.0 copy.30
  99.9 6.0 %collective-permute-done.9.refs_1_.refs_5_ = bf16[128,1152]{1,0:T(8,128)(2,1)S(1)} collective-permute-done((bf16[128,1152]{1,0:T(8,128)(2,1)}, bf16[128,1152]{1,0:T(8,128)(2,1)S(1)}, u32[]{:S(2)}, u32[]{:S(2)}) %collective-permute-start.9) | collective-permute-done | bytes 294944 | tf_op jit(solution)/shard_map/ppermute | solution.py:365
  105.9 16.3 %collective-permute-done.10.refs_2_.refs_6_ = bf16[128,1152]{1,0:T(8,128)(2,1)S(1)} collective-permute-done((bf16[128,1152]{1,0:T(8,128)(2,1)}, bf16[128,1152]{1,0:T(8,128)(2,1)S(1)}, u32[]{:S(2)}, u32[]{:S(2)}) %collective-permute-start.10) | collective-permute-done | bytes 294944 | tf_op jit(solution)/shard_map/ppermute | solution.py:365
  122.2 2.8 %collective-permute-done.11.refs_3_.refs_7_ = bf16[128,1152]{1,0:T(8,128)(2,1)S(1)} collective-permute-done((bf16[128,1152]{1,0:T(8,128)(2,1)}, bf16[128,1152]{1,0:T(8,128)(2,1)S(1)}, u32[]{:S(2)}, u32[]{:S(2)}) %collective-permute-start.11) | collective-permute-done | bytes 294944 | tf_op jit(solution)/shard_map/ppermute | solution.py:365
  125.0 0.7 copy-done.18
  125.7 6.6 %shard_map.88 = (bf16[8,1024,128]{2,1,0:T(8,128)(2,1)}, bf16[256,1152]{1,0:T(8,128)(2,1)}, bf16[256,1152]{1,0:T(8,128)(2,1)}) custom-call(s32[3]{0:T(128)} %pad_add_fusion.1.place_ref, bf16[128,1152]{1,0:T(8,128)(2,1)} %shard_map.87.refs_0_.refs_4_, bf16[128,1152]{1,0:T(8,128)(2,1)} %copy-done.16, bf16[128,1152]{1,0:T(8,128)(2,1)} %copy-done.17, ...), custom_call_target="tpu_custom_call" | custom-call | flops 1073741824 | bytes 3407872 | tf_op jit(solution)/shard_map/pallas_call | solution.py:37
  132.4 1.4 copy-done.1
  133.8 4.3 %all-to-all-start.2 = ((bf16[8,1024,128]{2,1,0:T(8,128)(2,1)}), bf16[8,1024,128]{2,1,0:T(8,128)(2,1)}, u32[]{:S(2)}, u32[]{:S(2)}) async-start(bf16[8,1024,128]{2,1,0:T(8,128)(2,1)} %get-tuple-element.41), calls=%async_computation.2 | async-start | bytes 4194304 | tf_op jit(solution)/shard_map/all_to_all | solution.py:448
  138.5 4.2 %shard_map.90 = (bf16[2,32,1024]{2,1,0:T(8,128)(2,1)}, bf16[2,32,1024]{2,1,0:T(8,128)(2,1)}, bf16[2,32,1024]{2,1,0:T(8,128)(2,1)}, bf16[2,32,1024]{2,1,0:T(8,128)(2,1)}) custom-call(s32[3]{0:T(128)} %pad_add_fusion.1.place_ref, bf16[8,128,1024]{2,1,0:T(8,128)(2,1)} %copy-done.1), custom_call_target="tpu_custom_call" | custom-call | flops 1048576 | bytes 2097152 | tf_op jit(solution)/shard_map/pallas_call | solution.py:37
  142.7 0.7 collective-permute-start.14
  143.3 2.0 %collective-permute-start.15 = (bf16[2,32,1024]{2,1,0:T(8,128)(2,1)}, bf16[2,32,1024]{2,1,0:T(8,128)(2,1)S(1)}, u32[]{:S(2)}, u32[]{:S(2)}) collective-permute-start(bf16[2,32,1024]{2,1,0:T(8,128)(2,1)} %get-tuple-element.46), channel_id=1, source_target_pairs={{0,3},{1,0},{2,1},{3,2},{4,7},{5,4},{6,5},{7,6},{8,11},{9,8},{10,9... | collective-permute-start | bytes 393224 | tf_op jit(solution)/shard_map/ppermute | solution.py:365
  145.3 0.8 copy-done.4
  146.1 5.9 %shard_map.89 = bf16[256,1024]{1,0:T(8,128)(2,1)} custom-call(s32[3]{0:T(128)} %pad_add_fusion.1.place_ref, bf16[256,1152]{1,0:T(8,128)(2,1)} %get-tuple-element.39.refs_0_, bf16[256,1152]{1,0:T(8,128)(2,1)} %copy-done.4, bf16[2,1024,1024]{2,1,0:T(8,128)(2,1)} %refs_2_.3, bf16[256,1024]{1,0:T(8,128)(2,1)} %refs_3_.1), custom_call_target="tpu_custom_call" | custom-call | flops 1073741824 | bytes 5898240 | tf_op jit(solution)/shard_map/pallas_call | solution.py:37
  152.1 2.8 %collective-permute-done.14.refs_2_ = bf16[2,32,1024]{2,1,0:T(8,128)(2,1)S(1)} collective-permute-done((bf16[2,32,1024]{2,1,0:T(8,128)(2,1)}, bf16[2,32,1024]{2,1,0:T(8,128)(2,1)S(1)}, u32[]{:S(2)}, u32[]{:S(2)}) %collective-permute-start.14) | collective-permute-done | bytes 131104 | tf_op jit(solution)/shard_map/ppermute | solution.py:365
  154.8 1.0 collective-permute-done.15.refs_3_
  155.8 0.7 copy-done.12
  156.4 2.7 %shard_map.91 = f32[32,2,2048]{2,1,0:T(2,128)} custom-call(s32[3]{0:T(128)} %pad_add_fusion.1.place_ref, bf16[2,32,1024]{2,1,0:T(8,128)(2,1)} %get-tuple-element.43.refs_0_, bf16[2,32,1024]{2,1,0:T(8,128)(2,1)} %copy-done.10, bf16[2,32,1024]{2,1,0:T(8,128)(2,1)} %copy-done.11, bf16[2,32,1024]{2,1,0:T(8,128)(2,1)} %copy-done.12), custom_call_target="tpu_custom_call" | custom-call | flops 262144 | bytes 524288 | tf_op jit(solution)/shard_map/pallas_call | solution.py:37
  159.1 5.6 %all-to-all-done.2 = bf16[8,1024,128]{2,1,0:T(8,128)(2,1)} async-done(((bf16[8,1024,128]{2,1,0:T(8,128)(2,1)}), bf16[8,1024,128]{2,1,0:T(8,128)(2,1)}, u32[]{:S(2)}, u32[]{:S(2)}) %all-to-all-start.2) | async-done | bytes 2097184 | tf_op jit(solution)/shard_map/all_to_all | solution.py:448
  164.8 3.0 %convert_reduce_fusion = f32[2,1024,128]{2,1,0:T(8,128)} fusion(bf16[4,2,1024,128]{3,2,1,0:T(8,128)(2,1)} %bitcast.30), kind=kLoop, calls=%fused_computation.1 | loop fusion | flops 1835008 | bytes 3145728 | tf_op jit(solution)/shard_map/reduce_sum | solution.py:449
  (74 shorter events, 4.6 us)
Async XLA Ops:
  0.6 31.9 %copy-start = (f32[2,1024]{1,0:T(2,128)S(1)}, f32[2,1024]{1,0:T(2,128)}, u32[]{:S(2)}) copy-start(f32[2,1024]{1,0:T(2,128)} %param.9) | copy-start | bytes 24580
  0.6 9.9 %copy-start.13 = (s32[2,64]{1,0:T(2,128)S(1)}, s32[2,64]{1,0:T(2,128)}, u32[]{:S(2)}) copy-start(s32[2,64]{1,0:T(2,128)} %param.11) | copy-start | bytes 1540
  0.7 9.9 %collective-permute-start = (s32[2,64]{1,0:T(2,128)}, s32[2,64]{1,0:T(2,128)S(1)}, u32[]{:S(2)}, u32[]{:S(2)}) collective-permute-start(s32[2,64]{1,0:T(2,128)} %param.11), channel_id=1, source_target_pairs={{0,4},{4,0},{8,12},{12,8},{16,20},{20,16},{24,28},{28,24},{1,5},{5... | collective-permute-start | bytes 1544 | tf_op jit(solution)/shard_map/ppermute | solution.py:375
  2.0 13.3 %collective-permute-start.1 = (bf16[256,1024]{0,1:T(8,128)(2,1)S(1)}, bf16[256,1024]{0,1:T(8,128)(2,1)S(1)}, u32[]{:S(2)}, u32[]{:S(2)}) collective-permute-start(bf16[256,1024]{0,1:T(8,128)(2,1)S(1)} %copy.26), channel_id=1, source_target_pairs={{0,4},{4,0},{8,12},{12,8},{16,20},{20,16},{24,28},{28,24},{1,5},{5... | collective-permute-start | bytes 1572872 | tf_op jit(solution)/shard_map/ppermute | solution.py:375
  4.6 17.9 %all-to-all-start = ((bf16[4,2,32,1024]{3,2,1,0:T(8,128)(2,1)}), bf16[4,2,32,1024]{3,2,1,0:T(8,128)(2,1)S(1)}, u32[]{:S(2)}, u32[]{:S(2)}) async-start(bf16[4,2,32,1024]{3,2,1,0:T(8,128)(2,1)} %bitcast.11), calls=%async_computation | async-start | bytes 1048576 | tf_op jit(solution)/shard_map/all_to_all | solution.py:394
  15.3 7.2 %copy-start.5 = (bf16[256,1024]{0,1:T(8,128)(2,1)}, bf16[256,1024]{0,1:T(8,128)(2,1)S(1)}, u32[]{:S(2)}) copy-start(bf16[256,1024]{0,1:T(8,128)(2,1)S(1)} %collective-permute-done.1) | copy-start | bytes 1572868
  24.2 8.3 %copy-start.15 = (bf16[128,1152]{1,0:T(8,128)(2,1)S(1)}, bf16[128,1152]{1,0:T(8,128)(2,1)}, u32[]{:S(2)}) copy-start(bf16[128,1152]{1,0:T(8,128)(2,1)} %get-tuple-element.30) | copy-start | bytes 884740
  24.2 47.6 %all-to-all-start.1 = ((bf16[8,128,1024]{2,1,0:T(8,128)(2,1)}), bf16[8,128,1024]{2,1,0:T(8,128)(2,1)S(1)}, u32[]{:S(2)}, u32[]{:S(2)}) async-start(bf16[8,128,1024]{2,1,0:T(8,128)(2,1)} %bitcast.47), calls=%async_computation.1 | async-start | bytes 4194304 | tf_op jit(solution)/shard_map/all_to_all | solution.py:409
  28.1 10.1 %collective-permute-start.2 = (bf16[128,1152]{1,0:T(8,128)(2,1)}, bf16[128,1152]{1,0:T(8,128)(2,1)S(1)}, u32[]{:S(2)}, u32[]{:S(2)}) collective-permute-start(bf16[128,1152]{1,0:T(8,128)(2,1)} %get-tuple-element.28), channel_id=1, source_target_pairs={{0,1},{1,2},{2,3},{3,0},{4,5},{5,6},{6,7},{7,4},{8,9},{9,10},{10,1... | collective-permute-start | bytes 884744 | tf_op jit(solution)/shard_map/ppermute | solution.py:365
  29.5 26.2 %collective-permute-start.3 = (bf16[128,1152]{1,0:T(8,128)(2,1)}, bf16[128,1152]{1,0:T(8,128)(2,1)S(1)}, u32[]{:S(2)}, u32[]{:S(2)}) collective-permute-start(bf16[128,1152]{1,0:T(8,128)(2,1)} %get-tuple-element.29), channel_id=1, source_target_pairs={{0,2},{1,3},{2,0},{3,1},{4,6},{5,7},{6,4},{7,5},{8,10},{9,11},{10,... | collective-permute-start | bytes 884744 | tf_op jit(solution)/shard_map/ppermute | solution.py:365
  32.5 25.7 %collective-permute-start.4 = (bf16[128,1152]{1,0:T(8,128)(2,1)S(1)}, bf16[128,1152]{1,0:T(8,128)(2,1)S(1)}, u32[]{:S(2)}, u32[]{:S(2)}) collective-permute-start(bf16[128,1152]{1,0:T(8,128)(2,1)S(1)} %copy-done.15), channel_id=1, source_target_pairs={{0,3},{1,0},{2,1},{3,2},{4,7},{5,4},{6,5},{7,6},{8,11},{9,8},{10,9... | collective-permute-start | bytes 884744 | tf_op jit(solution)/shard_map/ppermute | solution.py:365
  33.1 30.6 %collective-permute-start.7 = (s32[2,128]{1,0:T(2,128)S(1)}, s32[2,128]{1,0:T(2,128)S(1)}, u32[]{:S(2)}, u32[]{:S(2)}) collective-permute-start(s32[2,128]{1,0:T(2,128)S(1)} %reshape.96), channel_id=1, source_target_pairs={{0,1},{1,0},{2,3},{3,2},{4,5},{5,4},{6,7},{7,6},{8,9},{9,8},{10,11... | collective-permute-start | bytes 3080 | tf_op jit(solution)/shard_map/ppermute | solution.py:368
  38.2 20.0 %copy-start.6 = (bf16[128,1152]{1,0:T(8,128)(2,1)}, bf16[128,1152]{1,0:T(8,128)(2,1)S(1)}, u32[]{:S(2)}) copy-start(bf16[128,1152]{1,0:T(8,128)(2,1)S(1)} %collective-permute-done.2.refs_2_) | copy-start | bytes 884740
  55.7 2.5 %copy-start.7 = (bf16[128,1152]{1,0:T(8,128)(2,1)}, bf16[128,1152]{1,0:T(8,128)(2,1)S(1)}, u32[]{:S(2)}) copy-start(bf16[128,1152]{1,0:T(8,128)(2,1)S(1)} %collective-permute-done.3.refs_3_) | copy-start | bytes 884740
  58.2 0.7 copy-start.8
  63.6 8.1 %collective-permute-start.5 = (bf16[128,1024]{1,0:T(8,128)(2,1)}, bf16[128,1024]{1,0:T(8,128)(2,1)S(1)}, u32[]{:S(2)}, u32[]{:S(2)}) collective-permute-start(bf16[128,1024]{1,0:T(8,128)(2,1)} %get-tuple-element.31), channel_id=1, source_target_pairs={{0,1},{1,0},{2,3},{3,2},{4,5},{5,4},{6,7},{7,6},{8,9},{9,8},{10,11... | collective-permute-start | bytes 786440 | tf_op jit(solution)/shard_map/ppermute | solution.py:368
  72.9 3.7 %collective-permute-start.6 = (f32[2,2,128]{2,1,0:T(2,128)S(1)}, f32[2,2,128]{2,1,0:T(2,128)S(1)}, u32[]{:S(2)}, u32[]{:S(2)}) collective-permute-start(f32[2,2,128]{2,1,0:T(2,128)S(1)} %pad_maximum_fusion), channel_id=1, source_target_pairs={{0,1},{1,0},{2,3},{3,2},{4,5},{5,4},{6,7},{7,6},{8,9},{9,8},{10,11... | collective-permute-start | bytes 6152 | tf_op jit(solution)/shard_map/ppermute | solution.py:368
  77.8 1.0 copy-start.3
  78.8 6.4 %collective-permute-start.8 = (bf16[128,1024]{1,0:T(8,128)(2,1)S(1)}, bf16[128,1024]{1,0:T(8,128)(2,1)S(1)}, u32[]{:S(2)}, u32[]{:S(2)}) collective-permute-start(bf16[128,1024]{1,0:T(8,128)(2,1)S(1)} %slice.41), channel_id=1, source_target_pairs={{0,1},{1,0},{2,3},{3,2},{4,5},{5,4},{6,7},{7,6},{8,9},{9,8},{10,11... | collective-permute-start | bytes 786440 | tf_op jit(solution)/shard_map/ppermute | solution.py:368
  85.2 2.1 %copy-start.9 = (bf16[128,1024]{1,0:T(8,128)(2,1)}, bf16[128,1024]{1,0:T(8,128)(2,1)S(1)}, u32[]{:S(2)}) copy-start(bf16[128,1024]{1,0:T(8,128)(2,1)S(1)} %collective-permute-done.8.refs_1_) | copy-start | bytes 786436
  87.3 45.1 %all-to-all-start.3 = ((bf16[8,128,1024]{2,1,0:T(8,128)(2,1)}), bf16[8,128,1024]{2,1,0:T(8,128)(2,1)S(1)}, u32[]{:S(2)}, u32[]{:S(2)}) async-start(bf16[8,128,1024]{2,1,0:T(8,128)(2,1)} %bitcast.48), calls=%async_computation.3 | async-start | bytes 4194304 | tf_op jit(solution)/shard_map/all_to_all | solution.py:440
  90.9 8.0 %copy-start.2 = (bf16[256,1024]{1,0:T(8,128)(2,1)S(1)}, bf16[256,1024]{1,0:T(8,128)(2,1)}, u32[]{:S(2)}) copy-start(bf16[256,1024]{1,0:T(8,128)(2,1)} %refs_3_.1) | copy-start | bytes 1572868
  95.8 10.1 %collective-permute-start.9 = (bf16[128,1152]{1,0:T(8,128)(2,1)}, bf16[128,1152]{1,0:T(8,128)(2,1)S(1)}, u32[]{:S(2)}, u32[]{:S(2)}) collective-permute-start(bf16[128,1152]{1,0:T(8,128)(2,1)} %shard_map.87.refs_0_.refs_4_), channel_id=1, source_target_pairs={{0,1},{1,2},{2,3},{3,0},{4,5},{5,6},{6,7},{7,4},{8,9},{9,10},{10,1... | collective-permute-start | bytes 884744 | tf_op jit(solution)/shard_map/ppermute | solution.py:365
  95.8 26.4 %collective-permute-start.10 = (bf16[128,1152]{1,0:T(8,128)(2,1)}, bf16[128,1152]{1,0:T(8,128)(2,1)S(1)}, u32[]{:S(2)}, u32[]{:S(2)}) collective-permute-start(bf16[128,1152]{1,0:T(8,128)(2,1)} %shard_map.87.refs_0_.refs_4_), channel_id=1, source_target_pairs={{0,2},{1,3},{2,0},{3,1},{4,6},{5,7},{6,4},{7,5},{8,10},{9,11},{10,... | collective-permute-start | bytes 884744 | tf_op jit(solution)/shard_map/ppermute | solution.py:365
  98.5 26.5 %collective-permute-start.11 = (bf16[128,1152]{1,0:T(8,128)(2,1)}, bf16[128,1152]{1,0:T(8,128)(2,1)S(1)}, u32[]{:S(2)}, u32[]{:S(2)}) collective-permute-start(bf16[128,1152]{1,0:T(8,128)(2,1)} %shard_map.87.refs_0_.refs_4_), channel_id=1, source_target_pairs={{0,3},{1,0},{2,1},{3,2},{4,7},{5,4},{6,5},{7,6},{8,11},{9,8},{10,9... | collective-permute-start | bytes 884744 | tf_op jit(solution)/shard_map/ppermute | solution.py:365
  105.9 19.1 %copy-start.16 = (bf16[128,1152]{1,0:T(8,128)(2,1)}, bf16[128,1152]{1,0:T(8,128)(2,1)S(1)}, u32[]{:S(2)}) copy-start(bf16[128,1152]{1,0:T(8,128)(2,1)S(1)} %collective-permute-done.9.refs_1_.refs_5_) | copy-start | bytes 884740
  122.2 2.8 %copy-start.17 = (bf16[128,1152]{1,0:T(8,128)(2,1)}, bf16[128,1152]{1,0:T(8,128)(2,1)S(1)}, u32[]{:S(2)}) copy-start(bf16[128,1152]{1,0:T(8,128)(2,1)S(1)} %collective-permute-done.10.refs_2_.refs_6_) | copy-start | bytes 884740
  125.0 0.7 copy-start.18
  132.4 1.4 copy-start.1
  132.4 5.7 %copy-start.14 = (bf16[256,1152]{1,0:T(8,128)(2,1)S(1)}, bf16[256,1152]{1,0:T(8,128)(2,1)}, u32[]{:S(2)}) copy-start(bf16[256,1152]{1,0:T(8,128)(2,1)} %get-tuple-element.40) | copy-start | bytes 1769476
  133.8 31.0 %all-to-all-start.2 = ((bf16[8,1024,128]{2,1,0:T(8,128)(2,1)}), bf16[8,1024,128]{2,1,0:T(8,128)(2,1)}, u32[]{:S(2)}, u32[]{:S(2)}) async-start(bf16[8,1024,128]{2,1,0:T(8,128)(2,1)} %get-tuple-element.41), calls=%async_computation.2 | async-start | bytes 4194304 | tf_op jit(solution)/shard_map/all_to_all | solution.py:448
  138.1 7.2 %collective-permute-start.12 = (bf16[256,1152]{1,0:T(8,128)(2,1)S(1)}, bf16[256,1152]{1,0:T(8,128)(2,1)S(1)}, u32[]{:S(2)}, u32[]{:S(2)}) collective-permute-start(bf16[256,1152]{1,0:T(8,128)(2,1)S(1)} %copy-done.14), channel_id=1, source_target_pairs={{0,4},{4,0},{8,12},{12,8},{16,20},{20,16},{24,28},{28,24},{1,5},{5... | collective-permute-start | bytes 1769480 | tf_op jit(solution)/shard_map/ppermute | solution.py:375
  142.7 9.4 %collective-permute-start.13 = (bf16[2,32,1024]{2,1,0:T(8,128)(2,1)}, bf16[2,32,1024]{2,1,0:T(8,128)(2,1)S(1)}, u32[]{:S(2)}, u32[]{:S(2)}) collective-permute-start(bf16[2,32,1024]{2,1,0:T(8,128)(2,1)} %get-tuple-element.44), channel_id=1, source_target_pairs={{0,1},{1,2},{2,3},{3,0},{4,5},{5,6},{6,7},{7,4},{8,9},{9,10},{10,1... | collective-permute-start | bytes 393224 | tf_op jit(solution)/shard_map/ppermute | solution.py:365
  142.7 12.1 %collective-permute-start.14 = (bf16[2,32,1024]{2,1,0:T(8,128)(2,1)}, bf16[2,32,1024]{2,1,0:T(8,128)(2,1)S(1)}, u32[]{:S(2)}, u32[]{:S(2)}) collective-permute-start(bf16[2,32,1024]{2,1,0:T(8,128)(2,1)} %get-tuple-element.45), channel_id=1, source_target_pairs={{0,2},{1,3},{2,0},{3,1},{4,6},{5,7},{6,4},{7,5},{8,10},{9,11},{10,... | collective-permute-start | bytes 393224 | tf_op jit(solution)/shard_map/ppermute | solution.py:365
  143.3 12.4 %collective-permute-start.15 = (bf16[2,32,1024]{2,1,0:T(8,128)(2,1)}, bf16[2,32,1024]{2,1,0:T(8,128)(2,1)S(1)}, u32[]{:S(2)}, u32[]{:S(2)}) collective-permute-start(bf16[2,32,1024]{2,1,0:T(8,128)(2,1)} %get-tuple-element.46), channel_id=1, source_target_pairs={{0,3},{1,0},{2,1},{3,2},{4,7},{5,4},{6,5},{7,6},{8,11},{9,8},{10,9... | collective-permute-start | bytes 393224 | tf_op jit(solution)/shard_map/ppermute | solution.py:365
  145.3 0.8 copy-start.4
  152.0 3.7 %copy-start.10 = (bf16[2,32,1024]{2,1,0:T(8,128)(2,1)}, bf16[2,32,1024]{2,1,0:T(8,128)(2,1)S(1)}, u32[]{:S(2)}) copy-start(bf16[2,32,1024]{2,1,0:T(8,128)(2,1)S(1)} %collective-permute-done.13.refs_1_) | copy-start | bytes 393220
  154.8 1.0 copy-start.11
  155.8 0.7 copy-start.12
